TPU v7x, 32 devices: a whole 2x2x4 slice. The times are simulated.
32 devices in a mesh: gx: 8 (over y, x, core), gy: 4 (over z).
Axes of the slice: x: 2, y: 2, z: 4, core: 2. Of those that a mesh axis runs over, the one named last changes fastest.
Arguments:
- tokens: bfloat16 [16384, 2048], P(('gx', 'gy')), may hold values from -6 to 6
- reset_mask: int32 [16384], P(('gx', 'gy')), may hold values from 0 to 1, as said below
- weight: bfloat16 [2048, 6144], P(('gx', 'gy')), may hold values from -0.125 to 0.125
- vectors: bfloat16 [6, 2048], P(None, ('gx', 'gy')), may hold values from -2 to 15, as said below
- cotangent: bfloat16 [16384, 2048], P(('gx', 'gy')), may hold values from -6 to 6
Outputs:
- output: bfloat16 [16384, 2048], P(('gx', 'gy'))
- input_grad: float32 [16384, 2048], P(('gx', 'gy'))
- weight_grad: float32 [2048, 6144], P(('gx', 'gy'))
- vector_grad: float32 [6, 2048], P(None, ('gx', 'gy'))
Inputs may be any that keep to these rules, and one draw needn't show every extreme that they name: `vectors`: the gain row lies in 0.6 to 1.4, the forget bias row in 1 to 15, the other rows in -2 to 2. `reset_mask`: ones fall only among the first 512 and the last 512 tokens of the stream, with at least one among tokens 1 to 511 and at least one among the last 512.
All inputs are finite; a program needn't handle non-finite values.
Results may differ from a plain program's by a relative error of at most 0.005.
Values may be sent and summed in bfloat16 or wider, within the bound.
A program may use at most 256 MiB of HBM per device.

v0:
```python
import jax
import jax.numpy as jnp
from jax import lax
from jax.sharding import PartitionSpec as P


def entering(value, axis, join, neutral, backward):
    count, mine = (lax.axis_size(axis), lax.axis_index(axis))
    pieces = jax.tree.map(lambda part: lax.all_gather(part, axis), value)
    if backward:
        pieces = jax.tree.map(lambda part: part[::-1], pieces)
        mine = count - 1 - mine
    subtotal = jax.tree.map(
        lambda part, zero: jnp.full_like(part, 0) + jnp.asarray(zero, part.dtype), value, neutral
    )

    def lap(position, subtotal):
        longer = join(subtotal, jax.tree.map(lambda part: part[position], pieces))
        return jax.tree.map(lambda new, old: jnp.where(position < mine, new, old), longer, subtotal)

    return lax.fori_loop(0, count - 1, lap, subtotal)


def from_behind(block, axis, distance):
    devices = range(lax.axis_size(axis))
    route = [(i - distance, i) for i in devices if i - distance in devices]
    return lax.ppermute(block, axis, route)


def compose(earlier, later):
    return (earlier[0] * later[0], later[0] * earlier[1] + later[1])


def local(tokens, reset_mask, weight, vectors, cotangent):
    width = weight.shape[1] // 3
    whole_weight, whole_vectors = (
        lax.all_gather(weight, ("gx", "gy"), axis=0, tiled=True),
        lax.all_gather(vectors, ("gx", "gy"), axis=1, tiled=True),
    )
    params = whole_vectors.astype(jnp.float32)
    gain = params[0]
    shift_bias = params[1]
    forget_peep = params[2]
    forget_bias = params[3]
    reset_peep = params[4]
    reset_bias = params[5]
    inputs = tokens.astype(jnp.float32)
    keep = (1 - reset_mask).astype(jnp.float32)[:, None]
    centred = inputs - jnp.mean(inputs, axis=1, keepdims=True)
    inv_std = lax.rsqrt(jnp.mean(centred * centred, axis=1, keepdims=True) + 1e-05)
    normed = centred * inv_std
    scaled = normed * gain + shift_bias
    rounded = scaled.astype(jnp.bfloat16)
    projected = jnp.dot(rounded, whole_weight, preferred_element_type=jnp.float32)
    candidate = projected[:, :width]
    forget_pre = projected[:, width : 2 * width]
    reset_pre = projected[:, 2 * width :]
    forget = jax.nn.sigmoid(forget_pre + forget_peep * scaled + forget_bias)
    decay = forget * keep
    inflow = (1.0 - forget) * candidate
    cum_decay, cum_state = lax.associative_scan(compose, (decay, inflow), axis=0)
    unit = (jnp.ones_like(cum_decay[-1]), jnp.zeros_like(cum_state[-1]))
    before = entering((cum_decay[-1], cum_state[-1]), ("gx", "gy"), compose, unit, False)
    state_in = before[1]
    state = cum_decay * state_in + cum_state
    previous = keep * jnp.concatenate([state_in[None], state[:-1]], 0)
    reset = jax.nn.sigmoid(reset_pre + reset_peep * previous + reset_bias)
    output = reset * state + (1.0 - reset) * inputs
    upstream = cotangent.astype(jnp.float32)
    reset_grad = upstream * (state - inputs) * reset * (1.0 - reset)
    through = keep * reset_peep * reset_grad
    next_decay, next_through = from_behind((decay[0], through[0]), ("gx", "gy"), -1)
    ahead = jnp.concatenate([decay[1:], next_decay[None]], 0)
    local_term = upstream * reset + jnp.concatenate([through[1:], next_through[None]], 0)
    flip_mult, flip_sum = lax.associative_scan(compose, (ahead[::-1], local_term[::-1]), axis=0)
    mult_back = flip_mult[::-1]
    sum_back = flip_sum[::-1]
    after = entering((mult_back[0], sum_back[0]), ("gx", "gy"), compose, unit, True)
    state_grad = mult_back * after[1] + sum_back
    candidate_grad = state_grad * (1.0 - forget)
    forget_grad = state_grad * (previous - candidate) * forget * (1.0 - forget)
    proj_grad = jnp.concatenate([candidate_grad, forget_grad, reset_grad], 1).astype(jnp.bfloat16)
    weight_grad = lax.psum_scatter(
        lax.dot_general(
            rounded, proj_grad, (((0,), (0,)), ((), ())), preferred_element_type=jnp.float32
        ),
        ("gx", "gy"),
        scatter_dimension=0,
        tiled=True,
    )
    scaled_grad = lax.dot_general(
        proj_grad,
        lax.all_gather(weight, ("gx", "gy"), axis=0, tiled=True),
        (((1,), (1,)), ((), ())),
        preferred_element_type=jnp.float32,
    )
    scaled_grad = scaled_grad + forget_grad * forget_peep
    vector_terms = jnp.stack(
        [
            jnp.sum(scaled_grad * normed, axis=0),
            jnp.sum(scaled_grad, axis=0),
            jnp.sum(forget_grad * scaled, axis=0),
            jnp.sum(forget_grad, axis=0),
            jnp.sum(reset_grad * previous, axis=0),
            jnp.sum(reset_grad, axis=0),
        ],
        0,
    )
    vector_grad = lax.psum_scatter(vector_terms, ("gx", "gy"), scatter_dimension=1, tiled=True)
    normed_grad = scaled_grad * gain
    input_grad = upstream * (1.0 - reset) + inv_std * (
        normed_grad
        - jnp.mean(normed_grad, axis=1, keepdims=True)
        - normed * jnp.mean(normed_grad * normed, axis=1, keepdims=True)
    )
    return (output.astype(jnp.bfloat16), input_grad, weight_grad, vector_grad)


def solution(mesh):
    placed = (
        P(("gx", "gy"), None),
        P(("gx", "gy")),
        P(("gx", "gy"), None),
        P(None, ("gx", "gy")),
        P(("gx", "gy"), None),
    )
    return jax.shard_map(
        local,
        mesh=mesh,
        in_specs=placed,
        out_specs=(
            P(("gx", "gy"), None),
            P(("gx", "gy"), None),
            P(("gx", "gy"), None),
            P(None, ("gx", "gy")),
        ),
        check_vma=False,
    )
```

profile of v0, /device:TPU:0, one launch (start us, length us, event | category | flops | bytes accessed | tf_op | source)
XLA Modules:
  0.0 1861.0 jit_solution(3395406904725568107)
XLA Ops:
  8.0 71.9 %all-gather = bf16[32,64,6]{1,2,0:T(8,128)(2,1)S(1)} all-gather(bf16[1,64,6]{1,2,0:T(8,128)(2,1)} %bitcast.101), channel_id=1, replica_groups=mesh['gx'=8,'gy'=4] {'gx','gy'}, dimensions={0}, use_global_device_ids=true | all-gather | bytes 25344 | tf_op jit(solution)/shard_map/all_gather | solution.py:38
  83.4 85.4 %all-gather.7.cloned.1.call-done = bf16[2048,6144]{1,0:T(8,128)(2,1)} async-done(((bf16[64,6144]{1,0:T(8,128)(2,1)}), bf16[2048,6144]{1,0:T(8,128)(2,1)}) %all-gather.7.cloned.1.call-update) | async-done | bytes 25165840 | tf_op jit(solution)/shard_map/all_gather | solution.py:37
  168.8 20.9 %fusion.59 = f32[512,6144]{1,0:T(8,128)} fusion(bf16[2048,6144]{1,0:T(8,128)(2,1)} %all-gather.7.cloned.1.call-done, bf16[512,2048]{1,0:T(8,128)(2,1)S(1)} %copy-done.1, f32[2048]{0:T(1024)S(1)} %bitcast.74, f32[2048]{0:T(1024)S(1)} %bitcast.65, f32[512]{0:T(512)S(1)} %add_rsqrt_fusion, f32[512]{0:T(512)S(1)} %broadcast_multiply_fusion.3), kind=kOutput, calls=%fused_computation.193 | convolution fusion | flops 12891193344 | bytes 39866368 | tf_op jit(solution)/shard_map/dot_general | solution.py:54
  196.9 10.0 slice.640
  207.0 9.8 slice.601
  216.8 9.8 slice.600
  232.9 10.0 slice.684
  242.9 9.8 slice.645
  252.6 9.8 slice.644
  262.4 5.7 fusion.69
  269.4 5.5 slice.638
  274.9 5.4 slice.604
  280.3 5.4 slice.603
  286.6 5.5 slice.682
  292.1 5.4 slice.648
  297.5 5.4 slice.647
  378.7 8.6 pad.234
  387.2 8.6 pad.235
  413.3 16.6 pad.254
  429.9 16.5 pad.236
  446.4 16.6 pad.237
  463.9 69.4 %all-gather.1 = f32[32,1,2048]{2,1,0:T(1,128)S(1)} all-gather(f32[1,1,2048]{2,1,0:T(1,128)S(1)} %add_bitcast_fusion.3), channel_id=1, replica_groups=mesh['gx'=8,'gy'=4] {'gx','gy'}, dimensions={0}, use_global_device_ids=true | all-gather | bytes 270336 | tf_op jit(solution)/shard_map/all_gather | solution.py:9
  533.4 16.5 pad.255
  550.9 65.6 %all-gather.2 = f32[32,1,2048]{2,1,0:T(1,128)S(1)} all-gather(f32[1,1,2048]{2,1,0:T(1,128)S(1)} %add_bitcast_fusion.2), channel_id=1, replica_groups=mesh['gx'=8,'gy'=4] {'gx','gy'}, dimensions={0}, use_global_device_ids=true | all-gather | bytes 270336 | tf_op jit(solution)/shard_map/all_gather | solution.py:9
  618.5 7.9 multiply_add_fusion.2
  626.5 7.8 fusion.61
  644.1 9.8 slice.731
  653.9 9.8 slice.691
  663.7 9.8 slice.689
  673.5 5.6 fusion.23
  681.0 9.8 slice.779
  690.8 9.7 slice.739
  700.5 9.7 slice.737
  710.3 16.7 slice.690
  727.0 16.7 slice.692
  743.6 16.7 slice.738
  760.3 16.7 slice.740
  777.0 5.7 fusion.68
  784.1 5.5 slice.729
  789.6 5.4 slice.695
  795.0 5.4 slice.694
  801.3 5.5 slice.777
  806.8 5.4 slice.743
  812.1 5.4 slice.742
  841.9 17.1 slice.732
  859.0 17.0 slice.780
  925.8 8.7 pad.270
  934.5 8.5 pad.271
  960.0 16.6 pad.272
  976.5 16.5 pad.273
  993.9 6.7 add.552
  1002.2 16.5 pad.290
  1018.7 16.5 pad.291
  1036.1 6.5 add.579
  1042.6 32.7 %rev.14 = f32[512,2048]{1,0:T(8,128)} reverse(f32[512,2048]{1,0:T(8,128)} %add.552), dimensions={0} | reverse | bytes 8388608 | tf_op jit(solution)/shard_map/rev | solution.py:76
  1075.3 68.4 %all-gather.3 = f32[32,1,2048]{2,1,0:T(1,128)S(1)} all-gather(f32[1,1,2048]{2,1,0:T(1,128)S(1)} %add_bitcast_fusion.1), channel_id=1, replica_groups=mesh['gx'=8,'gy'=4] {'gx','gy'}, dimensions={0}, use_global_device_ids=true | all-gather | bytes 270336 | tf_op jit(solution)/shard_map/all_gather | solution.py:9
  1144.1 32.6 %rev.17 = f32[512,2048]{1,0:T(8,128)} reverse(f32[512,2048]{1,0:T(8,128)} %add.579), dimensions={0} | reverse | bytes 8388608 | tf_op jit(solution)/shard_map/rev | solution.py:77
  1176.8 65.5 %all-gather.4 = f32[32,1,2048]{2,1,0:T(1,128)S(1)} all-gather(f32[1,1,2048]{2,1,0:T(1,128)S(1)} %add_bitcast_fusion), channel_id=1, replica_groups=mesh['gx'=8,'gy'=4] {'gx','gy'}, dimensions={0}, use_global_device_ids=true | all-gather | bytes 270336 | tf_op jit(solution)/shard_map/all_gather | solution.py:9
  1245.2 11.4 fusion.65
  1256.6 24.2 %fusion.62 = (f32[2048]{0:T(1024)S(1)}, f32[2048]{0:T(1024)S(1)}, f32[2048]{0:T(1024)S(1)}, f32[512]{0:T(512)S(1)}, f32[512]{0:T(512)S(1)}, /*index=5*/f32[2048]{0:T(1024)S(1)}, f32[512,2048]{1,0:T(8,128)}) fusion(f32[512,2048]{1,0:T(8,128)} %get-tuple-element.265, f32[2048]{0:T(1024)S(1)} %bitcast.76, f32[2048]{0:T(1024)S(1)} %bitcast.67, ...), kind=kOutput, calls=%fused_computation.195 | convolution fusion | flops 12921593856 | bytes 42008576 | tf_op jit(solution)/shard_map/dot_general | solution.py:91
  1282.3 24.8 %fusion.33 = f32[2048,6144]{1,0:T(8,128)} fusion(bf16[512,2048]{1,0:T(8,128)(2,1)} %get-tuple-element.275, bf16[512,2048]{1,0:T(8,128)(2,1)} %get-tuple-element.264, bf16[512,2048]{1,0:T(8,128)(2,1)} %get-tuple-element.272, bf16[512,2048]{1,0:T(8,128)(2,1)S(1)} %copy-done.1, f32[2048]{0:T(1024)S(1)} %bitcast.77, f32[2048]{0:T(1024)S(1)} %bitcast.68, ...), kind=kOutput, calls=%fused_computation.59 | convolution fusion | flops 12910067712 | bytes 58740736 | tf_op jit(solution)/shard_map/dot_general | solution.py:84
  1307.2 8.2 fusion.20
  1315.4 101.9 %reduce-scatter.7.cloned.1.call-done = f32[64,6]{1,0:T(8,128)} async-done(((f32[2048,6]{1,0:T(8,128)}), f32[64,6]{1,0:T(8,128)}) %reduce-scatter.7.cloned.1.call-update) | async-done | bytes 1552
  1418.8 435.2 %reduce-scatter.5.cloned.1.call-done = f32[64,6144]{1,0:T(8,128)} async-done(((f32[2048,6144]{1,0:T(8,128)}), f32[64,6144]{1,0:T(8,128)}) %reduce-scatter.5.cloned.1.call-update) | async-done | bytes 1572880 | tf_op jit(solution)/shard_map/reduce_scatter | solution.py:83
  (504 shorter events, 232.6 us)
Async XLA Ops:
  7.2 75.5 %copy-start.1 = (bf16[512,2048]{1,0:T(8,128)(2,1)S(1)}, bf16[512,2048]{1,0:T(8,128)(2,1)}, u32[]{:S(2)}) copy-start(bf16[512,2048]{1,0:T(8,128)(2,1)} %param.9) | copy-start | bytes 6291460
  7.2 161.6 %all-gather.7.cloned.1.call-start = ((), (), s32[]{:S(2)}) async-start(), calls=%async_computation.2 | async-start | bytes 25952256 | tf_op jit(solution)/shard_map/all_gather | solution.py:37
  7.9 1409.4 %reduce-scatter.7.cloned.1.call-start = ((), (), s32[]{:S(2)}) async-start(), calls=%async_computation.4 | async-start | bytes 1081344
  82.6 107.1 %copy-start.38 = (f32[512]{0:T(512)}, f32[512]{0:T(512)S(1)}, u32[]{:S(2)}) copy-start(f32[512]{0:T(512)S(1)} %broadcast_multiply_fusion.3) | copy-start | bytes 6148
  83.3 106.4 %copy-start.42 = (f32[512]{0:T(512)}, f32[512]{0:T(512)S(1)}, u32[]{:S(2)}) copy-start(f32[512]{0:T(512)S(1)} %add_rsqrt_fusion) | copy-start | bytes 6148
  83.4 106.3 %copy-start.36 = (f32[1,2048]{1,0:T(1,128)}, f32[1,2048]{1,0:T(1,128)S(1)}, u32[]{:S(2)}) copy-start(f32[1,2048]{1,0:T(1,128)S(1)} %get-tuple-element.326) | copy-start | bytes 24580
  83.4 106.3 %copy-start.40 = (f32[1,2048]{1,0:T(1,128)}, f32[1,2048]{1,0:T(1,128)S(1)}, u32[]{:S(2)}) copy-start(f32[1,2048]{1,0:T(1,128)S(1)} %get-tuple-element.325) | copy-start | bytes 24580
  83.4 106.3 %copy-start.45 = (f32[1,2048]{1,0:T(1,128)}, f32[1,2048]{1,0:T(1,128)S(1)}, u32[]{:S(2)}) copy-start(f32[1,2048]{1,0:T(1,128)S(1)} %get-tuple-element.324) | copy-start | bytes 24580
  195.0 2.0 copy-start.2
  230.8 2.0 copy-start.5
  268.1 1.3 copy-start.15
  305.3 1.0 copy-start.28
  327.2 314.5 %collective-permute-start = (f32[2048]{0:T(1024)S(1)}, f32[2048]{0:T(1024)S(1)}, u32[]{:S(2)}, u32[]{:S(2)}) collective-permute-start(f32[2048]{0:T(1024)S(1)} %bitcast.93), channel_id=1, source_target_pairs={{1,0},{2,1},{3,2},{4,3},{5,4},{6,5},{7,6},{8,7},{9,8},{10,9},{11,1... | collective-permute-start | bytes 24584 | tf_op jit(solution)/shard_map/ppermute | solution.py:27
  364.5 5.2 copy-start.17
  364.6 5.2 copy-start.19
  364.6 5.2 copy-start.21
  364.6 5.2 copy-start.32
  364.6 5.2 copy-start.34
  376.2 19.6 %copy-start.30 = (f32[128,2048]{1,0:T(8,128)S(1)}, f32[128,2048]{1,0:T(8,128)}, u32[]{:S(2)}) copy-start(f32[128,2048]{1,0:T(8,128)} %add.532) | copy-start | bytes 3145732
  400.7 4.0 copy-start.9
  400.7 4.0 copy-start.11
  400.7 5.6 copy-start.24
  404.7 2.5 copy-start.7
  404.7 3.1 copy-start.13
  404.7 3.7 copy-start.23
  410.2 1.6 slice-start
  618.5 7.9 copy-start.6
  626.4 7.8 copy-start
  634.3 2.9 copy-start.3
  640.3 33.2 %collective-permute-start.1 = (f32[2048]{0:T(1024)S(1)}, f32[2048]{0:T(1024)S(1)}, u32[]{:S(2)}, u32[]{:S(2)}) collective-permute-start(f32[2048]{0:T(1024)S(1)} %bitcast.100), channel_id=1, source_target_pairs={{1,0},{2,1},{3,2},{4,3},{5,4},{6,5},{7,6},{8,7},{9,8},{10,9},{11,1... | collective-permute-start | bytes 24584 | tf_op jit(solution)/shard_map/ppermute | solution.py:27
  679.0 2.0 copy-start.4
  782.8 1.3 copy-start.16
  820.0 1.0 copy-start.29
  911.7 5.2 copy-start.18
  911.7 5.2 copy-start.20
  911.7 5.2 copy-start.22
  911.7 5.2 copy-start.33
  911.7 5.2 copy-start.35
  923.4 19.6 %copy-start.31 = (f32[128,2048]{1,0:T(8,128)S(1)}, f32[128,2048]{1,0:T(8,128)}, u32[]{:S(2)}) copy-start(f32[128,2048]{1,0:T(8,128)} %add.575) | copy-start | bytes 3145732
  947.8 4.1 copy-start.10
  947.8 4.1 copy-start.12
  947.8 5.7 copy-start.26
  951.9 2.5 copy-start.8
  951.9 3.1 copy-start.14
  951.9 3.7 copy-start.25
  993.9 6.7 copy-start.27
  1144.1 98.8 %copy-start.44 = (f32[2048]{0:T(1024)S(1)}, f32[2048]{0:T(1024)}, u32[]{:S(2)}) copy-start(f32[2048]{0:T(1024)} %custom-call.1) | copy-start | bytes 24580
  1245.1 11.4 copy-start.37
  1245.1 11.4 copy-start.39
  1245.2 11.4 copy-start.41
  1245.2 11.4 copy-start.43
  1245.2 11.4 copy-start.46
  1282.3 571.8 %reduce-scatter.5.cloned.1.call-start = ((), (), s32[]{:S(2)}) async-start(), calls=%async_computation.3 | async-start | bytes 51904512 | tf_op jit(solution)/shard_map/reduce_scatter | solution.py:83
Sparse Core Ops, SparseCore 0:
  10.9 157.8 all-gather.6
  1282.4 134.9 reduce-scatter.6
  1425.5 428.4 reduce-scatter.4
where the time goes:
time: 1890 us; the launch traced here: 1860 us
  local copies, waits for them, and re-layouts  640 us (34%)
  waiting for transfers between devices  623 us (33%)
  blocking collectives  341 us (18%)
  other arithmetic  165 us (9%)
  matrix products  69.9 us (4%)
    reduce_scatter x1, waiting for transfers between devices, local(): lax.psum_scatter(lax.dot_general(rounded, proj_grad, (((0,), (0,)), ((),...  435 us
    all_gather x4, blocking collectives, entering(): pieces = jax.tree.map(lambda part: lax.all_gather(part, axis), value)  269 us
    slice x65, local copies, waits for them, and re-layouts, local(): lax.associative_scan(compose, (ahead[::-1], local_term[::-1]), axis=0)  211 us
    pad x32, local copies, waits for them, and re-layouts, local(): lax.associative_scan(compose, (decay, inflow), axis=0)  115 us
    pad x32, local copies, waits for them, and re-layouts, local(): lax.associative_scan(compose, (ahead[::-1], local_term[::-1]), axis=0)  115 us
    slice x61, local copies, waits for them, and re-layouts, local(): lax.associative_scan(compose, (decay, inflow), axis=0)  110 us
    unnamed x4, waiting for transfers between devices  103 us
    all_gather x1, waiting for transfers between devices, local(): lax.all_gather(weight, ('gx', 'gy'), axis=0, tiled=True)  85.4 us
  transfers between devices with their start and end apart: 5, of which 3 were waited for; matrix products, arithmetic and copies ran while one was open for 13% of the time, Pallas kernels for 0%

commit v1 on v0

--- a/solution.py
+++ b/solution.py
@@ -1,7 +1,43 @@
+import functools
+
 import jax
 import jax.numpy as jnp
 from jax import lax
+from jax.experimental import pallas as pl
+from jax.experimental.pallas import tpu as pltpu
 from jax.sharding import PartitionSpec as P
+
+MESH = pl.DeviceIdType.MESH
+F32, BF16 = jnp.float32, jnp.bfloat16
+LANES, RUNS, GROUP, HALF = 128, 8, 4, 2
+EPS = 1e-05
+
+
+def place(ny):
+    gx, gy = lax.axis_index("gx"), lax.axis_index("gy")
+    core, xx, yy = lax.rem(gx, 2), lax.rem(gx // 2, 2), gx // 4
+    return gx, gy, core, gx + 1 - 2 * core, gx + 2 - 4 * xx, gx + 4 - 8 * yy
+
+
+def remote(src, dst, send, recv, to):
+    return pltpu.make_async_remote_copy(
+        src_ref=src, dst_ref=dst, send_sem=send, recv_sem=recv, device_id=to, device_id_type=MESH
+    )
+
+
+def lanes_of(b):
+    return pl.ds(pl.multiple_of(b * LANES, LANES), LANES)
+
+
+def run_matrix(tokens, back):
+    steps = tokens // RUNS
+    row = lax.broadcasted_iota(jnp.int32, (tokens, tokens), 0)
+    col = lax.broadcasted_iota(jnp.int32, (tokens, tokens), 1)
+    if back:
+        hit = col == lax.rem(row, steps) * RUNS + row // steps
+    else:
+        hit = col == lax.rem(row, RUNS) * steps + row // RUNS
+    return jnp.where(hit, 1.0, 0.0).astype(BF16)
 
 
 def entering(value, axis, join, neutral, backward):
@@ -116,6 +152,552 @@
     return (output.astype(jnp.bfloat16), input_grad, weight_grad, vector_grad)
 
 
+def front_kernel(
+    nx, ny, units,
+    tok, cot, keep, wsrc, vsrc,
+    wall, pg, rcat, outp, grest, nrmo, invo, vecs, vsum,
+    wv, vbuf, xs, gs, nrm, rnd, pj, pv, grs, outs, pgs, perm, stage,
+    ach, bch, qch, sin, cin, m1a, m1b, m2a, m2b,
+    zs, zr, os, bs, br, dsn, dr, cs, cr, ws,
+    vzs, vzr, vxs, vxr, vo, sts, rs, rr, ro, ps, pr, po, gos, e1as, e1ar, e1bs, e1br, e2as, e2ar, e2bs, e2br,
+):
+    gx, gy, core, mate, xn, yn = place(ny)
+    tokens, width = xs.shape
+    rows = wsrc.shape[1]
+    block = rows * ny
+    groups = units // GROUP
+    glanes = GROUP * LANES
+    diag = xn + yn - gx
+    first = gx * block
+    mine = first + gy * rows
+
+    def peer_y(j):
+        return lax.rem(gy + j, ny)
+
+    def peer_x(j):
+        return lax.rem(gx + j, nx)
+
+    barrier = pltpu.get_barrier_semaphore()
+    for j in range(1, ny):
+        pl.semaphore_signal(barrier, inc=1, device_id=(gx, peer_y(j)), device_id_type=MESH)
+    for j in range(1, nx):
+        pl.semaphore_signal(barrier, inc=1, device_id=(peer_x(j), gy), device_id_type=MESH)
+
+    def band(b, n=block):
+        return pl.ds(pl.multiple_of(b, 16), n)
+
+    def stage_copy(i):
+        src = tok if i < 4 else cot
+        c = i % 4
+        return pltpu.make_async_copy(src.at[:, pl.ds(c * glanes, glanes)], stage.at[i % 2], sts.at[i % 2])
+
+    stage_copy(0).start()
+    stage_copy(1).start()
+
+    def vz(j):
+        return remote(vsrc, vbuf.at[band(mine, rows)], vzs.at[j - 1], vzr.at[j - 1], (gx, peer_y(j)))
+
+    def vx(j):
+        return remote(vbuf.at[band(first)], vbuf.at[band(first)], vxs.at[j - 1], vxr.at[j - 1], (peer_x(j), gy))
+
+    own_vec = pltpu.make_async_copy(vsrc, vbuf.at[band(mine, rows)], vo)
+
+    def z_copy(u, j):
+        return remote(wsrc.at[u], wv.at[u, band(mine, rows)], zs.at[u, j - 1], zr.at[u, j - 1], (gx, peer_y(j)))
+
+    def own_copy(u):
+        return pltpu.make_async_copy(wsrc.at[u], wv.at[u, band(mine, rows)], os.at[u])
+
+    def band_copy(u, i):
+        to = (mate, xn, yn)[i]
+        recv = cr.at[u, 0] if i == 0 else br.at[u, i - 1]
+        part = wv.at[u, band(first)]
+        return remote(part, part, bs.at[u, i], recv, (to, gy))
+
+    def diag_copy(u, i):
+        at = (xn * block, yn * block + block // 2)[i]
+        part = wv.at[u, band(at, block // 2)]
+        return remote(part, part, dsn.at[u, i], dr.at[u, i], ((yn, xn)[i], gy))
+
+    def core_copy(u, i):
+        part = wv.at[u, band((None, xn, yn, diag)[i] * block)]
+        return remote(part, part, cs.at[u, i - 1], cr.at[u, i], (mate, gy))
+
+    def keep_copy(u):
+        return pltpu.make_async_copy(wv.at[u], wall.at[u], ws.at[u])
+
+    def z_start(u):
+        own_copy(u).start()
+        for j in range(1, ny):
+            z_copy(u, j).start()
+
+    def z_wait(u):
+        own_copy(u).wait()
+        for j in range(1, ny):
+            z_copy(u, j).wait_recv()
+        for i in (1, 2, 0):
+            band_copy(u, i).start()
+
+    def xy_wait(u):
+        for i in (1, 2):
+            band_copy(u, i).wait_recv()
+        for i in (0, 1):
+            diag_copy(u, i).start()
+        for i in (1, 2):
+            core_copy(u, i).start()
+
+    def diag_wait(u):
+        for i in (0, 1):
+            diag_copy(u, i).wait_recv()
+        core_copy(u, 3).start()
+
+    def core_wait(u):
+        band_copy(u, 0).wait_recv()
+        for i in (1, 2, 3):
+            core_copy(u, i).wait_recv()
+
+    pl.semaphore_wait(barrier, nx + ny - 2)
+    own_vec.start()
+    for j in range(1, ny):
+        vz(j).start()
+    AHEAD_Z, AHEAD_B = 5, 3
+    for u in range(AHEAD_Z):
+        z_start(u)
+
+    perm[...] = run_matrix(tokens, False)
+
+    def to_runs(i, into):
+        stage_copy(i).wait()
+        c = i % 4
+        into[:, c * glanes:(c + 1) * glanes] = jnp.dot(
+            perm[...], stage[i % 2], preferred_element_type=F32
+        ).astype(BF16)
+        if i + 2 < 8:
+            stage_copy(i + 2).start()
+
+    for i in range(4):
+        to_runs(i, xs)
+    z_wait(0)
+    own_vec.wait()
+    for j in range(1, ny):
+        vz(j).wait_recv()
+    for j in range(1, nx):
+        vx(j).start()
+    z_wait(1)
+
+    BAND = 32
+
+    def moments(i, _):
+        r = pl.ds(pl.multiple_of(i * BAND, BAND), BAND)
+        x = xs[r, :].astype(F32)
+        centred = x - jnp.mean(x, axis=1, keepdims=True)
+        inv = lax.rsqrt(jnp.mean(centred * centred, axis=1, keepdims=True) + EPS)
+        nrm[r, :] = centred * inv
+        invo[r, :] = jnp.broadcast_to(inv, (BAND, LANES))
+        return 0
+
+    lax.fori_loop(0, tokens // BAND, moments, 0)
+    nrm_copy = pltpu.make_async_copy(nrm, nrmo, gos.at[0, 2])
+    nrm_copy.start()
+    for u in range(2, AHEAD_B):
+        z_wait(u)
+    for i in range(4, 8):
+        to_runs(i, gs)
+    perm[...] = run_matrix(tokens, True)
+    for j in range(1, nx):
+        vx(j).wait_recv()
+
+    for c in range(width // LANES):
+        part = vbuf[c * LANES:(c + 1) * LANES, :].astype(F32)
+        vecs[:, c * LANES:(c + 1) * LANES] = part.T[0:8, :]
+
+    def rounding(i, _):
+        r = pl.ds(pl.multiple_of(i * BAND, BAND), BAND)
+        rnd[r, :] = (nrm[r, :] * vecs[0:1, :] + vecs[1:2, :]).astype(BF16)
+        return 0
+
+    lax.fori_loop(0, tokens // BAND, rounding, 0)
+
+    quads = nx // 2
+
+    def r_own(i):
+        src = rnd.at[:, pl.ds(pl.multiple_of((2 * i + core) * block, LANES), block)]
+        return pltpu.make_async_copy(src, rcat.at[0:tokens, pl.ds(i * block, block)], ro.at[i])
+
+    def r_mate(i):
+        src = rnd.at[:, pl.ds(pl.multiple_of((2 * i + 1 - core) * block, LANES), block)]
+        dst = rcat.at[tokens:2 * tokens, pl.ds(i * block, block)]
+        return remote(src, dst, rs.at[i], rr.at[i], (mate, gy))
+
+    for i in range(quads):
+        r_own(i).start()
+        r_mate(i).start()
+
+    def e_copies(buf, send, recv, q, level):
+        if level == 0:
+            return [
+                remote(buf.at[q, gy], buf.at[q, gy], send.at[q, j - 1], recv.at[q, j - 1], (gx, peer_y(j)))
+                for j in range(1, ny)
+            ]
+        return [
+            remote(buf.at[q, gx], buf.at[q, gx], send.at[q, j - 1], recv.at[q, j - 1], (peer_x(j), gy))
+            for j in range(1, nx)
+        ]
+
+    def e_start(*a):
+        for c in e_copies(*a):
+            c.start()
+
+    def e_wait(*a):
+        for c in e_copies(*a):
+            c.wait_recv()
+
+    double = tokens // (2 * RUNS)
+
+    def project(u):
+        slot = lax.rem(u, 2 * GROUP)
+        pj[slot] = jnp.dot(rnd[...], wv[u], preferred_element_type=F32)
+
+    def vec(i, u):
+        return vecs[i:i + 1, lanes_of(u)]
+
+    def gates(u):
+        slot = lax.rem(u, 2 * GROUP)
+        gain, shift, vf, bf = (vec(i, u) for i in range(4))
+
+        def step(i, carry):
+            a, b = carry
+            r = pl.ds(pl.multiple_of(i * 16, 16), 16)
+            scaled = nrm[r, lanes_of(u)] * gain + shift
+            f = jax.nn.sigmoid(pj[slot, r, LANES:2 * LANES] + vf * scaled + bf)
+            pj[slot, r, LANES:2 * LANES] = f
+            d = f * keep[r, :]
+            inflow = (1.0 - f) * pj[slot, r, 0:LANES]
+            for h in (0, 8):
+                a = a * d[h:h + 8]
+                b = d[h:h + 8] * b + inflow[h:h + 8]
+            return a, b
+
+        a, b = lax.fori_loop(0, double, step, (jnp.ones((RUNS, LANES), F32), jnp.zeros((RUNS, LANES), F32)), unroll=4)
+        g, j = lax.rem(u // GROUP, 2), lax.rem(u, GROUP)
+        ach[g, :, lanes_of(j)] = a
+        bch[g, :, lanes_of(j)] = b
+
+    def totals(q):
+        g = lax.rem(q, 2)
+        a, b = jnp.ones((1, glanes), F32), jnp.zeros((1, glanes), F32)
+        for s in range(RUNS):
+            one = ach[g, s:s + 1, :]
+            a = a * one
+            b = one * b + bch[g, s:s + 1, :]
+        m1a[q, gy, 0:1, :] = a
+        m1a[q, gy, 1:2, :] = b
+        e_start(m1a, e1as, e1ar, q, 0)
+
+    def totals_x(q):
+        e_wait(m1a, e1as, e1ar, q, 0)
+        a, b = jnp.ones((1, glanes), F32), jnp.zeros((1, glanes), F32)
+        for s in range(ny):
+            one = m1a[q, s, 0:1, :]
+            a = a * one
+            b = one * b + m1a[q, s, 1:2, :]
+        m1b[q, gx, 0:1, :] = a
+        m1b[q, gx, 1:2, :] = b
+        e_start(m1b, e1bs, e1br, q, 1)
+
+    def enter(q):
+        e_wait(m1b, e1bs, e1br, q, 1)
+        g = lax.rem(q, 2)
+        s = jnp.zeros((1, glanes), F32)
+        s = lax.fori_loop(0, gx, lambda i, s: m1b[q, i, 0:1, :] * s + m1b[q, i, 1:2, :], s)
+        s = lax.fori_loop(0, gy, lambda i, s: m1a[q, i, 0:1, :] * s + m1a[q, i, 1:2, :], s)
+        for r in range(RUNS):
+            sin[g, r:r + 1, :] = s
+            s = ach[g, r:r + 1, :] * s + bch[g, r:r + 1, :]
+
+    def forward(u):
+        slot = lax.rem(u, 2 * GROUP)
+        g, j = lax.rem(u // GROUP, 2), lax.rem(u, GROUP)
+        vr, br_ = vec(4, u), vec(5, u)
+        zero = jnp.zeros((RUNS, LANES), F32)
+
+        def step(i, carry):
+            s, run, q, v4, v5 = carry
+            r = pl.ds(pl.multiple_of(i * 16, 16), 16)
+            f = pj[slot, r, LANES:2 * LANES]
+            k = keep[r, :]
+            inflow = (1.0 - f) * pj[slot, r, 0:LANES]
+            prevs, states = [], []
+            for h in (0, 8):
+                prev = k[h:h + 8] * s
+                s = f[h:h + 8] * prev + inflow[h:h + 8]
+                prevs.append(prev)
+                states.append(s)
+            prev, state = jnp.concatenate(prevs, 0), jnp.concatenate(states, 0)
+            x = xs[r, lanes_of(u)].astype(F32)
+            up = gs[r, lanes_of(u)].astype(F32)
+            reset = jax.nn.sigmoid(pj[slot, r, 2 * LANES:3 * LANES] + vr * prev + br_)
+            rest = 1.0 - reset
+            outs[r, lanes_of(j)] = (reset * state + rest * x).astype(BF16)
+            rg = up * (state - x) * reset * rest
+            gr = up * rest
+            pj[slot, r, 2 * LANES:3 * LANES] = rg
+            pv[slot, r, :] = prev
+            grs[g, r, lanes_of(j)] = gr
+            local = up * reset
+            d, through = f * k, k * vr * rg
+            for h in (0, 8):
+                q = q + run * through[h:h + 8]
+                run = run * d[h:h + 8]
+                q = q + run * local[h:h + 8]
+                v4 = v4 + rg[h:h + 8] * prev[h:h + 8]
+                v5 = v5 + rg[h:h + 8]
+            return s, run, q, v4, v5
+
+        init = (sin[g, :, lanes_of(j)], jnp.ones((RUNS, LANES), F32), zero, zero, zero)
+        _, _, q, v4, v5 = lax.fori_loop(0, double, step, init, unroll=4)
+        qch[g, :, lanes_of(j)] = q
+        vsum[4:5, lanes_of(u)] = jnp.sum(v4, axis=0, keepdims=True)
+        vsum[5:6, lanes_of(u)] = jnp.sum(v5, axis=0, keepdims=True)
+
+    def out_copy(q):
+        c = pl.ds(pl.multiple_of(q * glanes, LANES), glanes)
+        return pltpu.make_async_copy(stage.at[lax.rem(q, 2)], outp.at[:, c], gos.at[q, 0])
+
+    def rest_copy(q):
+        c = pl.ds(pl.multiple_of(q * glanes, LANES), glanes)
+        return pltpu.make_async_copy(grs.at[lax.rem(q, 2)], grest.at[:, c], gos.at[q, 1])
+
+    def forward_group(q):
+        enter(q)
+        pl.when(q >= 2)(lambda: (rest_copy(q - 2).wait(), out_copy(q - 2).wait())[0])
+        lax.fori_loop(0, GROUP, lambda j, _: (forward(q * GROUP + j), 0)[1], 0)
+        g = lax.rem(q, 2)
+        s = jnp.zeros((1, glanes), F32)
+        for r in reversed(range(RUNS)):
+            s = ach[g, r:r + 1, :] * s + qch[g, r:r + 1, :]
+        m2a[q, gy, 0:1, :] = s
+        e_start(m2a, e2as, e2ar, q, 0)
+        rest_copy(q).start()
+        stage[g] = jnp.dot(perm[...], outs[...], preferred_element_type=F32).astype(BF16)
+        out_copy(q).start()
+
+    def grads_x(q):
+        e_wait(m2a, e2as, e2ar, q, 0)
+        s = jnp.zeros((1, glanes), F32)
+        for r in reversed(range(ny)):
+            s = m1a[q, r, 0:1, :] * s + m2a[q, r, 0:1, :]
+        m2b[q, gx, 0:1, :] = s
+        e_start(m2b, e2bs, e2br, q, 1)
+
+    def enter_back(q):
+        e_wait(m2b, e2bs, e2br, q, 1)
+        g = lax.rem(q, 2)
+        s = jnp.zeros((1, glanes), F32)
+
+        def over_x(i, s):
+            return m1b[q, nx - 1 - i, 0:1, :] * s + m2b[q, nx - 1 - i, 0:1, :]
+
+        def over_y(i, s):
+            return m1a[q, ny - 1 - i, 0:1, :] * s + m2a[q, ny - 1 - i, 0:1, :]
+
+        s = lax.fori_loop(0, nx - 1 - gx, over_x, s)
+        s = lax.fori_loop(0, ny - 1 - gy, over_y, s)
+        for r in reversed(range(RUNS)):
+            cin[g, r:r + 1, :] = s
+            s = ach[g, r:r + 1, :] * s + qch[g, r:r + 1, :]
+
+    def pg_own(u):
+        return pltpu.make_async_copy(pgs.at[u], pg.at[u, 0:tokens], po.at[u])
+
+    def pg_mate(u):
+        return remote(pgs.at[u], pg.at[u, tokens:2 * tokens], ps.at[u], pr.at[u], (mate, gy))
+
+    def backward(u):
+        slot = lax.rem(u, 2 * GROUP)
+        g, j = lax.rem(u // GROUP, 2), lax.rem(u, GROUP)
+        gain, shift, vr = vec(0, u), vec(1, u), vec(4, u)
+        zero = jnp.zeros((RUNS, LANES), F32)
+
+        def step(i, carry):
+            c, v2, v3 = carry
+            r = pl.ds(pl.multiple_of((double - 1 - i) * 16, 16), 16)
+            f = pj[slot, r, LANES:2 * LANES]
+            k = keep[r, :]
+            rg = pj[slot, r, 2 * LANES:3 * LANES]
+            local = gs[r, lanes_of(u)].astype(F32) - grs[g, r, lanes_of(j)]
+            d, through = f * k, k * vr * rg
+            grads = [None, None]
+            for h in (1, 0):
+                part = slice(8 * h, 8 * h + 8)
+                grads[h] = local[part] + c
+                c = d[part] * grads[h] + through[part]
+            grad = jnp.concatenate(grads, 0)
+            cg = grad * (1.0 - f)
+            fg = cg * (pv[slot, r, :] - pj[slot, r, 0:LANES]) * f
+            scaled = nrm[r, lanes_of(u)] * gain + shift
+            pgs[u, r, 0:LANES] = cg.astype(BF16)
+            pgs[u, r, LANES:2 * LANES] = fg.astype(BF16)
+            pgs[u, r, 2 * LANES:3 * LANES] = rg.astype(BF16)
+            fs = fg * scaled
+            return c, v2 + fs[0:8] + fs[8:16], v3 + fg[0:8] + fg[8:16]
+
+        _, v2, v3 = lax.fori_loop(0, double, step, (cin[g, :, lanes_of(j)], zero, zero), unroll=4)
+        vsum[2:3, lanes_of(u)] = jnp.sum(v2, axis=0, keepdims=True)
+        vsum[3:4, lanes_of(u)] = jnp.sum(v3, axis=0, keepdims=True)
+        pg_own(u).start()
+        pg_mate(u).start()
+
+    def backward_group(q):
+        enter_back(q)
+        lax.fori_loop(0, GROUP, lambda j, _: (backward(q * GROUP + j), 0)[1], 0)
+
+    vsum[...] = jnp.zeros_like(vsum)
+
+    def tick(k, _):
+        u = k - 2
+        q, m = u // GROUP, lax.rem(u, GROUP)
+        pl.when(k + AHEAD_Z < units)(lambda: z_start(k + AHEAD_Z))
+        pl.when(k + AHEAD_B < units)(lambda: z_wait(k + AHEAD_B))
+        pl.when(k < units)(lambda: xy_wait(k))
+        pl.when((k >= 1) & (k <= units))(lambda: diag_wait(k - 1))
+        late = (u >= GROUP)
+        pl.when(late & (m == 0))(lambda: totals_x(q - 1))
+        pl.when(late & (m == 1))(lambda: forward_group(q - 1))
+        pl.when(late & (m == 2))(lambda: grads_x(q - 1))
+        pl.when(late & (m == 3))(lambda: backward_group(q - 1))
+
+        @pl.when((u >= 0) & (u < units))
+        def _():
+            core_wait(u)
+            keep_copy(u).start()
+            project(u)
+            gates(u)
+            pl.when(m == GROUP - 1)(lambda: totals(q))
+
+        return 0
+
+    lax.fori_loop(0, units + 2 + GROUP, tick, 0)
+
+    def drain(u, _):
+        for j in range(1, ny):
+            z_copy(u, j).wait_send()
+        for i in range(3):
+            band_copy(u, i).wait_send()
+        for i in (0, 1):
+            diag_copy(u, i).wait_send()
+        for i in (1, 2, 3):
+            core_copy(u, i).wait_send()
+        keep_copy(u).wait()
+        pg_own(u).wait()
+        pg_mate(u).wait()
+        return 0
+
+    lax.fori_loop(0, units, drain, 0)
+
+    def drain_group(q, _):
+        for a in ((m1a, e1as, e1ar, q, 0), (m1b, e1bs, e1br, q, 1), (m2a, e2as, e2ar, q, 0), (m2b, e2bs, e2br, q, 1)):
+            for c in e_copies(*a):
+                c.wait_send()
+        return 0
+
+    lax.fori_loop(0, groups, drain_group, 0)
+    for q in range(groups - 2, groups):
+        rest_copy(q).wait()
+        out_copy(q).wait()
+    nrm_copy.wait()
+    for j in range(1, ny):
+        vz(j).wait_send()
+    for j in range(1, nx):
+        vx(j).wait_send()
+    for i in range(quads):
+        r_own(i).wait()
+        r_mate(i).wait()
+
+
+def front(nx, ny, tok, cot, keep, wsrc, vsrc):
+    tokens, width = tok.shape
+    units, rows, cols = wsrc.shape
+    groups, glanes, block = units // GROUP, GROUP * LANES, rows * ny
+    dma = pltpu.SemaphoreType.DMA
+    any_, vmem = pl.BlockSpec(memory_space=pl.ANY), pl.BlockSpec(memory_space=pltpu.VMEM)
+    msg = RUNS, glanes
+    s = jax.ShapeDtypeStruct
+    return pl.pallas_call(
+        functools.partial(front_kernel, nx, ny, units),
+        out_shape=(
+            s((units, width, cols), BF16), s((units, 2 * tokens, cols), BF16), s((2 * tokens, width // 2), BF16),
+            s((tokens, width), BF16), s((tokens, width), F32), s((tokens, width), F32), s((tokens, LANES), F32),
+            s((8, width), F32), s((8, width), F32),
+        ),
+        in_specs=[any_, any_, vmem, any_, any_],
+        out_specs=(any_,) * 6 + (vmem,) * 3,
+        scratch_shapes=[
+            pltpu.VMEM((units, width, cols), BF16),
+            pltpu.VMEM((width, LANES), BF16),
+            pltpu.VMEM((tokens, width), BF16),
+            pltpu.VMEM((tokens, width), BF16),
+            pltpu.VMEM((tokens, width), F32),
+            pltpu.VMEM((tokens, width), BF16),
+            pltpu.VMEM((2 * GROUP, tokens, cols), F32),
+            pltpu.VMEM((2 * GROUP, tokens, LANES), F32),
+            pltpu.VMEM((2, tokens, glanes), F32),
+            pltpu.VMEM((tokens, glanes), BF16),
+            pltpu.VMEM((units, tokens, cols), BF16),
+            pltpu.VMEM((tokens, tokens), BF16),
+            pltpu.VMEM((2, tokens, glanes), BF16),
+            pltpu.VMEM((2,) + msg, F32), pltpu.VMEM((2,) + msg, F32), pltpu.VMEM((2,) + msg, F32),
+            pltpu.VMEM((2,) + msg, F32), pltpu.VMEM((2,) + msg, F32),
+            pltpu.VMEM((groups, ny) + msg, F32), pltpu.VMEM((groups, nx) + msg, F32),
+            pltpu.VMEM((groups, ny) + msg, F32), pltpu.VMEM((groups, nx) + msg, F32),
+            dma((units, ny - 1)), dma((units, ny - 1)), dma((units,)), dma((units, 3)), dma((units, 2)),
+            dma((units, 2)), dma((units, 2)), dma((units, 3)), dma((units, 4)), dma((units,)),
+            dma((ny - 1,)), dma((ny - 1,)), dma((nx - 1,)), dma((nx - 1,)), dma, dma((2,)),
+            dma((nx // 2,)), dma((nx // 2,)), dma((nx // 2,)), dma((units,)), dma((units,)), dma((units,)),
+            dma((groups, 3)),
+            dma((groups, ny - 1)), dma((groups, ny - 1)), dma((groups, nx - 1)), dma((groups, nx - 1)),
+            dma((groups, ny - 1)), dma((groups, ny - 1)), dma((groups, nx - 1)), dma((groups, nx - 1)),
+        ],
+        compiler_params=pltpu.CompilerParams(
+            collective_id=0, has_side_effects=True, vmem_limit_bytes=61 * 2**20
+        ),
+        cost_estimate=pl.CostEstimate(
+            flops=2 * tokens * width * units * cols, bytes_accessed=2 * width * units * cols, transcendentals=0
+        ),
+    )(tok, cot, keep, wsrc, vsrc)
+
+
+def fast(nx, ny, tokens, reset_mask, weight, vectors, cotangent):
+    count, width = tokens.shape
+    rows = weight.shape[0]
+    units, steps = width // LANES, count // RUNS
+    keep = (1 - reset_mask).astype(F32).reshape(RUNS, steps).T.reshape(count, 1)
+    keep = jnp.broadcast_to(keep, (count, LANES))
+    wsrc = weight.reshape(rows, 3, units, LANES).transpose(2, 0, 1, 3).reshape(units, rows, 3 * LANES)
+    vsrc = jnp.pad(vectors.T, ((0, 0), (0, LANES - 6)))
+    wall, pg, rcat, outp, grest, nrm, inv, vecs, vsum = front(nx, ny, tokens, cotangent, keep, wsrc, vsrc)
+    rounded = (nrm * vecs[0] + vecs[1]).astype(BF16)
+    own = pg[:, :count].transpose(1, 0, 2).reshape(count, units, 3, LANES).transpose(0, 2, 1, 3).reshape(count, 3 * width)
+    weight_grad = lax.psum_scatter(
+        lax.dot_general(rounded, own, (((0,), (0,)), ((), ())), preferred_element_type=F32),
+        ("gx", "gy"), scatter_dimension=0, tiled=True,
+    )
+    flat = pg[:, :count].transpose(1, 0, 2).reshape(count, 3 * width)
+    wflat = wall.transpose(1, 0, 2).reshape(width, 3 * width)
+    scaled_grad = lax.dot_general(flat, wflat, (((1,), (1,)), ((), ())), preferred_element_type=F32)
+    scaled_grad = scaled_grad + own[:, width:2 * width].astype(F32) * vecs[2]
+    terms = jnp.concatenate([
+        jnp.sum(scaled_grad * nrm, axis=0)[None], jnp.sum(scaled_grad, axis=0)[None], vsum[2:6],
+    ], 0)
+    vector_grad = lax.psum_scatter(terms, ("gx", "gy"), scatter_dimension=1, tiled=True)
+    n = scaled_grad * vecs[0]
+    grad = grest + inv[:, :1] * (
+        n - jnp.mean(n, axis=1, keepdims=True) - nrm * jnp.mean(n * nrm, axis=1, keepdims=True)
+    )
+    grad = grad.reshape(steps, RUNS, width).transpose(1, 0, 2).reshape(count, width)
+    return outp, grad, weight_grad, vector_grad
+
+
 def solution(mesh):
     placed = (
         P(("gx", "gy"), None),
@@ -124,8 +706,16 @@
         P(None, ("gx", "gy")),
         P(("gx", "gy"), None),
     )
+    nx, ny = mesh.shape["gx"], mesh.shape["gy"]
+
+    def body(tokens, reset_mask, weight, vectors, cotangent):
+        whole_tiles = weight.shape[0] % 16 == 0 and tokens.shape[0] % 256 == 0
+        if nx == 8 and whole_tiles and (weight.shape[0] * ny) % 256 == 0 and tokens.shape[1] % 2048 == 0:
+            return fast(nx, ny, tokens, reset_mask, weight, vectors, cotangent)
+        return local(tokens, reset_mask, weight, vectors, cotangent)
+
     return jax.shard_map(
-        local,
+        body,
         mesh=mesh,
         in_specs=placed,
         out_specs=(

time: 1890 us -> 824 us (0.44); the launches traced: 1860 us -> 823 us
  local copies, waits for them, and re-layouts: 640 us -> 45.5 us
  blocking collectives: 341 us -> 0 us
  Pallas kernels: 0 us -> 179 us
  other arithmetic: 165 us -> 6.4 us
  waiting for transfers between devices: 623 us -> 533 us
  matrix products: 69.9 us -> 45.3 us
    all_gather x5 -> x0, blocking collectives: 341 us -> none  [the longest x4 269 us: entering(): pieces = jax.tree.map(lambda part: lax.all_gather(part, axis), value)]
    slice x130 -> x3, local copies, waits for them, and re-layouts: 324 us -> 1.96 us  [the longest x1 0.97 us: fast(): rounded = (nrm * vecs[0] + vecs[1]).astype(BF16)]
    pad x64 -> x1, local copies, waits for them, and re-layouts: 229 us -> 0.61 us  [fast(): vsrc = jnp.pad(vectors.T, ((0, 0), (0, LANES - 6)))]
    pallas_call x0 -> x1, Pallas kernels: none -> 179 us  [front(): pl.pallas_call(functools.partial(front_kernel, nx, ny, units), out_shape=...]
    all_gather x1 -> x0, waiting for transfers between devices: 85.4 us -> none  [local(): lax.all_gather(weight, ('gx', 'gy'), axis=0, tiled=True)]
    rev x4 -> x0, local copies, waits for them, and re-layouts: 66.2 us -> none  [the longest x1 32.7 us: local(): mult_back = flip_mult[::-1]]
    add x36 -> x0, other arithmetic: 65.8 us -> none  [the longest x18 28.7 us: local(): lax.associative_scan(compose, (ahead[::-1], local_term[::-1]), axis=0)]
    mul x34 -> x0, other arithmetic: 48 us -> none  [the longest x32 38.5 us: compose(): return (earlier[0] * later[0], later[0] * earlier[1] + later[1])]
  transfers between devices with their start and end apart: 5 -> 2, of which waited for: 3 -> 2; matrix products, arithmetic and copies ran while one was open for 13% -> 4% of each run, Pallas kernels for 0% -> 0%
where the time goes in v1:
time: 824 us; the launch traced here: 823 us
  waiting for transfers between devices  533 us (65%)
  Pallas kernels  179 us (22%)
  local copies, waits for them, and re-layouts  45.5 us (6%)
  matrix products  45.3 us (5%)
  between operations  14.1 us (2%)
    reduce_scatter x1, waiting for transfers between devices, fast(): lax.psum_scatter(lax.dot_general(rounded, own, (((0,), (0,)), ((), ())),...  435 us
    pallas_call x1, Pallas kernels, front(): pl.pallas_call(functools.partial(front_kernel, nx, ny, units), out_shape=...  179 us
    unnamed x3, waiting for transfers between devices  97.7 us
    dot_general x1, matrix products, fast(): lax.dot_general(rounded, own, (((0,), (0,)), ((), ())), preferred_element...  24.7 us
    dot_general x1, matrix products, fast(): lax.dot_general(flat, wflat, (((1,), (1,)), ((), ())), preferred_element_...  20.6 us
  transfers between devices with their start and end apart: 2, of which 2 were waited for; matrix products, arithmetic and copies ran while one was open for 4% of the time, Pallas kernels for 0%

profile of v1, /device:TPU:0, one launch (start us, length us, event | category | flops | bytes accessed | tf_op | source)
XLA Modules:
  0.0 823.1 jit_solution(11310910625711191248)
XLA Ops:
  7.2 0.0 reduce-scatter.7.cloned.1.call-start
  7.2 0.7 subtract_convert_fusion
  7.9 0.1 reshape.41
  8.0 0.8 copy.26
  8.8 0.1 copy.24
  8.8 0.1 broadcast_in_dim.15
  8.9 1.3 copy.32
  10.2 0.5 copy.38
  10.7 1.4 reshape.43.wsrc
  12.2 0.6 pad.4.vsrc
  12.8 0.8 broadcast_in_dim.16.keep
  13.6 179.1 %shard_map.84 = (bf16[16,2048,384]{2,1,0:T(8,128)(2,1)}, bf16[16,1024,384]{2,1,0:T(8,128)(2,1)}, bf16[1024,1024]{1,0:T(8,128)(2,1)}, bf16[512,2048]{1,0:T(8,128)...) custom-call(bf16[512,2048]{1,0:T(8,128)(2,1)} %tok.1, ...), custom_call_target="tpu_custom_call" | custom-call | flops 12884901888 | bytes 25165824 | tf_op jit(solution)/shard_map/pallas_call | solution.py:626
  192.7 1.0 fusion.7
  193.7 0.8 slice.29
  194.5 6.2 slice_bitcast_fusion
  200.7 8.7 %copy.27 = bf16[512,16,384]{0,2,1:T(8,128)(2,1)} copy(bf16[512,16,384]{2,0,1:T(8,128)(2,1)} %slice_bitcast_fusion) | data formatting | bytes 12582912 | tf_op jit(solution)/shard_map/transpose | solution.py:685
  209.4 9.0 %copy.28 = bf16[512,3,16,128]{3,2,1,0:T(8,128)(2,1)} copy(bf16[512,3,16,128]{0,3,1,2:T(8,128)(2,1)} %bitcast.45) | data formatting | bytes 12582912 | tf_op jit(solution)/shard_map/transpose | solution.py:680
  218.4 0.0 copy-start
  218.4 4.6 copy.37
  222.9 0.0 copy-done
  222.9 20.6 %multiply_reduce_fusion = (f32[2048]{0:T(1024)S(1)}, f32[512]{0:T(512)S(1)}, f32[512]{0:T(512)S(1)}, f32[2048]{0:T(1024)S(1)}, f32[512,2048]{1,0:T(8,128)}) fusion(f32[512,2048]{1,0:T(8,128)S(1)} %copy-done, f32[2048]{0:T(1024)S(1)} %bitcast.53, f32[2048]{0:T(1024)S(1)} %bitcast.61, bf16[512,6144]{1,0:T(8,128)(2,1)S(1)} %bitcast.46, ...), kind=kOutput, calls=%fused_computation.5 | convolution fusion | flops 12895383552 | bytes 41979904 | tf_op jit(solution)/shard_map/dot_general | solution.py:687
  243.6 1.3 copy.30
  244.9 0.0 reduce-scatter.7.cloned.1.call-update
  244.9 0.0 reduce-scatter.5.cloned.1.call-start
  245.0 24.7 %fusion.4 = f32[2048,6144]{1,0:T(8,128)} fusion(f32[512,2048]{1,0:T(8,128)} %get-tuple-element.18, f32[2048]{0:T(1024)S(1)} %bitcast.60, f32[2048]{0:T(1024)S(1)} %bitcast.54, bf16[64,8,48,128]{3,2,1,0:T(8,128)(2,1)} %bitcast.44), kind=kOutput, calls=%fused_computation.10 | convolution fusion | flops 12888047616 | bytes 60833792 | tf_op jit(solution)/shard_map/dot_general | solution.py:682
  269.6 0.0 copy-start.2
  269.6 0.0 reduce-scatter.5.cloned.1.call-update
  269.7 0.9 copy-done.2
  270.6 0.1 slice_reduce_fusion
  270.8 5.7 add_bitcast_fusion
  276.4 0.0 copy-start.1
  276.5 4.4 copy.29
  280.9 97.6 %reduce-scatter.7.cloned.1.call-done = f32[64,6]{1,0:T(8,128)} async-done(((f32[2048,6]{1,0:T(8,128)}), f32[64,6]{1,0:T(8,128)}) %reduce-scatter.7.cloned.1.call-update) | async-done | bytes 1552
  378.5 1.4 copy.31
  380.0 435.0 %reduce-scatter.5.cloned.1.call-done = f32[64,6144]{1,0:T(8,128)} async-done(((f32[2048,6144]{1,0:T(8,128)}), f32[64,6144]{1,0:T(8,128)}) %reduce-scatter.5.cloned.1.call-update) | async-done | bytes 1572880 | tf_op jit(solution)/shard_map/reduce_scatter | solution.py:681
  815.0 0.0 copy-done.1
  815.0 1.3 copy.40
  (2 shorter events, 0.0 us)
Async XLA Ops:
  7.2 371.4 %reduce-scatter.7.cloned.1.call-start = ((), (), s32[]{:S(2)}) async-start(), calls=%async_computation.3 | async-start | bytes 1081344
  218.4 4.6 copy-start
  244.9 570.0 %reduce-scatter.5.cloned.1.call-start = ((), (), s32[]{:S(2)}) async-start(), calls=%async_computation.2 | async-start | bytes 51904512 | tf_op jit(solution)/shard_map/reduce_scatter | solution.py:681
  269.6 0.9 copy-start.2
  276.4 538.5 %copy-start.1 = (bf16[512,2048]{1,0:T(8,128)(2,1)S(1)}, bf16[512,2048]{1,0:T(8,128)(2,1)}, u32[]{:S(2)}) copy-start(bf16[512,2048]{1,0:T(8,128)(2,1)} %get-tuple-element.34) | copy-start | bytes 6291460
Sparse Core Ops, SparseCore 0:
  245.0 133.4 reduce-scatter.6
  386.7 428.2 reduce-scatter.4

commit v2 on v1

--- a/solution.py
+++ b/solution.py
@@ -667,6 +667,265 @@
     )(tok, cot, keep, wsrc, vsrc)
 
 
+def back_kernel(
+    nx, ny, units,
+    pg, rcat, wall, nrmi, inv, resti, vecs, vsum,
+    igo, wgo, vgo,
+    rt, rbuf, pgb, wb, sb, rd, rx, ry, rz, zb, sg, nrm, rest, vtot, vin, perm, outb,
+    lds, pgl, wl, dsn, drc, xsn, xrc, ysn, yrc, zsn, zrc, vsn, vrc, ous,
+):
+    gx, gy, core, mate, xn, yn = place(ny)
+    tokens, width = sg.shape
+    cols = pgb.shape[2]
+    block = zb.shape[1]
+    half, rows = block // 2, block // ny
+    diag = xn + yn - gx
+    count = nx * ny
+    me = gx * ny + gy
+
+    barrier = pltpu.get_barrier_semaphore()
+
+    def greet(j, _):
+        to = lax.rem(me + j, count)
+        pl.semaphore_signal(barrier, inc=1, device_id=(to // ny, lax.rem(to, ny)), device_id_type=MESH)
+        return 0
+
+    lax.fori_loop(1, count, greet, 0)
+
+    def pg_load(u):
+        return pltpu.make_async_copy(pg.at[u], pgb.at[lax.rem(u, 2)], pgl.at[lax.rem(u, 2)])
+
+    def w_load(u):
+        return pltpu.make_async_copy(wall.at[u], wb.at[lax.rem(u, 2)], wl.at[lax.rem(u, 2)])
+
+    r_load = pltpu.make_async_copy(rcat, rbuf, lds.at[0])
+    r_load.start()
+    pg_load(0).start()
+    w_load(0).start()
+    nrm_load = pltpu.make_async_copy(nrmi, nrm, lds.at[1])
+    rest_load = pltpu.make_async_copy(resti, rest, lds.at[2])
+    nrm_load.start()
+    rest_load.start()
+
+    def rows_of(chip, part, n=half):
+        return pl.ds(pl.multiple_of((chip // 2) * block + part * half, 16), n)
+
+    def d_copy(u, i):
+        return remote(
+            sb.at[u, rows_of(diag, i)], rd.at[u, i * half:(i + 1) * half], dsn.at[u, i], drc.at[u, i], ((yn, xn)[i], gy)
+        )
+
+    def x_copy(u, i):
+        return remote(sb.at[u, rows_of(xn, i)], rx.at[u, i * half:(i + 1) * half], xsn.at[u, i], xrc.at[u, i], (xn, gy))
+
+    def y_copy(u, i):
+        return remote(sb.at[u, rows_of(yn, i)], ry.at[u, i * half:(i + 1) * half], ysn.at[u, i], yrc.at[u, i], (yn, gy))
+
+    def z_copy(u, j):
+        to = lax.rem(gy + j, ny)
+        src = zb.at[u, pl.ds(pl.multiple_of(to * rows, 16), rows)]
+        return remote(src, rz.at[u, j - 1], zsn.at[u, j - 1], zrc.at[u, j - 1], (gx, to))
+
+    r_load.wait()
+    rt[...] = rbuf[...].T
+    sg[...] = jnp.zeros_like(sg)
+    pl.semaphore_wait(barrier, count - 1)
+
+    def weigh(u):
+        slot = lax.rem(u, 2)
+        pg_load(u).wait()
+
+        @pl.when(u + 1 < units)
+        def _():
+            pg_load(u + 1).start()
+
+        sb[u] = jnp.dot(rt[...], pgb[slot], preferred_element_type=F32).astype(BF16)
+        for i in (0, 1):
+            d_copy(u, i).start()
+        x_copy(u, 1).start()
+        y_copy(u, 0).start()
+        w_load(u).wait()
+
+        @pl.when(u + 1 < units)
+        def _():
+            w_load(u + 1).start()
+
+        mine = pgb[slot, 0:tokens, :]
+        sg[...] += lax.dot_general(mine, wb[slot], (((1,), (1,)), ((), ())), preferred_element_type=F32)
+        sg[:, lanes_of(u)] += pgb[slot, 0:tokens, LANES:2 * LANES].astype(F32) * vecs[2:3, lanes_of(u)]
+
+    def fold(into, at, more):
+        into[at] = (into[at].astype(F32) + more.astype(F32)).astype(BF16)
+
+    def meet(u):
+        for i in (0, 1):
+            d_copy(u, i).wait_recv()
+        own = sb.at[u]
+        fold(own, (rows_of(xn, 0), slice(None)), rd[u, 0:half])
+        x_copy(u, 0).start()
+        fold(own, (rows_of(yn, 1), slice(None)), rd[u, half:block])
+        y_copy(u, 1).start()
+
+    def column(u):
+        for i in (0, 1):
+            x_copy(u, i).wait_recv()
+            y_copy(u, i).wait_recv()
+        total = sb[u, rows_of(gx, 0, block), :].astype(F32) + rx[u].astype(F32) + ry[u].astype(F32)
+        zb[u] = total.astype(BF16)
+        for j in range(1, ny):
+            z_copy(u, j).start()
+
+    def settle(u):
+        r = pl.ds(pl.multiple_of(gy * rows, 16), rows)
+        at = pl.ds(pl.multiple_of((gx // 2) * block + gy * rows, 16), rows)
+        total = sb[u, at, :].astype(F32) + rx[u, r, :].astype(F32) + ry[u, r, :].astype(F32)
+        for j in range(1, ny):
+            z_copy(u, j).wait_recv()
+        for j in range(1, ny):
+            total = total + rz[u, j - 1].astype(F32)
+        for i in range(3):
+            wgo[:, lanes_of(u + i * units)] = total[:, i * LANES:(i + 1) * LANES]
+
+    BAND = 32
+    bands = tokens // BAND
+
+    def finish(i, _):
+        r = pl.ds(pl.multiple_of(i * BAND, BAND), BAND)
+        s, z = sg[r, :], nrm[r, :]
+        sz = s * z
+        gain = vecs[0:1, :]
+        vtot_rows[0][...] += jnp.sum(sz.reshape(BAND // 8, 8, width), axis=0)
+        vtot_rows[1][...] += jnp.sum(s.reshape(BAND // 8, 8, width), axis=0)
+        n = s * gain
+        m1 = jnp.mean(n, axis=1, keepdims=True)
+        m2 = jnp.mean(sz * gain, axis=1, keepdims=True)
+        sg[r, :] = rest[r, :] + inv[r, 0:1] * (n - m1 - z * m2)
+        return 0
+
+    vtot_rows = (outb.at[0, 0:8, :], outb.at[0, 8:16, :])
+
+    def v_copy(j):
+        to = lax.rem(me + j, count)
+        return remote(vtot.at[to // 2], vin.at[me], vsn.at[to], vrc.at[me], (to // ny, lax.rem(to, ny)))
+
+    def v_recv(j):
+        at = lax.rem(me + j, count)
+        return remote(vtot.at[0], vin.at[at], vsn.at[at], vrc.at[at], (at // ny, lax.rem(at, ny)))
+
+    def vectors_out():
+        zero = jnp.zeros((2, LANES), F32)
+        for c in range(width // LANES):
+            at = slice(c * LANES, (c + 1) * LANES)
+            top = [jnp.sum(v[:, at], axis=0, keepdims=True) for v in vtot_rows]
+            vtot[c] = jnp.concatenate(top + [vsum[2:6, at], zero], 0)
+        lax.fori_loop(1, count, lambda j, _: (v_copy(j).start(), 0)[1], 0)
+
+    chunk = outb.shape[2] // 4
+
+    def out_copy(c):
+        return pltpu.make_async_copy(rest.at[:, pl.ds(c * chunk, chunk)], igo.at[:, pl.ds(c * chunk, chunk)], ous.at[c])
+
+    def natural():
+        perm[...] = run_matrix(tokens, True)
+        for c in range(4):
+            at = slice(c * chunk, (c + 1) * chunk)
+            v = sg[:, at]
+            high = v.astype(BF16)
+            low = (v - high.astype(F32)).astype(BF16)
+            rest[:, at] = jnp.dot(perm[...], high, preferred_element_type=F32) + jnp.dot(
+                perm[...], low, preferred_element_type=F32
+            )
+            out_copy(c).start()
+
+    LAG1, LAG2, LAG3 = 2, 4, 6
+
+    def tick(k, _):
+        pl.when(k < units)(lambda: weigh(k))
+        pl.when((k >= LAG1) & (k < units + LAG1))(lambda: meet(k - LAG1))
+        pl.when((k >= LAG2) & (k < units + LAG2))(lambda: column(k - LAG2))
+        pl.when(k >= LAG3)(lambda: settle(k - LAG3))
+
+        @pl.when(k == units)
+        def _():
+            nrm_load.wait()
+            rest_load.wait()
+            for v in vtot_rows:
+                v[...] = jnp.zeros_like(v)
+            lax.fori_loop(0, bands // 2, finish, 0)
+
+        @pl.when(k == units + 1)
+        def _():
+            lax.fori_loop(bands // 2, bands, finish, 0)
+            vectors_out()
+
+        pl.when(k == units + 2)(natural)
+        return 0
+
+    lax.fori_loop(0, units + LAG3, tick, 0)
+
+    lax.fori_loop(1, count, lambda j, _: (v_recv(j).wait_recv(), 0)[1], 0)
+    vin[me] = vtot[me // 2]
+    vgo[...] = lax.fori_loop(0, count, lambda j, s: s + vin[j], jnp.zeros((8, LANES), F32))
+
+    def drain(u, _):
+        for i in (0, 1):
+            d_copy(u, i).wait_send()
+            x_copy(u, i).wait_send()
+            y_copy(u, i).wait_send()
+        for j in range(1, ny):
+            z_copy(u, j).wait_send()
+        return 0
+
+    lax.fori_loop(0, units, drain, 0)
+    lax.fori_loop(1, count, lambda j, _: (v_copy(j).wait_send(), 0)[1], 0)
+    for c in range(4):
+        out_copy(c).wait()
+
+
+def back(nx, ny, pg, rcat, wall, nrm, inv, rest, vecs, vsum):
+    units, both, cols = pg.shape
+    tokens, width = nrm.shape
+    block = width // nx
+    rows = block // ny
+    dma = pltpu.SemaphoreType.DMA
+    any_, vmem = pl.BlockSpec(memory_space=pl.ANY), pl.BlockSpec(memory_space=pltpu.VMEM)
+    s = jax.ShapeDtypeStruct
+    return pl.pallas_call(
+        functools.partial(back_kernel, nx, ny, units),
+        out_shape=(s((tokens, width), F32), s((rows, 3 * width), F32), s((8, LANES), F32)),
+        in_specs=[any_, any_, any_, any_, vmem, any_, vmem, vmem],
+        out_specs=(any_, vmem, vmem),
+        scratch_shapes=[
+            pltpu.VMEM((width // 2, both), BF16),
+            pltpu.VMEM((both, width // 2), BF16),
+            pltpu.VMEM((2, both, cols), BF16),
+            pltpu.VMEM((2, width, cols), BF16),
+            pltpu.VMEM((units, width // 2, cols), BF16),
+            pltpu.VMEM((units, block, cols), BF16),
+            pltpu.VMEM((units, block, cols), BF16),
+            pltpu.VMEM((units, block, cols), BF16),
+            pltpu.VMEM((units, ny - 1, rows, cols), BF16),
+            pltpu.VMEM((units, block, cols), BF16),
+            pltpu.VMEM((tokens, width), F32),
+            pltpu.VMEM((tokens, width), F32),
+            pltpu.VMEM((tokens, width), F32),
+            pltpu.VMEM((width // LANES, 8, LANES), F32),
+            pltpu.VMEM((nx * ny, 8, LANES), F32),
+            pltpu.VMEM((tokens, tokens), BF16),
+            pltpu.VMEM((1, 16, width), F32),
+            dma((3,)), dma((2,)), dma((2,)),
+            dma((units, 2)), dma((units, 2)), dma((units, 2)), dma((units, 2)), dma((units, 2)), dma((units, 2)),
+            dma((units, ny - 1)), dma((units, ny - 1)), dma((nx * ny,)), dma((nx * ny,)), dma((4,)),
+        ],
+        compiler_params=pltpu.CompilerParams(
+            collective_id=1, has_side_effects=True, vmem_limit_bytes=61 * 2**20
+        ),
+        cost_estimate=pl.CostEstimate(
+            flops=4 * tokens * width * units * cols, bytes_accessed=2 * width * units * cols, transcendentals=0
+        ),
+    )(pg, rcat, wall, nrm, inv, rest, vecs, vsum)
+
+
 def fast(nx, ny, tokens, reset_mask, weight, vectors, cotangent):
     count, width = tokens.shape
     rows = weight.shape[0]
@@ -676,25 +935,9 @@
     wsrc = weight.reshape(rows, 3, units, LANES).transpose(2, 0, 1, 3).reshape(units, rows, 3 * LANES)
     vsrc = jnp.pad(vectors.T, ((0, 0), (0, LANES - 6)))
     wall, pg, rcat, outp, grest, nrm, inv, vecs, vsum = front(nx, ny, tokens, cotangent, keep, wsrc, vsrc)
-    rounded = (nrm * vecs[0] + vecs[1]).astype(BF16)
-    own = pg[:, :count].transpose(1, 0, 2).reshape(count, units, 3, LANES).transpose(0, 2, 1, 3).reshape(count, 3 * width)
-    weight_grad = lax.psum_scatter(
-        lax.dot_general(rounded, own, (((0,), (0,)), ((), ())), preferred_element_type=F32),
-        ("gx", "gy"), scatter_dimension=0, tiled=True,
-    )
-    flat = pg[:, :count].transpose(1, 0, 2).reshape(count, 3 * width)
-    wflat = wall.transpose(1, 0, 2).reshape(width, 3 * width)
-    scaled_grad = lax.dot_general(flat, wflat, (((1,), (1,)), ((), ())), preferred_element_type=F32)
-    scaled_grad = scaled_grad + own[:, width:2 * width].astype(F32) * vecs[2]
-    terms = jnp.concatenate([
-        jnp.sum(scaled_grad * nrm, axis=0)[None], jnp.sum(scaled_grad, axis=0)[None], vsum[2:6],
-    ], 0)
-    vector_grad = lax.psum_scatter(terms, ("gx", "gy"), scatter_dimension=1, tiled=True)
-    n = scaled_grad * vecs[0]
-    grad = grest + inv[:, :1] * (
-        n - jnp.mean(n, axis=1, keepdims=True) - nrm * jnp.mean(n * nrm, axis=1, keepdims=True)
-    )
-    grad = grad.reshape(steps, RUNS, width).transpose(1, 0, 2).reshape(count, width)
+    grad, weight_grad, tile = back(nx, ny, pg, rcat, wall, nrm, inv, grest, vecs, vsum)
+    odd = lax.rem(lax.axis_index("gx") * ny + lax.axis_index("gy"), 2) == 1
+    vector_grad = jnp.where(odd, tile[:6, rows:2 * rows], tile[:6, :rows])
     return outp, grad, weight_grad, vector_grad
 
 
@@ -710,7 +953,7 @@
 
     def body(tokens, reset_mask, weight, vectors, cotangent):
         whole_tiles = weight.shape[0] % 16 == 0 and tokens.shape[0] % 256 == 0
-        if nx == 8 and whole_tiles and (weight.shape[0] * ny) % 256 == 0 and tokens.shape[1] % 2048 == 0:
+        if nx == 8 and whole_tiles and 2 * weight.shape[0] == LANES and tokens.shape[1] % 2048 == 0:
             return fast(nx, ny, tokens, reset_mask, weight, vectors, cotangent)
         return local(tokens, reset_mask, weight, vectors, cotangent)
 

time: 824 us -> 321 us (0.39)
  waiting for transfers between devices: 533 us -> 0 us
  Pallas kernels: 179 us -> 306 us
  matrix products: 45.3 us -> 0 us
  local copies, waits for them, and re-layouts: 45.5 us -> 11.7 us
  between operations: 14.1 us -> 0.69 us
    reduce_scatter x1 -> x0, waiting for transfers between devices: 435 us -> none  [fast(): lax.psum_scatter(lax.dot_general(rounded, own, (((0,), (0,)), ((), ())),...]
    pallas_call x0 -> x1, Pallas kernels: none -> 127 us  [back(): pl.pallas_call(functools.partial(back_kernel, nx, ny, units), out_shape=(...]
    unnamed x3 -> x0, waiting for transfers between devices: 97.7 us -> none
    dot_general x2 -> x0, matrix products: 45.3 us -> none  [the longest x1 24.7 us: fast(): lax.dot_general(rounded, own, (((0,), (0,)), ((), ())), preferred_element...]
    transpose x4 -> x0, local copies, waits for them, and re-layouts: 28.3 us -> none  [the longest x2 14.9 us: fast(): flat = pg[:, :count].transpose(1, 0, 2).reshape(count, 3 * width)]
  transfers between devices with their start and end apart: 2 -> 0, of which waited for: 2 -> 0; matrix products, arithmetic and copies ran while one was open for 4% -> 0% of each run, Pallas kernels for 0% -> 0%
where the time goes in v2:
time: 321 us
  Pallas kernels  306 us (95%)
  local copies, waits for them, and re-layouts  11.7 us (4%)
    pallas_call x1, Pallas kernels, front(): pl.pallas_call(functools.partial(front_kernel, nx, ny, units), out_shape=...  179 us
    pallas_call x1, Pallas kernels, back(): pl.pallas_call(functools.partial(back_kernel, nx, ny, units), out_shape=(...  127 us
    unnamed x13, local copies, waits for them, and re-layouts  8.01 us

profile of v2, /device:TPU:0, one launch (start us, length us, event | category | flops | bytes accessed | tf_op | source)
XLA Modules:
  0.0 320.5 jit_solution(712893024123565207)
XLA Ops:
  0.6 0.7 subtract_convert_fusion
  1.3 0.1 reshape.19
  1.4 0.1 copy.13
  1.5 0.1 broadcast_in_dim.7
  1.6 0.8 broadcast_in_dim.8.keep
  2.4 1.3 copy.16
  3.7 0.0 copy-start.3
  3.7 0.5 copy.18
  4.2 1.4 reshape.21.wsrc
  5.6 0.0 copy-done.3
  5.6 0.1 copy.15
  5.8 0.6 pad.4.vsrc
  6.4 179.1 %shard_map.84 = (bf16[16,2048,384]{2,1,0:T(8,128)(2,1)}, bf16[16,1024,384]{2,1,0:T(8,128)(2,1)}, bf16[1024,1024]{1,0:T(8,128)(2,1)}, bf16[512,2048]{1,0:T(8,128)...) custom-call(bf16[512,2048]{1,0:T(8,128)(2,1)} %tok.1, ...), custom_call_target="tpu_custom_call" | custom-call | flops 12884901888 | bytes 25165824 | tf_op jit(solution)/shard_map/pallas_call | solution.py:626
  185.5 0.0 copy-start.1
  185.5 127.0 %shard_map.85 = (f32[512,2048]{1,0:T(8,128)}, f32[64,6144]{1,0:T(8,128)}, f32[8,128]{1,0:T(8,128)}) custom-call(bf16[16,1024,384]{2,1,0:T(8,128)(2,1)} %get-tuple-element.17.pg, bf16[1024,1024]{1,0:T(8,128)(2,1)} %get-tuple-element.18.rcat, bf16[16,2048,384]{2,1,0:T(8,128)(2,1)} %get-tuple-element.19.wall, f32[512,2048]{1,0:T(8,128)} %get-tuple-element.20.nrmi, ...), custom_call_target="tpu_custom_call" | custom-call | flops 25769803776 | bytes 25165824 | tf_op jit(solution)/shard_map/pallas_call | solution.py:893
  312.5 1.4 slice_select_fusion
  313.9 0.0 copy-done.1
  313.9 0.0 copy-start
  313.9 1.3 copy.22
  315.2 1.6 copy-done
  316.8 0.0 copy-start.2
  316.8 2.0 copy.23
  318.9 0.5 copy-done.2
  319.4 1.1 copy.24
Async XLA Ops:
  3.7 2.0 copy-start.3
  185.5 128.4 %copy-start.1 = (bf16[512,2048]{1,0:T(8,128)(2,1)S(1)}, bf16[512,2048]{1,0:T(8,128)(2,1)}, u32[]{:S(2)}) copy-start(bf16[512,2048]{1,0:T(8,128)(2,1)} %get-tuple-element.32) | copy-start | bytes 6291460
  313.9 2.9 copy-start
  316.8 2.5 copy-start.2

commit v3 on v2

--- a/solution.py
+++ b/solution.py
@@ -9,7 +9,7 @@
 
 MESH = pl.DeviceIdType.MESH
 F32, BF16 = jnp.float32, jnp.bfloat16
-LANES, RUNS, GROUP, HALF = 128, 8, 4, 2
+LANES, RUNS, GROUP = 128, 8, 2
 EPS = 1e-05
 
 
@@ -34,9 +34,9 @@
     row = lax.broadcasted_iota(jnp.int32, (tokens, tokens), 0)
     col = lax.broadcasted_iota(jnp.int32, (tokens, tokens), 1)
     if back:
-        hit = col == lax.rem(row, steps) * RUNS + row // steps
+        hit = row == (col & (RUNS - 1)) * steps + (col >> 3)
     else:
-        hit = col == lax.rem(row, RUNS) * steps + row // RUNS
+        hit = col == (row & (RUNS - 1)) * steps + (row >> 3)
     return jnp.where(hit, 1.0, 0.0).astype(BF16)
 
 
@@ -152,6 +152,10 @@
     return (output.astype(jnp.bfloat16), input_grad, weight_grad, vector_grad)
 
 
+SLOTS = 8
+TOTALS, FORE, GRADS, BACK = 3, 5, 6, 8
+
+
 def front_kernel(
     nx, ny, units,
     tok, cot, keep, wsrc, vsrc,
@@ -170,6 +174,7 @@
     diag = xn + yn - gx
     first = gx * block
     mine = first + gy * rows
+    me = gx * ny + gy
 
     def peer_y(j):
         return lax.rem(gy + j, ny)
@@ -186,21 +191,24 @@
     def band(b, n=block):
         return pl.ds(pl.multiple_of(b, 16), n)
 
+    chunks = width // glanes
+
     def stage_copy(i):
-        src = tok if i < 4 else cot
-        c = i % 4
+        src = tok if i < chunks else cot
+        c = i % chunks
         return pltpu.make_async_copy(src.at[:, pl.ds(c * glanes, glanes)], stage.at[i % 2], sts.at[i % 2])
 
     stage_copy(0).start()
     stage_copy(1).start()
 
     def vz(j):
-        return remote(vsrc, vbuf.at[band(mine, rows)], vzs.at[j - 1], vzr.at[j - 1], (gx, peer_y(j)))
+        return remote(vsrc, vbuf.at[me], vzs.at[j - 1], vzr.at[j - 1], (gx, peer_y(j)))
 
     def vx(j):
-        return remote(vbuf.at[band(first)], vbuf.at[band(first)], vxs.at[j - 1], vxr.at[j - 1], (peer_x(j), gy))
-
-    own_vec = pltpu.make_async_copy(vsrc, vbuf.at[band(mine, rows)], vo)
+        part = vbuf.at[pl.ds(gx * ny, ny)]
+        return remote(part, part, vxs.at[j - 1], vxr.at[j - 1], (peer_x(j), gy))
+
+    own_vec = pltpu.make_async_copy(vsrc, vbuf.at[me], vo)
 
     def z_copy(u, j):
         return remote(wsrc.at[u], wv.at[u, band(mine, rows)], zs.at[u, j - 1], zr.at[u, j - 1], (gx, peer_y(j)))
@@ -268,14 +276,14 @@
 
     def to_runs(i, into):
         stage_copy(i).wait()
-        c = i % 4
+        c = i % chunks
         into[:, c * glanes:(c + 1) * glanes] = jnp.dot(
             perm[...], stage[i % 2], preferred_element_type=F32
         ).astype(BF16)
-        if i + 2 < 8:
+        if i + 2 < 2 * chunks:
             stage_copy(i + 2).start()
 
-    for i in range(4):
+    for i in range(chunks):
         to_runs(i, xs)
     z_wait(0)
     own_vec.wait()
@@ -301,15 +309,15 @@
     nrm_copy.start()
     for u in range(2, AHEAD_B):
         z_wait(u)
-    for i in range(4, 8):
+    for i in range(chunks, 2 * chunks):
         to_runs(i, gs)
     perm[...] = run_matrix(tokens, True)
     for j in range(1, nx):
         vx(j).wait_recv()
 
     for c in range(width // LANES):
-        part = vbuf[c * LANES:(c + 1) * LANES, :].astype(F32)
-        vecs[:, c * LANES:(c + 1) * LANES] = part.T[0:8, :]
+        part = vbuf[2 * c].astype(F32) + vbuf[2 * c + 1].astype(F32)
+        vecs[:, c * LANES:(c + 1) * LANES] = part[0:8, :]
 
     def rounding(i, _):
         r = pl.ds(pl.multiple_of(i * BAND, BAND), BAND)
@@ -355,14 +363,14 @@
     double = tokens // (2 * RUNS)
 
     def project(u):
-        slot = lax.rem(u, 2 * GROUP)
+        slot = lax.rem(u, SLOTS)
         pj[slot] = jnp.dot(rnd[...], wv[u], preferred_element_type=F32)
 
     def vec(i, u):
         return vecs[i:i + 1, lanes_of(u)]
 
     def gates(u):
-        slot = lax.rem(u, 2 * GROUP)
+        slot = lax.rem(u, SLOTS)
         gain, shift, vf, bf = (vec(i, u) for i in range(4))
 
         def step(i, carry):
@@ -379,17 +387,16 @@
             return a, b
 
         a, b = lax.fori_loop(0, double, step, (jnp.ones((RUNS, LANES), F32), jnp.zeros((RUNS, LANES), F32)), unroll=4)
-        g, j = lax.rem(u // GROUP, 2), lax.rem(u, GROUP)
-        ach[g, :, lanes_of(j)] = a
-        bch[g, :, lanes_of(j)] = b
+        q, j = u // GROUP, lax.rem(u, GROUP)
+        ach[q, :, lanes_of(j)] = a
+        bch[q, :, lanes_of(j)] = b
 
     def totals(q):
-        g = lax.rem(q, 2)
         a, b = jnp.ones((1, glanes), F32), jnp.zeros((1, glanes), F32)
         for s in range(RUNS):
-            one = ach[g, s:s + 1, :]
+            one = ach[q, s:s + 1, :]
             a = a * one
-            b = one * b + bch[g, s:s + 1, :]
+            b = one * b + bch[q, s:s + 1, :]
         m1a[q, gy, 0:1, :] = a
         m1a[q, gy, 1:2, :] = b
         e_start(m1a, e1as, e1ar, q, 0)
@@ -412,17 +419,18 @@
         s = lax.fori_loop(0, gx, lambda i, s: m1b[q, i, 0:1, :] * s + m1b[q, i, 1:2, :], s)
         s = lax.fori_loop(0, gy, lambda i, s: m1a[q, i, 0:1, :] * s + m1a[q, i, 1:2, :], s)
         for r in range(RUNS):
-            sin[g, r:r + 1, :] = s
-            s = ach[g, r:r + 1, :] * s + bch[g, r:r + 1, :]
+            sin[q, r:r + 1, :] = s
+            s = ach[q, r:r + 1, :] * s + bch[q, r:r + 1, :]
 
     def forward(u):
-        slot = lax.rem(u, 2 * GROUP)
-        g, j = lax.rem(u // GROUP, 2), lax.rem(u, GROUP)
+        slot = lax.rem(u, SLOTS)
+        q, j = u // GROUP, lax.rem(u, GROUP)
+        g = lax.rem(q, 2)
         vr, br_ = vec(4, u), vec(5, u)
         zero = jnp.zeros((RUNS, LANES), F32)
 
         def step(i, carry):
-            s, run, q, v4, v5 = carry
+            s, run, t, v4, v5 = carry
             r = pl.ds(pl.multiple_of(i * 16, 16), 16)
             f = pj[slot, r, LANES:2 * LANES]
             k = keep[r, :]
@@ -447,16 +455,16 @@
             local = up * reset
             d, through = f * k, k * vr * rg
             for h in (0, 8):
-                q = q + run * through[h:h + 8]
+                t = t + run * through[h:h + 8]
                 run = run * d[h:h + 8]
-                q = q + run * local[h:h + 8]
+                t = t + run * local[h:h + 8]
                 v4 = v4 + rg[h:h + 8] * prev[h:h + 8]
                 v5 = v5 + rg[h:h + 8]
-            return s, run, q, v4, v5
-
-        init = (sin[g, :, lanes_of(j)], jnp.ones((RUNS, LANES), F32), zero, zero, zero)
-        _, _, q, v4, v5 = lax.fori_loop(0, double, step, init, unroll=4)
-        qch[g, :, lanes_of(j)] = q
+            return s, run, t, v4, v5
+
+        init = (sin[q, :, lanes_of(j)], jnp.ones((RUNS, LANES), F32), zero, zero, zero)
+        _, _, t, v4, v5 = lax.fori_loop(0, double, step, init, unroll=4)
+        qch[q, :, lanes_of(j)] = t
         vsum[4:5, lanes_of(u)] = jnp.sum(v4, axis=0, keepdims=True)
         vsum[5:6, lanes_of(u)] = jnp.sum(v5, axis=0, keepdims=True)
 
@@ -475,7 +483,7 @@
         g = lax.rem(q, 2)
         s = jnp.zeros((1, glanes), F32)
         for r in reversed(range(RUNS)):
-            s = ach[g, r:r + 1, :] * s + qch[g, r:r + 1, :]
+            s = ach[q, r:r + 1, :] * s + qch[q, r:r + 1, :]
         m2a[q, gy, 0:1, :] = s
         e_start(m2a, e2as, e2ar, q, 0)
         rest_copy(q).start()
@@ -504,8 +512,8 @@
         s = lax.fori_loop(0, nx - 1 - gx, over_x, s)
         s = lax.fori_loop(0, ny - 1 - gy, over_y, s)
         for r in reversed(range(RUNS)):
-            cin[g, r:r + 1, :] = s
-            s = ach[g, r:r + 1, :] * s + qch[g, r:r + 1, :]
+            cin[q, r:r + 1, :] = s
+            s = ach[q, r:r + 1, :] * s + qch[q, r:r + 1, :]
 
     def pg_own(u):
         return pltpu.make_async_copy(pgs.at[u], pg.at[u, 0:tokens], po.at[u])
@@ -514,8 +522,9 @@
         return remote(pgs.at[u], pg.at[u, tokens:2 * tokens], ps.at[u], pr.at[u], (mate, gy))
 
     def backward(u):
-        slot = lax.rem(u, 2 * GROUP)
-        g, j = lax.rem(u // GROUP, 2), lax.rem(u, GROUP)
+        slot = lax.rem(u, SLOTS)
+        q, j = u // GROUP, lax.rem(u, GROUP)
+        g = lax.rem(q, 2)
         gain, shift, vr = vec(0, u), vec(1, u), vec(4, u)
         zero = jnp.zeros((RUNS, LANES), F32)
 
@@ -542,7 +551,7 @@
             fs = fg * scaled
             return c, v2 + fs[0:8] + fs[8:16], v3 + fg[0:8] + fg[8:16]
 
-        _, v2, v3 = lax.fori_loop(0, double, step, (cin[g, :, lanes_of(j)], zero, zero), unroll=4)
+        _, v2, v3 = lax.fori_loop(0, double, step, (cin[q, :, lanes_of(j)], zero, zero), unroll=4)
         vsum[2:3, lanes_of(u)] = jnp.sum(v2, axis=0, keepdims=True)
         vsum[3:4, lanes_of(u)] = jnp.sum(v3, axis=0, keepdims=True)
         pg_own(u).start()
@@ -561,11 +570,15 @@
         pl.when(k + AHEAD_B < units)(lambda: z_wait(k + AHEAD_B))
         pl.when(k < units)(lambda: xy_wait(k))
         pl.when((k >= 1) & (k <= units))(lambda: diag_wait(k - 1))
-        late = (u >= GROUP)
-        pl.when(late & (m == 0))(lambda: totals_x(q - 1))
-        pl.when(late & (m == 1))(lambda: forward_group(q - 1))
-        pl.when(late & (m == 2))(lambda: grads_x(q - 1))
-        pl.when(late & (m == 3))(lambda: backward_group(q - 1))
+
+        def event(lag, run):
+            g = (u - lag) // GROUP
+            pl.when((u >= lag) & (lax.rem(u - lag + GROUP, GROUP) == 0) & (g < groups))(lambda: run(g))
+
+        event(BACK, backward_group)
+        event(GRADS, grads_x)
+        event(FORE, forward_group)
+        event(TOTALS, totals_x)
 
         @pl.when((u >= 0) & (u < units))
         def _():
@@ -577,7 +590,7 @@
 
         return 0
 
-    lax.fori_loop(0, units + 2 + GROUP, tick, 0)
+    lax.fori_loop(0, units + BACK - GROUP + 1 + 2, tick, 0)
 
     def drain(u, _):
         for j in range(1, ny):
@@ -625,6 +638,7 @@
     s = jax.ShapeDtypeStruct
     return pl.pallas_call(
         functools.partial(front_kernel, nx, ny, units),
+        name="front",
         out_shape=(
             s((units, width, cols), BF16), s((units, 2 * tokens, cols), BF16), s((2 * tokens, width // 2), BF16),
             s((tokens, width), BF16), s((tokens, width), F32), s((tokens, width), F32), s((tokens, LANES), F32),
@@ -634,20 +648,19 @@
         out_specs=(any_,) * 6 + (vmem,) * 3,
         scratch_shapes=[
             pltpu.VMEM((units, width, cols), BF16),
-            pltpu.VMEM((width, LANES), BF16),
+            pltpu.VMEM((nx * ny, 16, LANES), BF16),
             pltpu.VMEM((tokens, width), BF16),
             pltpu.VMEM((tokens, width), BF16),
             pltpu.VMEM((tokens, width), F32),
             pltpu.VMEM((tokens, width), BF16),
-            pltpu.VMEM((2 * GROUP, tokens, cols), F32),
-            pltpu.VMEM((2 * GROUP, tokens, LANES), F32),
+            pltpu.VMEM((SLOTS, tokens, cols), F32),
+            pltpu.VMEM((SLOTS, tokens, LANES), F32),
             pltpu.VMEM((2, tokens, glanes), F32),
             pltpu.VMEM((tokens, glanes), BF16),
             pltpu.VMEM((units, tokens, cols), BF16),
             pltpu.VMEM((tokens, tokens), BF16),
             pltpu.VMEM((2, tokens, glanes), BF16),
-            pltpu.VMEM((2,) + msg, F32), pltpu.VMEM((2,) + msg, F32), pltpu.VMEM((2,) + msg, F32),
-            pltpu.VMEM((2,) + msg, F32), pltpu.VMEM((2,) + msg, F32),
+            *[pltpu.VMEM((groups,) + msg, F32)] * 5,
             pltpu.VMEM((groups, ny) + msg, F32), pltpu.VMEM((groups, nx) + msg, F32),
             pltpu.VMEM((groups, ny) + msg, F32), pltpu.VMEM((groups, nx) + msg, F32),
             dma((units, ny - 1)), dma((units, ny - 1)), dma((units,)), dma((units, 3)), dma((units, 2)),
@@ -892,6 +905,7 @@
     s = jax.ShapeDtypeStruct
     return pl.pallas_call(
         functools.partial(back_kernel, nx, ny, units),
+        name="back",
         out_shape=(s((tokens, width), F32), s((rows, 3 * width), F32), s((8, LANES), F32)),
         in_specs=[any_, any_, any_, any_, vmem, any_, vmem, vmem],
         out_specs=(any_, vmem, vmem),
@@ -933,10 +947,11 @@
     keep = (1 - reset_mask).astype(F32).reshape(RUNS, steps).T.reshape(count, 1)
     keep = jnp.broadcast_to(keep, (count, LANES))
     wsrc = weight.reshape(rows, 3, units, LANES).transpose(2, 0, 1, 3).reshape(units, rows, 3 * LANES)
-    vsrc = jnp.pad(vectors.T, ((0, 0), (0, LANES - 6)))
+    odd = lax.rem(lax.axis_index("gx") * ny + lax.axis_index("gy"), 2) == 1
+    low, high = (jnp.pad(vectors, ((0, 10), side)) for side in ((0, rows), (rows, 0)))
+    vsrc = jnp.where(odd, high, low)
     wall, pg, rcat, outp, grest, nrm, inv, vecs, vsum = front(nx, ny, tokens, cotangent, keep, wsrc, vsrc)
     grad, weight_grad, tile = back(nx, ny, pg, rcat, wall, nrm, inv, grest, vecs, vsum)
-    odd = lax.rem(lax.axis_index("gx") * ny + lax.axis_index("gy"), 2) == 1
     vector_grad = jnp.where(odd, tile[:6, rows:2 * rows], tile[:6, :rows])
     return outp, grad, weight_grad, vector_grad
 

time: 321 us -> 307 us (0.956)
  Pallas kernels: 306 us -> 291 us
    pallas_call x2, Pallas kernels: 306 us -> 291 us  [the longest x1 164 us: front(): pl.pallas_call(functools.partial(front_kernel, nx, ny, units), name='fron...]
    unnamed x13 -> x10, local copies, waits for them, and re-layouts: 8.01 us -> 7.89 us
where the time goes in v3:
time: 307 us; the launch traced here: 306 us
  Pallas kernels  291 us (95%)
  local copies, waits for them, and re-layouts  10.9 us (4%)
  other arithmetic  3.53 us (1%)
    pallas_call x1, Pallas kernels, front(): pl.pallas_call(functools.partial(front_kernel, nx, ny, units), name='fron...  164 us
    pallas_call x1, Pallas kernels, back(): pl.pallas_call(functools.partial(back_kernel, nx, ny, units), name='back'...  127 us
    unnamed x10, local copies, waits for them, and re-layouts  7.89 us

profile of v3, /device:TPU:0, one launch (start us, length us, event | category | flops | bytes accessed | tf_op | source)
XLA Modules:
  0.0 306.3 jit_solution(18020071760314154643)
XLA Ops:
  0.6 0.7 subtract_convert_fusion
  1.3 0.1 reshape.19
  1.4 1.4 pad_select_fusion.vsrc
  2.8 0.1 copy.11
  2.9 0.1 broadcast_in_dim.7
  3.0 0.8 broadcast_in_dim.8.keep
  3.8 1.3 copy.13
  5.1 0.5 copy.15
  5.6 1.4 reshape.21.wsrc
  7.1 164.3 %front.1 = (bf16[16,2048,384]{2,1,0:T(8,128)(2,1)}, bf16[16,1024,384]{2,1,0:T(8,128)(2,1)}, bf16[1024,1024]{1,0:T(8,128)(2,1)}, bf16[512,2048]{1,0:T(8,128)(2,1)...) custom-call(bf16[512,2048]{1,0:T(8,128)(2,1)} %tok.1, ...), custom_call_target="tpu_custom_call" | custom-call | flops 12884901888 | bytes 25165824 | tf_op jit(solution)/shard_map/front/pallas_call | solution.py:639
  171.3 0.0 copy-start.1
  171.3 126.9 %back.1 = (f32[512,2048]{1,0:T(8,128)}, f32[64,6144]{1,0:T(8,128)}, f32[8,128]{1,0:T(8,128)}) custom-call(bf16[16,1024,384]{2,1,0:T(8,128)(2,1)} %get-tuple-element.17.pg, bf16[1024,1024]{1,0:T(8,128)(2,1)} %get-tuple-element.18.rcat, bf16[16,2048,384]{2,1,0:T(8,128)(2,1)} %get-tuple-element.19.wall, f32[512,2048]{1,0:T(8,128)} %get-tuple-element.20.nrmi, ...), custom_call_target="tpu_custom_call" | custom-call | flops 25769803776 | bytes 25165824 | tf_op jit(solution)/shard_map/back/pallas_call | solution.py:906
  298.2 1.4 slice_select_fusion
  299.7 0.0 copy-done.1
  299.7 0.0 copy-start
  299.7 1.3 copy.19
  301.0 1.6 copy-done
  302.6 0.0 copy-start.2
  302.6 2.0 copy.20
  304.6 0.5 copy-done.2
  305.1 1.1 copy.21
Async XLA Ops:
  171.3 128.3 %copy-start.1 = (bf16[512,2048]{1,0:T(8,128)(2,1)S(1)}, bf16[512,2048]{1,0:T(8,128)(2,1)}, u32[]{:S(2)}) copy-start(bf16[512,2048]{1,0:T(8,128)(2,1)} %get-tuple-element.32) | copy-start | bytes 6291460
  299.7 2.9 copy-start
  302.6 2.5 copy-start.2

commit v4 on v1

v4 whole, which is shorter than its diff:
```python
import functools

import jax
import jax.numpy as jnp
from jax import lax
from jax.experimental import pallas as pl
from jax.experimental.pallas import tpu as pltpu
from jax.sharding import PartitionSpec as P

MESH = pl.DeviceIdType.MESH
F32, BF16 = jnp.float32, jnp.bfloat16
LANES, RUNS, GROUP = 128, 8, 2
EPS = 1e-05


def place(ny):
    gx, gy = lax.axis_index("gx"), lax.axis_index("gy")
    core, xx, yy = lax.rem(gx, 2), lax.rem(gx // 2, 2), gx // 4
    return gx, gy, core, gx + 1 - 2 * core, gx + 2 - 4 * xx, gx + 4 - 8 * yy


def remote(src, dst, send, recv, to):
    return pltpu.make_async_remote_copy(
        src_ref=src, dst_ref=dst, send_sem=send, recv_sem=recv, device_id=to, device_id_type=MESH
    )


def lanes_of(b):
    return pl.ds(pl.multiple_of(b * LANES, LANES), LANES)


def run_matrix(tokens, back):
    steps = tokens // RUNS
    row = lax.broadcasted_iota(jnp.int32, (tokens, tokens), 0)
    col = lax.broadcasted_iota(jnp.int32, (tokens, tokens), 1)
    if back:
        hit = row == (col & (RUNS - 1)) * steps + (col >> 3)
    else:
        hit = col == (row & (RUNS - 1)) * steps + (row >> 3)
    return jnp.where(hit, 1.0, 0.0).astype(BF16)


def entering(value, axis, join, neutral, backward):
    count, mine = (lax.axis_size(axis), lax.axis_index(axis))
    pieces = jax.tree.map(lambda part: lax.all_gather(part, axis), value)
    if backward:
        pieces = jax.tree.map(lambda part: part[::-1], pieces)
        mine = count - 1 - mine
    subtotal = jax.tree.map(
        lambda part, zero: jnp.full_like(part, 0) + jnp.asarray(zero, part.dtype), value, neutral
    )

    def lap(position, subtotal):
        longer = join(subtotal, jax.tree.map(lambda part: part[position], pieces))
        return jax.tree.map(lambda new, old: jnp.where(position < mine, new, old), longer, subtotal)

    return lax.fori_loop(0, count - 1, lap, subtotal)


def from_behind(block, axis, distance):
    devices = range(lax.axis_size(axis))
    route = [(i - distance, i) for i in devices if i - distance in devices]
    return lax.ppermute(block, axis, route)


def compose(earlier, later):
    return (earlier[0] * later[0], later[0] * earlier[1] + later[1])


def local(tokens, reset_mask, weight, vectors, cotangent):
    width = weight.shape[1] // 3
    whole_weight, whole_vectors = (
        lax.all_gather(weight, ("gx", "gy"), axis=0, tiled=True),
        lax.all_gather(vectors, ("gx", "gy"), axis=1, tiled=True),
    )
    params = whole_vectors.astype(jnp.float32)
    gain = params[0]
    shift_bias = params[1]
    forget_peep = params[2]
    forget_bias = params[3]
    reset_peep = params[4]
    reset_bias = params[5]
    inputs = tokens.astype(jnp.float32)
    keep = (1 - reset_mask).astype(jnp.float32)[:, None]
    centred = inputs - jnp.mean(inputs, axis=1, keepdims=True)
    inv_std = lax.rsqrt(jnp.mean(centred * centred, axis=1, keepdims=True) + 1e-05)
    normed = centred * inv_std
    scaled = normed * gain + shift_bias
    rounded = scaled.astype(jnp.bfloat16)
    projected = jnp.dot(rounded, whole_weight, preferred_element_type=jnp.float32)
    candidate = projected[:, :width]
    forget_pre = projected[:, width : 2 * width]
    reset_pre = projected[:, 2 * width :]
    forget = jax.nn.sigmoid(forget_pre + forget_peep * scaled + forget_bias)
    decay = forget * keep
    inflow = (1.0 - forget) * candidate
    cum_decay, cum_state = lax.associative_scan(compose, (decay, inflow), axis=0)
    unit = (jnp.ones_like(cum_decay[-1]), jnp.zeros_like(cum_state[-1]))
    before = entering((cum_decay[-1], cum_state[-1]), ("gx", "gy"), compose, unit, False)
    state_in = before[1]
    state = cum_decay * state_in + cum_state
    previous = keep * jnp.concatenate([state_in[None], state[:-1]], 0)
    reset = jax.nn.sigmoid(reset_pre + reset_peep * previous + reset_bias)
    output = reset * state + (1.0 - reset) * inputs
    upstream = cotangent.astype(jnp.float32)
    reset_grad = upstream * (state - inputs) * reset * (1.0 - reset)
    through = keep * reset_peep * reset_grad
    next_decay, next_through = from_behind((decay[0], through[0]), ("gx", "gy"), -1)
    ahead = jnp.concatenate([decay[1:], next_decay[None]], 0)
    local_term = upstream * reset + jnp.concatenate([through[1:], next_through[None]], 0)
    flip_mult, flip_sum = lax.associative_scan(compose, (ahead[::-1], local_term[::-1]), axis=0)
    mult_back = flip_mult[::-1]
    sum_back = flip_sum[::-1]
    after = entering((mult_back[0], sum_back[0]), ("gx", "gy"), compose, unit, True)
    state_grad = mult_back * after[1] + sum_back
    candidate_grad = state_grad * (1.0 - forget)
    forget_grad = state_grad * (previous - candidate) * forget * (1.0 - forget)
    proj_grad = jnp.concatenate([candidate_grad, forget_grad, reset_grad], 1).astype(jnp.bfloat16)
    weight_grad = lax.psum_scatter(
        lax.dot_general(
            rounded, proj_grad, (((0,), (0,)), ((), ())), preferred_element_type=jnp.float32
        ),
        ("gx", "gy"),
        scatter_dimension=0,
        tiled=True,
    )
    scaled_grad = lax.dot_general(
        proj_grad,
        lax.all_gather(weight, ("gx", "gy"), axis=0, tiled=True),
        (((1,), (1,)), ((), ())),
        preferred_element_type=jnp.float32,
    )
    scaled_grad = scaled_grad + forget_grad * forget_peep
    vector_terms = jnp.stack(
        [
            jnp.sum(scaled_grad * normed, axis=0),
            jnp.sum(scaled_grad, axis=0),
            jnp.sum(forget_grad * scaled, axis=0),
            jnp.sum(forget_grad, axis=0),
            jnp.sum(reset_grad * previous, axis=0),
            jnp.sum(reset_grad, axis=0),
        ],
        0,
    )
    vector_grad = lax.psum_scatter(vector_terms, ("gx", "gy"), scatter_dimension=1, tiled=True)
    normed_grad = scaled_grad * gain
    input_grad = upstream * (1.0 - reset) + inv_std * (
        normed_grad
        - jnp.mean(normed_grad, axis=1, keepdims=True)
        - normed * jnp.mean(normed_grad * normed, axis=1, keepdims=True)
    )
    return (output.astype(jnp.bfloat16), input_grad, weight_grad, vector_grad)


SLOTS, SEND, PAIR, ZSEND = 8, 8, 4, 4
TOTALS, FORE, GRADS, BACK, WEIGH = 3, 5, 6, 8, 10
LAG1, LAG2, LAG3 = 2, 4, 6
AHEAD_Z, AHEAD_B = 5, 3
BAND = 32


def layer_kernel(
    nx, ny, units,
    tok, cot, keep, wsrc, vsrc,
    wall, pgm, outp, igo, wgo, vgo,
    vbuf, vecs, xs, gs, means, invs, rnd, rt, rtm, wf, pj, pv, grs, outs, stage, perm, pgs,
    wb, sb, rd, rx, ry, rz, zb, sg, vsum, vrows, vtot, vin,
    ach, bch, qch, sin, cin, m1a, m1b, m2a, m2b,
    zs, zr, os, bs, br, dsn, dr, cs, cr, ws,
    vzs, vzr, vxs, vxr, vo, sts, rs, rr, ps, pr, pl_, wl, gos,
    e1as, e1ar, e1bs, e1br, e2as, e2ar, e2bs, e2br,
    fds, fdr, fxs, fxr, fys, fyr, fzs, fzr, vsn, vrc, ous,
):
    gx, gy, core, mate, xn, yn = place(ny)
    tokens, width = xs.shape
    rows = wsrc.shape[1]
    block = rows * ny
    half = block // 2
    groups = units // GROUP
    glanes = GROUP * LANES
    diag = xn + yn - gx
    first = gx * block
    mine = first + gy * rows
    count = nx * ny
    me = gx * ny + gy

    def peer_y(j):
        return lax.rem(gy + j, ny)

    def peer_x(j):
        return lax.rem(gx + j, nx)

    def each(n, run, start=0):
        lax.fori_loop(start, n, lambda i, _: (run(i), 0)[1], 0)

    barrier = pltpu.get_barrier_semaphore()

    def greet(j):
        to = lax.rem(me + j, count)
        pl.semaphore_signal(barrier, inc=1, device_id=(to // ny, lax.rem(to, ny)), device_id_type=MESH)

    each(count, greet, 1)

    def band(b, n=block):
        return pl.ds(pl.multiple_of(b, 16), n)

    chunks = width // glanes

    def stage_copy(i):
        src = tok if i < chunks else cot
        c = i % chunks
        return pltpu.make_async_copy(src.at[:, pl.ds(c * glanes, glanes)], stage.at[i % 2], sts.at[i % 2])

    stage_copy(0).start()
    stage_copy(1).start()

    def vz(j):
        return remote(vsrc, vbuf.at[me], vzs.at[j - 1], vzr.at[j - 1], (gx, peer_y(j)))

    def vx(j):
        part = vbuf.at[pl.ds(gx * ny, ny)]
        return remote(part, part, vxs.at[j - 1], vxr.at[j - 1], (peer_x(j), gy))

    own_vec = pltpu.make_async_copy(vsrc, vbuf.at[me], vo)

    def z_copy(u, j):
        return remote(wsrc.at[u], wall.at[u, band(mine, rows)], zs.at[u, j - 1], zr.at[u, j - 1], (gx, peer_y(j)))

    def own_copy(u):
        return pltpu.make_async_copy(wsrc.at[u], wall.at[u, band(mine, rows)], os.at[u])

    def band_copy(u, i):
        to = (mate, xn, yn)[i]
        recv = cr.at[u, 0] if i == 0 else br.at[u, i - 1]
        part = wall.at[u, band(first)]
        return remote(part, part, bs.at[u, i], recv, (to, gy))

    def diag_copy(u, i):
        part = wall.at[u, band((xn * block, yn * block + half)[i], half)]
        return remote(part, part, dsn.at[u, i], dr.at[u, i], ((yn, xn)[i], gy))

    def core_copy(u, i):
        part = wall.at[u, band((None, xn, yn, diag)[i] * block)]
        return remote(part, part, cs.at[u, i - 1], cr.at[u, i], (mate, gy))

    def z_start(u):
        own_copy(u).start()
        for j in range(1, ny):
            z_copy(u, j).start()

    def z_wait(u):
        own_copy(u).wait()
        for j in range(1, ny):
            z_copy(u, j).wait_recv()
        for i in (1, 2, 0):
            band_copy(u, i).start()

    def xy_wait(u):
        for i in (1, 2):
            band_copy(u, i).wait_recv()
        for i in (0, 1):
            diag_copy(u, i).start()
        for i in (1, 2):
            core_copy(u, i).start()

    def diag_wait(u):
        for i in (0, 1):
            diag_copy(u, i).wait_recv()
        core_copy(u, 3).start()

    def core_wait(u):
        band_copy(u, 0).wait_recv()
        for i in (1, 2, 3):
            core_copy(u, i).wait_recv()

    pl.semaphore_wait(barrier, count - 1)
    own_vec.start()
    for j in range(1, ny):
        vz(j).start()
    for u in range(AHEAD_Z):
        z_start(u)

    perm[...] = run_matrix(tokens, False)

    def to_runs(i, into):
        stage_copy(i).wait()
        c = i % chunks
        into[:, c * glanes:(c + 1) * glanes] = jnp.dot(
            perm[...], stage[i % 2], preferred_element_type=F32
        ).astype(BF16)
        if i + 2 < 2 * chunks:
            stage_copy(i + 2).start()

    for i in range(chunks):
        to_runs(i, xs)
    z_wait(0)
    own_vec.wait()
    for j in range(1, ny):
        vz(j).wait_recv()
    for j in range(1, nx):
        vx(j).start()
    z_wait(1)

    def moments(i):
        r = pl.ds(pl.multiple_of(i * BAND, BAND), BAND)
        x = xs[r, :].astype(F32)
        mean = jnp.mean(x, axis=1, keepdims=True)
        centred = x - mean
        inv = lax.rsqrt(jnp.mean(centred * centred, axis=1, keepdims=True) + EPS)
        means[r, :] = jnp.broadcast_to(mean, (BAND, LANES))
        invs[r, :] = jnp.broadcast_to(inv, (BAND, LANES))

    each(tokens // BAND, moments)
    for u in range(2, AHEAD_B):
        z_wait(u)
    for j in range(1, nx):
        vx(j).wait_recv()
    for c in range(width // LANES):
        part = vbuf[2 * c].astype(F32) + vbuf[2 * c + 1].astype(F32)
        vecs[:, c * LANES:(c + 1) * LANES] = part[0:8, :]

    def rounding(i):
        r = pl.ds(pl.multiple_of(i * BAND, BAND), BAND)
        normed = (xs[r, :].astype(F32) - means[r, 0:1]) * invs[r, 0:1]
        rnd[r, :] = (normed * vecs[0:1, :] + vecs[1:2, :]).astype(BF16)

    each(tokens // BAND, rounding)

    quads = nx // 2

    def turn(i):
        at = pl.ds(pl.multiple_of(i * block, 16), block)
        rt[at, 0:tokens] = rnd[:, pl.ds(pl.multiple_of((2 * i + core) * block, LANES), block)].T
        rtm[at, :] = rnd[:, pl.ds(pl.multiple_of((2 * i + 1 - core) * block, LANES), block)].T

    r_mate = remote(rtm, rt.at[:, tokens:2 * tokens], rs, rr, (mate, gy))

    def late_start():
        each(quads, turn)
        r_mate.start()
        for i in range(chunks, 2 * chunks):
            to_runs(i, gs)
        perm[...] = run_matrix(tokens, True)

    def e_copies(buf, send, recv, q, level):
        if level == 0:
            return [
                remote(buf.at[q, gy], buf.at[q, gy], send.at[q, j - 1], recv.at[q, j - 1], (gx, peer_y(j)))
                for j in range(1, ny)
            ]
        return [
            remote(buf.at[q, gx], buf.at[q, gx], send.at[q, j - 1], recv.at[q, j - 1], (peer_x(j), gy))
            for j in range(1, nx)
        ]

    def e_start(*a):
        for c in e_copies(*a):
            c.start()

    def e_wait(*a):
        for c in e_copies(*a):
            c.wait_recv()

    double = tokens // (2 * RUNS)

    def front_load(u):
        return pltpu.make_async_copy(wall.at[u], wf, ws)

    def project(u):
        front_load(u).wait()
        pj[lax.rem(u, SLOTS)] = jnp.dot(rnd[...], wf[...], preferred_element_type=F32)

    def vec(i, u):
        return vecs[i:i + 1, lanes_of(u)]

    def scale(u, r, gain, shift):
        return (xs[r, lanes_of(u)].astype(F32) - means[r, :]) * invs[r, :] * gain + shift

    def gates(u):
        slot = lax.rem(u, SLOTS)
        gain, shift, vf, bf = (vec(i, u) for i in range(4))

        def step(i, carry):
            a, b = carry
            r = pl.ds(pl.multiple_of(i * 16, 16), 16)
            f = jax.nn.sigmoid(pj[slot, r, LANES:2 * LANES] + vf * scale(u, r, gain, shift) + bf)
            pj[slot, r, LANES:2 * LANES] = f
            d = f * keep[r, :]
            inflow = (1.0 - f) * pj[slot, r, 0:LANES]
            for h in (0, 8):
                a = a * d[h:h + 8]
                b = d[h:h + 8] * b + inflow[h:h + 8]
            return a, b

        a, b = lax.fori_loop(0, double, step, (jnp.ones((RUNS, LANES), F32), jnp.zeros((RUNS, LANES), F32)), unroll=4)
        q, j = u // GROUP, lax.rem(u, GROUP)
        ach[q, :, lanes_of(j)] = a
        bch[q, :, lanes_of(j)] = b

    def totals(q):
        a, b = jnp.ones((1, glanes), F32), jnp.zeros((1, glanes), F32)
        for s in range(RUNS):
            one = ach[q, s:s + 1, :]
            a = a * one
            b = one * b + bch[q, s:s + 1, :]
        m1a[q, gy, 0:1, :] = a
        m1a[q, gy, 1:2, :] = b
        e_start(m1a, e1as, e1ar, q, 0)

    def totals_x(q):
        e_wait(m1a, e1as, e1ar, q, 0)
        a, b = jnp.ones((1, glanes), F32), jnp.zeros((1, glanes), F32)
        for s in range(ny):
            one = m1a[q, s, 0:1, :]
            a = a * one
            b = one * b + m1a[q, s, 1:2, :]
        m1b[q, gx, 0:1, :] = a
        m1b[q, gx, 1:2, :] = b
        e_start(m1b, e1bs, e1br, q, 1)

    def enter(q):
        e_wait(m1b, e1bs, e1br, q, 1)
        s = jnp.zeros((1, glanes), F32)
        s = lax.fori_loop(0, gx, lambda i, s: m1b[q, i, 0:1, :] * s + m1b[q, i, 1:2, :], s)
        s = lax.fori_loop(0, gy, lambda i, s: m1a[q, i, 0:1, :] * s + m1a[q, i, 1:2, :], s)
        for r in range(RUNS):
            sin[q, r:r + 1, :] = s
            s = ach[q, r:r + 1, :] * s + bch[q, r:r + 1, :]

    def forward(u):
        slot = lax.rem(u, SLOTS)
        q, j = u // GROUP, lax.rem(u, GROUP)
        vr, br_ = vec(4, u), vec(5, u)
        zero = jnp.zeros((RUNS, LANES), F32)

        def step(i, carry):
            s, run, t, v4, v5 = carry
            r = pl.ds(pl.multiple_of(i * 16, 16), 16)
            f = pj[slot, r, LANES:2 * LANES]
            k = keep[r, :]
            inflow = (1.0 - f) * pj[slot, r, 0:LANES]
            prevs, states = [], []
            for h in (0, 8):
                prev = k[h:h + 8] * s
                s = f[h:h + 8] * prev + inflow[h:h + 8]
                prevs.append(prev)
                states.append(s)
            prev, state = jnp.concatenate(prevs, 0), jnp.concatenate(states, 0)
            x = xs[r, lanes_of(u)].astype(F32)
            up = gs[r, lanes_of(u)].astype(F32)
            reset = jax.nn.sigmoid(pj[slot, r, 2 * LANES:3 * LANES] + vr * prev + br_)
            rest = 1.0 - reset
            outs[r, lanes_of(j)] = (reset * state + rest * x).astype(BF16)
            rg = up * (state - x) * reset * rest
            pj[slot, r, 2 * LANES:3 * LANES] = rg
            pv[slot, r, :] = prev
            grs[r, lanes_of(u)] = up * rest
            local = up * reset
            d, through = f * k, k * vr * rg
            for h in (0, 8):
                t = t + run * through[h:h + 8]
                run = run * d[h:h + 8]
                t = t + run * local[h:h + 8]
                v4 = v4 + rg[h:h + 8] * prev[h:h + 8]
                v5 = v5 + rg[h:h + 8]
            return s, run, t, v4, v5

        init = (sin[q, :, lanes_of(j)], jnp.ones((RUNS, LANES), F32), zero, zero, zero)
        _, _, t, v4, v5 = lax.fori_loop(0, double, step, init, unroll=4)
        qch[q, :, lanes_of(j)] = t
        vsum[4:5, lanes_of(u)] = jnp.sum(v4, axis=0, keepdims=True)
        vsum[5:6, lanes_of(u)] = jnp.sum(v5, axis=0, keepdims=True)

    def out_copy(q):
        c = pl.ds(pl.multiple_of(q * glanes, LANES), glanes)
        return pltpu.make_async_copy(stage.at[lax.rem(q, 2)], outp.at[:, c], gos.at[q])

    def forward_group(q):
        enter(q)
        pl.when(q >= 2)(lambda: out_copy(q - 2).wait())
        each(GROUP, lambda j: forward(q * GROUP + j))
        s = jnp.zeros((1, glanes), F32)
        for r in reversed(range(RUNS)):
            s = ach[q, r:r + 1, :] * s + qch[q, r:r + 1, :]
        m2a[q, gy, 0:1, :] = s
        e_start(m2a, e2as, e2ar, q, 0)
        stage[lax.rem(q, 2)] = jnp.dot(perm[...], outs[...], preferred_element_type=F32).astype(BF16)
        out_copy(q).start()

    def grads_x(q):
        e_wait(m2a, e2as, e2ar, q, 0)
        s = jnp.zeros((1, glanes), F32)
        for r in reversed(range(ny)):
            s = m1a[q, r, 0:1, :] * s + m2a[q, r, 0:1, :]
        m2b[q, gx, 0:1, :] = s
        e_start(m2b, e2bs, e2br, q, 1)

    def enter_back(q):
        e_wait(m2b, e2bs, e2br, q, 1)
        s = jnp.zeros((1, glanes), F32)

        def over_x(i, s):
            return m1b[q, nx - 1 - i, 0:1, :] * s + m2b[q, nx - 1 - i, 0:1, :]

        def over_y(i, s):
            return m1a[q, ny - 1 - i, 0:1, :] * s + m2a[q, ny - 1 - i, 0:1, :]

        s = lax.fori_loop(0, nx - 1 - gx, over_x, s)
        s = lax.fori_loop(0, ny - 1 - gy, over_y, s)
        for r in reversed(range(RUNS)):
            cin[q, r:r + 1, :] = s
            s = ach[q, r:r + 1, :] * s + qch[q, r:r + 1, :]

    def pg_mate(u):
        return remote(pgs.at[lax.rem(u, PAIR), 0:tokens], pgm.at[u], ps.at[u], pr.at[u], (mate, gy))

    def backward(u):
        slot, pair = lax.rem(u, SLOTS), lax.rem(u, PAIR)
        q, j = u // GROUP, lax.rem(u, GROUP)
        gain, shift, vr = vec(0, u), vec(1, u), vec(4, u)
        zero = jnp.zeros((RUNS, LANES), F32)

        def step(i, carry):
            c, v2, v3 = carry
            r = pl.ds(pl.multiple_of((double - 1 - i) * 16, 16), 16)
            f = pj[slot, r, LANES:2 * LANES]
            k = keep[r, :]
            rg = pj[slot, r, 2 * LANES:3 * LANES]
            local = gs[r, lanes_of(u)].astype(F32) - grs[r, lanes_of(u)]
            d, through = f * k, k * vr * rg
            grads = [None, None]
            for h in (1, 0):
                part = slice(8 * h, 8 * h + 8)
                grads[h] = local[part] + c
                c = d[part] * grads[h] + through[part]
            grad = jnp.concatenate(grads, 0)
            cg = grad * (1.0 - f)
            fg = cg * (pv[slot, r, :] - pj[slot, r, 0:LANES]) * f
            pgs[pair, r, 0:LANES] = cg.astype(BF16)
            pgs[pair, r, LANES:2 * LANES] = fg.astype(BF16)
            pgs[pair, r, 2 * LANES:3 * LANES] = rg.astype(BF16)
            fs = fg * scale(u, r, gain, shift)
            return c, v2 + fs[0:8] + fs[8:16], v3 + fg[0:8] + fg[8:16]

        _, v2, v3 = lax.fori_loop(0, double, step, (cin[q, :, lanes_of(j)], zero, zero), unroll=4)
        vsum[2:3, lanes_of(u)] = jnp.sum(v2, axis=0, keepdims=True)
        vsum[3:4, lanes_of(u)] = jnp.sum(v3, axis=0, keepdims=True)
        pg_mate(u).start()

    def backward_group(q):
        enter_back(q)
        each(GROUP, lambda j: backward(q * GROUP + j))

    def pg_load(u):
        return pltpu.make_async_copy(pgm.at[u], pgs.at[lax.rem(u, PAIR), tokens:2 * tokens], pl_)

    def back_load(u):
        return pltpu.make_async_copy(wall.at[u], wb, wl)

    def rows_of(chip, part, n=half):
        return pl.ds(pl.multiple_of((chip // 2) * block + part * half, 16), n)

    def sent(u):
        return sb.at[lax.rem(u, SEND)]

    def d_copy(u, i):
        return remote(
            sent(u).at[rows_of(diag, i)], rd.at[u, i * half:(i + 1) * half], fds.at[u, i], fdr.at[u, i], ((yn, xn)[i], gy)
        )

    def x_copy(u, i):
        return remote(sent(u).at[rows_of(xn, i)], rx.at[u, i * half:(i + 1) * half], fxs.at[u, i], fxr.at[u, i], (xn, gy))

    def y_copy(u, i):
        return remote(sent(u).at[rows_of(yn, i)], ry.at[u, i * half:(i + 1) * half], fys.at[u, i], fyr.at[u, i], (yn, gy))

    def f_copy(u, j):
        to = lax.rem(gy + j, ny)
        src = zb.at[lax.rem(u, ZSEND), pl.ds(pl.multiple_of(to * rows, 16), rows)]
        return remote(src, rz.at[u, j - 1], fzs.at[u, j - 1], fzr.at[u, j - 1], (gx, to))

    def next_loads(u):
        pg_mate(u).wait_recv()
        pg_load(u).start()
        back_load(u).start()

    def weigh(u):
        slot, pair = lax.rem(u, SEND), lax.rem(u, PAIR)

        @pl.when(u >= SEND)
        def _():
            for i in (0, 1):
                d_copy(u - SEND, i).wait_send()
                x_copy(u - SEND, i).wait_send()
                y_copy(u - SEND, i).wait_send()

        pg_load(u).wait()
        sb[slot] = jnp.dot(rt[...], pgs[pair], preferred_element_type=F32).astype(BF16)
        for i in (0, 1):
            d_copy(u, i).start()
        x_copy(u, 1).start()
        y_copy(u, 0).start()

    def spread(u):
        pair = lax.rem(u, PAIR)
        back_load(u).wait()
        own = pgs[pair, 0:tokens, :]
        sg[...] += lax.dot_general(own, wb[...], (((1,), (1,)), ((), ())), preferred_element_type=F32)
        sg[:, lanes_of(u)] += pgs[pair, 0:tokens, LANES:2 * LANES].astype(F32) * vecs[2:3, lanes_of(u)]
        pg_mate(u).wait_send()

    def fold(slot, r, more):
        sb[slot, r, :] = (sb[slot, r, :].astype(F32) + more.astype(F32)).astype(BF16)

    def meet(u):
        slot = lax.rem(u, SEND)
        for i in (0, 1):
            d_copy(u, i).wait_recv()
        fold(slot, rows_of(xn, 0), rd[u, 0:half])
        x_copy(u, 0).start()
        fold(slot, rows_of(yn, 1), rd[u, half:block])
        y_copy(u, 1).start()

    def column(u):
        slot, zslot = lax.rem(u, SEND), lax.rem(u, ZSEND)

        @pl.when(u >= ZSEND)
        def _():
            for j in range(1, ny):
                f_copy(u - ZSEND, j).wait_send()

        for i in (0, 1):
            x_copy(u, i).wait_recv()
            y_copy(u, i).wait_recv()
        total = sb[slot, rows_of(gx, 0, block), :].astype(F32) + rx[u].astype(F32) + ry[u].astype(F32)
        zb[zslot] = total.astype(BF16)
        for j in range(1, ny):
            f_copy(u, j).start()

    def settle(u):
        slot = lax.rem(u, SEND)
        r = pl.ds(pl.multiple_of(gy * rows, 16), rows)
        at = pl.ds(pl.multiple_of((gx // 2) * block + gy * rows, 16), rows)
        total = sb[slot, at, :].astype(F32) + rx[u, r, :].astype(F32) + ry[u, r, :].astype(F32)
        for j in range(1, ny):
            f_copy(u, j).wait_recv()
        for j in range(1, ny):
            total = total + rz[u, j - 1].astype(F32)
        for i in range(3):
            wgo[:, lanes_of(u + i * units)] = total[:, i * LANES:(i + 1) * LANES]

    bands = tokens // BAND

    def finish(i):
        r = pl.ds(pl.multiple_of(i * BAND, BAND), BAND)
        s = sg[r, :]
        inv = invs[r, 0:1]
        z = (xs[r, :].astype(F32) - means[r, 0:1]) * inv
        sz = s * z
        gain = vecs[0:1, :]
        vrows[0:8, :] += jnp.sum(sz.reshape(BAND // 8, 8, width), axis=0)
        vrows[8:16, :] += jnp.sum(s.reshape(BAND // 8, 8, width), axis=0)
        n = s * gain
        m1 = jnp.mean(n, axis=1, keepdims=True)
        m2 = jnp.mean(sz * gain, axis=1, keepdims=True)
        sg[r, :] = grs[r, :] + inv * (n - m1 - z * m2)

    def v_copy(j):
        to = lax.rem(me + j, count)
        return remote(vtot.at[to // 2], vin.at[me], vsn.at[to], vrc.at[me], (to // ny, lax.rem(to, ny)))

    def v_recv(j):
        at = lax.rem(me + j, count)
        return remote(vtot.at[0], vin.at[at], vsn.at[at], vrc.at[at], (at // ny, lax.rem(at, ny)))

    def vectors_out():
        zero = jnp.zeros((2, LANES), F32)
        for c in range(width // LANES):
            at = slice(c * LANES, (c + 1) * LANES)
            top = [jnp.sum(vrows[8 * v:8 * v + 8, at], axis=0, keepdims=True) for v in (0, 1)]
            vtot[c] = jnp.concatenate(top + [vsum[2:6, at], zero], 0)
        each(count, lambda j: v_copy(j).start(), 1)

    quarter = width // 4

    def grad_copy(c):
        return pltpu.make_async_copy(grs.at[:, pl.ds(c * quarter, quarter)], igo.at[:, pl.ds(c * quarter, quarter)], ous.at[c])

    def natural():
        for c in range(4):
            at = slice(c * quarter, (c + 1) * quarter)
            v = sg[:, at]
            high = v.astype(BF16)
            low = (v - high.astype(F32)).astype(BF16)
            grs[:, at] = jnp.dot(perm[...], high, preferred_element_type=F32) + jnp.dot(
                perm[...], low, preferred_element_type=F32
            )
            grad_copy(c).start()

    def tick(k, _):
        u = k - 3
        v = u - WEIGH
        pl.when(k + AHEAD_Z < units)(lambda: z_start(k + AHEAD_Z))
        pl.when(k + AHEAD_B < units)(lambda: z_wait(k + AHEAD_B))
        pl.when(k < units)(lambda: xy_wait(k))
        pl.when((k >= 1) & (k <= units))(lambda: diag_wait(k - 1))
        pl.when(k == 0)(late_start)

        pl.when((v >= LAG1) & (v < units + LAG1))(lambda: meet(v - LAG1))
        pl.when((v >= LAG2) & (v < units + LAG2))(lambda: column(v - LAG2))
        pl.when(v >= LAG3)(lambda: settle(v - LAG3))

        @pl.when(v == 0)
        def _():
            r_mate.wait_recv()
            sg[...] = jnp.zeros_like(sg)
            vrows[...] = jnp.zeros_like(vrows)

        @pl.when((v >= 0) & (v < units))
        def _():
            weigh(v)
            spread(v)

        pl.when((v >= -1) & (v < units - 1))(lambda: next_loads(v + 1))

        def event(lag, run):
            g = (u - lag) // GROUP
            pl.when((u >= lag) & (lax.rem(u - lag + GROUP, GROUP) == 0) & (g < groups))(lambda: run(g))

        event(BACK, backward_group)
        event(GRADS, grads_x)
        event(FORE, forward_group)
        event(TOTALS, totals_x)

        @pl.when((u >= 0) & (u < units))
        def _():
            project(u)

        @pl.when((u >= -1) & (u < units - 1))
        def _():
            core_wait(u + 1)
            front_load(u + 1).start()

        @pl.when((u >= 0) & (u < units))
        def _():
            gates(u)
            pl.when(lax.rem(u, GROUP) == GROUP - 1)(lambda: totals(u // GROUP))

        pl.when(v == units)(lambda: each(bands // 2, finish))

        @pl.when(v == units + 1)
        def _():
            each(bands, finish, bands // 2)
            vectors_out()

        pl.when(v == units + 2)(natural)
        return 0

    lax.fori_loop(0, units + WEIGH + 3 + LAG3, tick, 0)

    each(count, lambda j: v_recv(j).wait_recv(), 1)
    vin[me] = vtot[me // 2]
    vgo[...] = lax.fori_loop(0, count, lambda j, s: s + vin[j], jnp.zeros((8, LANES), F32))

    def drain(u):
        for j in range(1, ny):
            z_copy(u, j).wait_send()
        for i in range(3):
            band_copy(u, i).wait_send()
        for i in (0, 1):
            diag_copy(u, i).wait_send()
        for i in (1, 2, 3):
            core_copy(u, i).wait_send()

    each(units, drain)

    def drain_send(u):
        for i in (0, 1):
            d_copy(u, i).wait_send()
            x_copy(u, i).wait_send()
            y_copy(u, i).wait_send()

    each(units, drain_send, units - SEND)

    def drain_z(u):
        for j in range(1, ny):
            f_copy(u, j).wait_send()

    each(units, drain_z, units - ZSEND)

    def drain_group(q):
        for a in ((m1a, e1as, e1ar, q, 0), (m1b, e1bs, e1br, q, 1), (m2a, e2as, e2ar, q, 0), (m2b, e2bs, e2br, q, 1)):
            for c in e_copies(*a):
                c.wait_send()

    each(groups, drain_group)
    for q in range(groups - 2, groups):
        out_copy(q).wait()
    for j in range(1, ny):
        vz(j).wait_send()
    for j in range(1, nx):
        vx(j).wait_send()
    r_mate.wait_send()
    each(count, lambda j: v_copy(j).wait_send(), 1)
    for c in range(4):
        grad_copy(c).wait()


def layer(nx, ny, tok, cot, keep, wsrc, vsrc):
    tokens, width = tok.shape
    units, rows, cols = wsrc.shape
    groups, glanes, block, count = units // GROUP, GROUP * LANES, rows * ny, nx * ny
    dma = pltpu.SemaphoreType.DMA
    any_, vmem = pl.BlockSpec(memory_space=pl.ANY), pl.BlockSpec(memory_space=pltpu.VMEM)
    msg = RUNS, glanes
    s, v = jax.ShapeDtypeStruct, pltpu.VMEM
    return pl.pallas_call(
        functools.partial(layer_kernel, nx, ny, units),
        name="layer",
        out_shape=(
            s((units, width, cols), BF16), s((units, tokens, cols), BF16),
            s((tokens, width), BF16), s((tokens, width), F32), s((rows, 3 * width), F32), s((8, LANES), F32),
        ),
        in_specs=[any_, any_, vmem, any_, any_],
        out_specs=(any_,) * 4 + (vmem,) * 2,
        scratch_shapes=[
            v((count, 16, LANES), BF16), v((8, width), F32),
            v((tokens, width), BF16), v((tokens, width), BF16), v((tokens, LANES), F32), v((tokens, LANES), F32),
            v((tokens, width), BF16), v((width // 2, 2 * tokens), BF16), v((width // 2, tokens), BF16),
            v((width, cols), BF16),
            v((SLOTS, tokens, cols), F32), v((SLOTS, tokens, LANES), F32),
            v((tokens, width), F32), v((tokens, glanes), BF16), v((2, tokens, glanes), BF16),
            v((tokens, tokens), BF16), v((PAIR, 2 * tokens, cols), BF16),
            v((width, cols), BF16), v((SEND, width // 2, cols), BF16),
            v((units, block, cols), BF16), v((units, block, cols), BF16), v((units, block, cols), BF16),
            v((units, ny - 1, rows, cols), BF16), v((ZSEND, block, cols), BF16),
            v((tokens, width), F32), v((8, width), F32), v((16, width), F32),
            v((width // LANES, 8, LANES), F32), v((count, 8, LANES), F32),
            *[v((groups,) + msg, F32)] * 5,
            v((groups, ny) + msg, F32), v((groups, nx) + msg, F32),
            v((groups, ny) + msg, F32), v((groups, nx) + msg, F32),
            dma((units, ny - 1)), dma((units, ny - 1)), dma((units,)), dma((units, 3)), dma((units, 2)),
            dma((units, 2)), dma((units, 2)), dma((units, 3)), dma((units, 4)), dma,
            dma((ny - 1,)), dma((ny - 1,)), dma((nx - 1,)), dma((nx - 1,)), dma, dma((2,)),
            dma, dma, dma((units,)), dma((units,)), dma, dma, dma((groups,)),
            dma((groups, ny - 1)), dma((groups, ny - 1)), dma((groups, nx - 1)), dma((groups, nx - 1)),
            dma((groups, ny - 1)), dma((groups, ny - 1)), dma((groups, nx - 1)), dma((groups, nx - 1)),
            *[dma((units, 2))] * 6, dma((units, ny - 1)), dma((units, ny - 1)),
            dma((count,)), dma((count,)), dma((4,)),
        ],
        compiler_params=pltpu.CompilerParams(
            collective_id=0, has_side_effects=True, vmem_limit_bytes=62 * 2**20
        ),
        cost_estimate=pl.CostEstimate(
            flops=6 * tokens * width * units * cols, bytes_accessed=4 * width * units * cols, transcendentals=0
        ),
    )(tok, cot, keep, wsrc, vsrc)


def fast(nx, ny, tokens, reset_mask, weight, vectors, cotangent):
    count, width = tokens.shape
    rows = weight.shape[0]
    units, steps = width // LANES, count // RUNS
    keep = (1 - reset_mask).astype(F32).reshape(RUNS, steps).T.reshape(count, 1)
    keep = jnp.broadcast_to(keep, (count, LANES))
    wsrc = weight.reshape(rows, 3, units, LANES).transpose(2, 0, 1, 3).reshape(units, rows, 3 * LANES)
    odd = lax.rem(lax.axis_index("gx") * ny + lax.axis_index("gy"), 2) == 1
    low, high = (jnp.pad(vectors, ((0, 10), side)) for side in ((0, rows), (rows, 0)))
    vsrc = jnp.where(odd, high, low)
    _, _, outp, grad, weight_grad, tile = layer(nx, ny, tokens, cotangent, keep, wsrc, vsrc)
    vector_grad = jnp.where(odd, tile[:6, rows:2 * rows], tile[:6, :rows])
    return outp, grad, weight_grad, vector_grad


def solution(mesh):
    placed = (
        P(("gx", "gy"), None),
        P(("gx", "gy")),
        P(("gx", "gy"), None),
        P(None, ("gx", "gy")),
        P(("gx", "gy"), None),
    )
    nx, ny = mesh.shape["gx"], mesh.shape["gy"]

    def body(tokens, reset_mask, weight, vectors, cotangent):
        whole_tiles = weight.shape[0] % 16 == 0 and tokens.shape[0] % 256 == 0
        if nx == 8 and whole_tiles and 2 * weight.shape[0] == LANES and tokens.shape[1] % 2048 == 0:
            return fast(nx, ny, tokens, reset_mask, weight, vectors, cotangent)
        return local(tokens, reset_mask, weight, vectors, cotangent)

    return jax.shard_map(
        body,
        mesh=mesh,
        in_specs=placed,
        out_specs=(
            P(("gx", "gy"), None),
            P(("gx", "gy"), None),
            P(("gx", "gy"), None),
            P(None, ("gx", "gy")),
        ),
        check_vma=False,
    )
```

time: 824 us -> 271 us (0.33)
  waiting for transfers between devices: 533 us -> 0 us
  Pallas kernels: 179 us -> 255 us
  matrix products: 45.3 us -> 0 us
  local copies, waits for them, and re-layouts: 45.5 us -> 11.3 us
  between operations: 14.1 us -> 0.67 us
    reduce_scatter x1 -> x0, waiting for transfers between devices: 435 us -> none  [fast(): lax.psum_scatter(lax.dot_general(rounded, own, (((0,), (0,)), ((), ())),...]
    unnamed x3 -> x0, waiting for transfers between devices: 97.7 us -> none
    pallas_call x1, Pallas kernels: 179 us -> 255 us  [layer(): pl.pallas_call(functools.partial(layer_kernel, nx, ny, units), name='laye...]
    dot_general x2 -> x0, matrix products: 45.3 us -> none  [the longest x1 24.7 us: fast(): lax.dot_general(rounded, own, (((0,), (0,)), ((), ())), preferred_element...]
    transpose x4 -> x0, local copies, waits for them, and re-layouts: 28.3 us -> none  [the longest x2 14.9 us: fast(): flat = pg[:, :count].transpose(1, 0, 2).reshape(count, 3 * width)]
  transfers between devices with their start and end apart: 2 -> 0, of which waited for: 2 -> 0; matrix products, arithmetic and copies ran while one was open for 4% -> 0% of each run, Pallas kernels for 0% -> 0%
where the time goes in v4:
time: 271 us
  Pallas kernels  255 us (94%)
  local copies, waits for them, and re-layouts  11.3 us (4%)
  other arithmetic  3.52 us (1%)
    pallas_call x1, Pallas kernels, layer(): pl.pallas_call(functools.partial(layer_kernel, nx, ny, units), name='laye...  255 us
    unnamed x8, local copies, waits for them, and re-layouts  8.25 us

profile of v4, /device:TPU:0, one launch (start us, length us, event | category | flops | bytes accessed | tf_op | source)
XLA Modules:
  0.0 270.7 jit_solution(8423820403082964999)
XLA Ops:
  0.6 0.7 subtract_convert_fusion
  1.3 0.1 reshape.19
  1.4 1.4 pad_select_fusion.vsrc
  2.8 0.1 copy.11
  2.9 0.1 broadcast_in_dim.7
  3.0 0.8 broadcast_in_dim.8.keep
  3.8 1.3 copy.13
  5.1 0.5 copy.15
  5.6 1.4 reshape.21.wsrc
  7.1 255.3 %layer.1 = (bf16[16,2048,384]{2,1,0:T(8,128)(2,1)}, bf16[16,512,384]{2,1,0:T(8,128)(2,1)}, bf16[512,2048]{1,0:T(8,128)(2,1)}, f32[512,2048]{1,0:T(8,128)}, f32[64,6144]{1,0:T(8,128)}, /*index=5*/f32[8,128]{1,0:T(8,128)}) custom-call(bf16[512,2048]{1,0:T(8,128)(2,1)} %tok.1, bf16[512,2048]{1,0:T(8,128)(2,1)} %cot.1, f32[512,128]{1,0:T(8,128)} %broadcast_in_dim.8.keep, ...), custom_call_target="tpu_custom_call" | custom-call | flops 38654705664 | bytes 50331648 | tf_op jit(solution)/shard_map/layer/pallas_call | solution.py:817
  262.3 1.4 slice_select_fusion
  263.7 0.0 copy-start
  263.7 3.3 %copy.19 = bf16[512,2048]{1,0:T(8,128)(2,1)} copy(bf16[512,2048]{1,0:T(8,128)(2,1)} %get-tuple-element.16) | data formatting | bytes 4194304
  267.1 0.0 copy-done
  267.1 0.0 copy-start.1
  267.1 2.0 copy.20
  269.1 0.5 copy-done.1
  269.6 1.1 copy.21
Async XLA Ops:
  263.7 3.3 %copy-start = (f32[512,2048]{1,0:T(8,128)S(1)}, f32[512,2048]{1,0:T(8,128)}, u32[]{:S(2)}) copy-start(f32[512,2048]{1,0:T(8,128)} %get-tuple-element.17) | copy-start | bytes 12582916
  267.1 2.5 copy-start.1

commit v5 on v4

--- a/solution.py
+++ b/solution.py
@@ -155,32 +155,36 @@
 SLOTS, SEND, PAIR, ZSEND = 8, 8, 4, 4
 TOTALS, FORE, GRADS, BACK, WEIGH = 3, 5, 6, 8, 10
 LAG1, LAG2, LAG3 = 2, 4, 6
-AHEAD_Z, AHEAD_B = 5, 3
+LAST = 6
+AHEAD_Z, AHEAD_B = 4, 3
 BAND = 32
+ACROSS = ((10, (0, 3, 6)), (15, (8, 11, 13)))
+ACROSS_SUM = ()
+PACE, GATHER, MEET, SETTLE = 2, 7, 9, 11
 
 
 def layer_kernel(
     nx, ny, units,
-    tok, cot, keep, wsrc, vsrc,
+    tok, cot, mask, weight, vectors,
     wall, pgm, outp, igo, wgo, vgo,
     vbuf, vecs, xs, gs, means, invs, rnd, rt, rtm, wf, pj, pv, grs, outs, stage, perm, pgs,
-    wb, sb, rd, rx, ry, rz, zb, sg, vsum, vrows, vtot, vin,
+    wb, sb, rd, rx, ry, rz, zb, sg, vsum, vrows, vtot, vin, cz, keep, wraw, wsrc, vsrc,
     ach, bch, qch, sin, cin, m1a, m1b, m2a, m2b,
     zs, zr, os, bs, br, dsn, dr, cs, cr, ws,
-    vzs, vzr, vxs, vxr, vo, sts, rs, rr, ps, pr, pl_, wl, gos,
+    vzs, vzr, vxs, vxr, vo, wls, sts, rs, rr, ps, pr, pl_, wl, gos,
     e1as, e1ar, e1bs, e1br, e2as, e2ar, e2bs, e2br,
     fds, fdr, fxs, fxr, fys, fyr, fzs, fzr, vsn, vrc, ous,
 ):
     gx, gy, core, mate, xn, yn = place(ny)
     tokens, width = xs.shape
     rows = wsrc.shape[1]
+    cols = wsrc.shape[2]
     block = rows * ny
-    half = block // 2
+    half, short = ny // 2, rows // 2
     groups = units // GROUP
     glanes = GROUP * LANES
     diag = xn + yn - gx
-    first = gx * block
-    mine = first + gy * rows
+    own, xq, yq, dq = gx // 2, xn // 2, yn // 2, diag // 2
     count = nx * ny
     me = gx * ny + gy
 
@@ -199,10 +203,20 @@
         to = lax.rem(me + j, count)
         pl.semaphore_signal(barrier, inc=1, device_id=(to // ny, lax.rem(to, ny)), device_id_type=MESH)
 
+    raw = pltpu.make_async_copy(weight, wraw, wls)
+    raw.start()
     each(count, greet, 1)
 
-    def band(b, n=block):
-        return pl.ds(pl.multiple_of(b, 16), n)
+    def among(u, some):
+        hit = u < 0
+        for s in some:
+            hit = hit | (u == s)
+        return hit
+
+    across = tuple(c for c, _ in ACROSS)
+
+    def straight(u, run):
+        pl.when(jnp.logical_not(among(u, across)))(lambda: run(u))
 
     chunks = width // glanes
 
@@ -224,23 +238,23 @@
     own_vec = pltpu.make_async_copy(vsrc, vbuf.at[me], vo)
 
     def z_copy(u, j):
-        return remote(wsrc.at[u], wall.at[u, band(mine, rows)], zs.at[u, j - 1], zr.at[u, j - 1], (gx, peer_y(j)))
+        return remote(wsrc.at[u], wall.at[u, own, core, gy], zs.at[u, j - 1], zr.at[u, j - 1], (gx, peer_y(j)))
 
     def own_copy(u):
-        return pltpu.make_async_copy(wsrc.at[u], wall.at[u, band(mine, rows)], os.at[u])
+        return pltpu.make_async_copy(wsrc.at[u], wall.at[u, own, core, gy], os.at[u])
 
     def band_copy(u, i):
         to = (mate, xn, yn)[i]
         recv = cr.at[u, 0] if i == 0 else br.at[u, i - 1]
-        part = wall.at[u, band(first)]
+        part = wall.at[u, own, core]
         return remote(part, part, bs.at[u, i], recv, (to, gy))
 
     def diag_copy(u, i):
-        part = wall.at[u, band((xn * block, yn * block + half)[i], half)]
+        part = wall.at[u, (xq, yq)[i], core, half * i:half * (i + 1)]
         return remote(part, part, dsn.at[u, i], dr.at[u, i], ((yn, xn)[i], gy))
 
     def core_copy(u, i):
-        part = wall.at[u, band((None, xn, yn, diag)[i] * block)]
+        part = wall.at[u, (own, xq, yq, dq)[i], core]
         return remote(part, part, cs.at[u, i - 1], cr.at[u, i], (mate, gy))
 
     def z_start(u):
@@ -273,14 +287,65 @@
         for i in (1, 2, 3):
             core_copy(u, i).wait_recv()
 
+    def a_copy(u, i):
+        return remote(
+            wsrc.at[u], wall.at[u, own, core, gy], bs.at[u, i], br.at[u, i - 1], ((None, xn, yn)[i], gy)
+        )
+
+    def a_diag(u, i):
+        part = wall.at[u, (xq, yq)[i], core, gy, short * i:short * (i + 1)]
+        return remote(part, part, dsn.at[u, i], dr.at[u, i], ((yn, xn)[i], gy))
+
+    def a_z(u, j):
+        part = wall.at[u, :, core, gy]
+        return remote(part, part, zs.at[u, j - 1], zr.at[u, j - 1], (gx, peer_y(j)))
+
+    def a_core(u):
+        part = wall.at[u, :, core]
+        return remote(part, part, bs.at[u, 0], cr.at[u, 0], (mate, gy))
+
+    def a_start(u):
+        own_copy(u).start()
+        for i in (1, 2):
+            a_copy(u, i).start()
+
+    def a_turn(u):
+        own_copy(u).wait()
+        for i in (1, 2):
+            a_copy(u, i).wait_recv()
+        for i in (0, 1):
+            a_diag(u, i).start()
+
+    def a_meet(u):
+        for i in (0, 1):
+            a_diag(u, i).wait_recv()
+
+    def a_share(u):
+        for j in range(1, ny):
+            a_z(u, j).wait_recv()
+        a_core(u).start()
+
+    zero = jnp.zeros((vectors.shape[0], LANES - rows), BF16)
+    odd = lax.rem(me, 2) == 1
+    tile = jnp.where(
+        odd, jnp.concatenate([zero, vectors[...]], 1).astype(F32), jnp.concatenate([vectors[...], zero], 1).astype(F32)
+    )
+    pad = jnp.zeros((16 - vectors.shape[0], LANES), F32)
+    vsrc[...] = jnp.concatenate([tile, pad], 0).astype(BF16)
+    raw.wait()
+    for u in range(units):
+        for s in range(3):
+            at = s * width + u * LANES
+            wsrc[u, :, s * LANES:(s + 1) * LANES] = wraw[:, at:at + LANES]
+
     pl.semaphore_wait(barrier, count - 1)
     own_vec.start()
     for j in range(1, ny):
         vz(j).start()
+    for u in across:
+        a_start(u)
     for u in range(AHEAD_Z):
         z_start(u)
-
-    perm[...] = run_matrix(tokens, False)
 
     def to_runs(i, into):
         stage_copy(i).wait()
@@ -291,16 +356,6 @@
         if i + 2 < 2 * chunks:
             stage_copy(i + 2).start()
 
-    for i in range(chunks):
-        to_runs(i, xs)
-    z_wait(0)
-    own_vec.wait()
-    for j in range(1, ny):
-        vz(j).wait_recv()
-    for j in range(1, nx):
-        vx(j).start()
-    z_wait(1)
-
     def moments(i):
         r = pl.ds(pl.multiple_of(i * BAND, BAND), BAND)
         x = xs[r, :].astype(F32)
@@ -310,37 +365,77 @@
         means[r, :] = jnp.broadcast_to(mean, (BAND, LANES))
         invs[r, :] = jnp.broadcast_to(inv, (BAND, LANES))
 
-    each(tokens // BAND, moments)
+    def rounding(i):
+        r = pl.ds(pl.multiple_of(i * BAND, BAND), BAND)
+        normed = (xs[r, :].astype(F32) - means[r, 0:1]) * invs[r, 0:1]
+        rnd[r, :] = (normed * vecs[0:1, :] + vecs[1:2, :]).astype(BF16)
+
+    quads = nx // 2
+
+    def turn(i):
+        at = pl.ds(pl.multiple_of(i * block, 16), block)
+        rt[at, 0:tokens] = rnd[:, pl.ds(pl.multiple_of((2 * i + core) * block, LANES), block)].T
+        rtm[at, :] = rnd[:, pl.ds(pl.multiple_of((2 * i + 1 - core) * block, LANES), block)].T
+
+    r_mate = remote(rtm, rt.at[:, tokens:2 * tokens], rs, rr, (mate, gy))
+
+    def gather_tick(k):
+        pl.when(k + AHEAD_Z < units)(lambda: straight(k + AHEAD_Z, z_start))
+        pl.when(k + AHEAD_B < units)(lambda: straight(k + AHEAD_B, z_wait))
+        pl.when(k < units)(lambda: straight(k, xy_wait))
+        pl.when((k >= 1) & (k <= units))(lambda: straight(k - 1, diag_wait))
+        for c, times in ACROSS:
+            for j, t in enumerate(times):
+                pl.when(k == t)(lambda c=c, j=j: a_z(c, j + 1).start())
+            pl.when(k == c + 1)(functools.partial(a_share, c))
+
+    bands = tokens // BAND
+    perm[...] = run_matrix(tokens, False)
+    for i in range(chunks // 2):
+        to_runs(i, xs)
+    z_wait(0)
+    for i in range(chunks // 2, chunks):
+        to_runs(i, xs)
+    own_vec.wait()
+    for j in range(1, ny):
+        vz(j).wait_recv()
+    for j in range(1, nx):
+        vx(j).start()
+    for u in across:
+        a_turn(u)
+    z_wait(1)
+    each(bands // 2, moments)
     for u in range(2, AHEAD_B):
         z_wait(u)
+    for u in across:
+        a_meet(u)
+    gather_tick(0)
+    each(bands, moments, bands // 2)
     for j in range(1, nx):
         vx(j).wait_recv()
     for c in range(width // LANES):
         part = vbuf[2 * c].astype(F32) + vbuf[2 * c + 1].astype(F32)
         vecs[:, c * LANES:(c + 1) * LANES] = part[0:8, :]
-
-    def rounding(i):
-        r = pl.ds(pl.multiple_of(i * BAND, BAND), BAND)
-        normed = (xs[r, :].astype(F32) - means[r, 0:1]) * invs[r, 0:1]
-        rnd[r, :] = (normed * vecs[0:1, :] + vecs[1:2, :]).astype(BF16)
-
-    each(tokens // BAND, rounding)
-
-    quads = nx // 2
-
-    def turn(i):
-        at = pl.ds(pl.multiple_of(i * block, 16), block)
-        rt[at, 0:tokens] = rnd[:, pl.ds(pl.multiple_of((2 * i + core) * block, LANES), block)].T
-        rtm[at, :] = rnd[:, pl.ds(pl.multiple_of((2 * i + 1 - core) * block, LANES), block)].T
-
-    r_mate = remote(rtm, rt.at[:, tokens:2 * tokens], rs, rr, (mate, gy))
+    each(bands // 2, rounding)
+    gather_tick(1)
+    each(bands, rounding, bands // 2)
+    kept = (1 - mask[...]).astype(F32)
+    keep[...] = jnp.dot(
+        (perm[...].astype(F32) * kept).astype(BF16), jnp.ones((tokens, LANES), BF16), preferred_element_type=F32
+    )
+    for i in range(chunks, chunks + chunks // 2):
+        to_runs(i, gs)
+    gather_tick(2)
+    straight(0, core_wait)
 
     def late_start():
+        for i in range(chunks + chunks // 2, 2 * chunks):
+            to_runs(i, gs)
+        perm[...] = run_matrix(tokens, True)
+
+    def late_turn():
         each(quads, turn)
         r_mate.start()
-        for i in range(chunks, 2 * chunks):
-            to_runs(i, gs)
-        perm[...] = run_matrix(tokens, True)
 
     def e_copies(buf, send, recv, q, level):
         if level == 0:
@@ -368,7 +463,7 @@
 
     def project(u):
         front_load(u).wait()
-        pj[lax.rem(u, SLOTS)] = jnp.dot(rnd[...], wf[...], preferred_element_type=F32)
+        pj[lax.rem(u, SLOTS)] = jnp.dot(rnd[...], wf[...].reshape(width, -1), preferred_element_type=F32)
 
     def vec(i, u):
         return vecs[i:i + 1, lanes_of(u)]
@@ -557,27 +652,26 @@
     def back_load(u):
         return pltpu.make_async_copy(wall.at[u], wb, wl)
 
-    def rows_of(chip, part, n=half):
-        return pl.ds(pl.multiple_of((chip // 2) * block + part * half, 16), n)
+    def some(part):
+        return pl.ds(part * half, half)
 
     def sent(u):
         return sb.at[lax.rem(u, SEND)]
 
     def d_copy(u, i):
         return remote(
-            sent(u).at[rows_of(diag, i)], rd.at[u, i * half:(i + 1) * half], fds.at[u, i], fdr.at[u, i], ((yn, xn)[i], gy)
+            sent(u).at[dq, some(i)], rd.at[u, some(i)], fds.at[u, i], fdr.at[u, i], ((yn, xn)[i], gy)
         )
 
     def x_copy(u, i):
-        return remote(sent(u).at[rows_of(xn, i)], rx.at[u, i * half:(i + 1) * half], fxs.at[u, i], fxr.at[u, i], (xn, gy))
+        return remote(sent(u).at[xq, some(i)], rx.at[u, some(i)], fxs.at[u, i], fxr.at[u, i], (xn, gy))
 
     def y_copy(u, i):
-        return remote(sent(u).at[rows_of(yn, i)], ry.at[u, i * half:(i + 1) * half], fys.at[u, i], fyr.at[u, i], (yn, gy))
+        return remote(sent(u).at[yq, some(i)], ry.at[u, some(i)], fys.at[u, i], fyr.at[u, i], (yn, gy))
 
     def f_copy(u, j):
         to = lax.rem(gy + j, ny)
-        src = zb.at[lax.rem(u, ZSEND), pl.ds(pl.multiple_of(to * rows, 16), rows)]
-        return remote(src, rz.at[u, j - 1], fzs.at[u, j - 1], fzr.at[u, j - 1], (gx, to))
+        return remote(zb.at[lax.rem(u, ZSEND), to], rz.at[u, j - 1], fzs.at[u, j - 1], fzr.at[u, j - 1], (gx, to))
 
     def next_loads(u):
         pg_mate(u).wait_recv()
@@ -587,7 +681,7 @@
     def weigh(u):
         slot, pair = lax.rem(u, SEND), lax.rem(u, PAIR)
 
-        @pl.when(u >= SEND)
+        @pl.when((u >= SEND) & jnp.logical_not(among(u - SEND, ACROSS_SUM)))
         def _():
             for i in (0, 1):
                 d_copy(u - SEND, i).wait_send()
@@ -595,36 +689,39 @@
                 y_copy(u - SEND, i).wait_send()
 
         pg_load(u).wait()
-        sb[slot] = jnp.dot(rt[...], pgs[pair], preferred_element_type=F32).astype(BF16)
-        for i in (0, 1):
-            d_copy(u, i).start()
-        x_copy(u, 1).start()
-        y_copy(u, 0).start()
+        sb[slot] = jnp.dot(rt[...], pgs[pair], preferred_element_type=F32).astype(BF16).reshape(sb.shape[1:])
+
+        @pl.when(jnp.logical_not(among(u, ACROSS_SUM)))
+        def _():
+            for i in (0, 1):
+                d_copy(u, i).start()
+            x_copy(u, 1).start()
+            y_copy(u, 0).start()
 
     def spread(u):
         pair = lax.rem(u, PAIR)
         back_load(u).wait()
-        own = pgs[pair, 0:tokens, :]
-        sg[...] += lax.dot_general(own, wb[...], (((1,), (1,)), ((), ())), preferred_element_type=F32)
+        mine = pgs[pair, 0:tokens, :]
+        sg[...] += lax.dot_general(mine, wb[...].reshape(width, -1), (((1,), (1,)), ((), ())), preferred_element_type=F32)
         sg[:, lanes_of(u)] += pgs[pair, 0:tokens, LANES:2 * LANES].astype(F32) * vecs[2:3, lanes_of(u)]
         pg_mate(u).wait_send()
 
-    def fold(slot, r, more):
-        sb[slot, r, :] = (sb[slot, r, :].astype(F32) + more.astype(F32)).astype(BF16)
+    def fold(ref, at, more):
+        ref[at] = (ref[at].astype(F32) + more.astype(F32)).astype(BF16)
 
     def meet(u):
         slot = lax.rem(u, SEND)
         for i in (0, 1):
             d_copy(u, i).wait_recv()
-        fold(slot, rows_of(xn, 0), rd[u, 0:half])
+        fold(sb, (slot, xq, some(0)), rd[u, 0:half])
         x_copy(u, 0).start()
-        fold(slot, rows_of(yn, 1), rd[u, half:block])
+        fold(sb, (slot, yq, some(1)), rd[u, half:ny])
         y_copy(u, 1).start()
 
     def column(u):
         slot, zslot = lax.rem(u, SEND), lax.rem(u, ZSEND)
 
-        @pl.when(u >= ZSEND)
+        @pl.when((u >= ZSEND) & jnp.logical_not(among(u - ZSEND, ACROSS_SUM)))
         def _():
             for j in range(1, ny):
                 f_copy(u - ZSEND, j).wait_send()
@@ -632,24 +729,73 @@
         for i in (0, 1):
             x_copy(u, i).wait_recv()
             y_copy(u, i).wait_recv()
-        total = sb[slot, rows_of(gx, 0, block), :].astype(F32) + rx[u].astype(F32) + ry[u].astype(F32)
+        total = sb[slot, own].astype(F32) + rx[u].astype(F32) + ry[u].astype(F32)
         zb[zslot] = total.astype(BF16)
         for j in range(1, ny):
             f_copy(u, j).start()
 
     def settle(u):
         slot = lax.rem(u, SEND)
-        r = pl.ds(pl.multiple_of(gy * rows, 16), rows)
-        at = pl.ds(pl.multiple_of((gx // 2) * block + gy * rows, 16), rows)
-        total = sb[slot, at, :].astype(F32) + rx[u, r, :].astype(F32) + ry[u, r, :].astype(F32)
+        total = sb[slot, own, gy].astype(F32) + rx[u, gy].astype(F32) + ry[u, gy].astype(F32)
         for j in range(1, ny):
             f_copy(u, j).wait_recv()
         for j in range(1, ny):
             total = total + rz[u, j - 1].astype(F32)
+        place_sum(u, total)
+
+    def place_sum(u, total):
         for i in range(3):
             wgo[:, lanes_of(u + i * units)] = total[:, i * LANES:(i + 1) * LANES]
 
-    bands = tokens // BAND
+    def part(i):
+        return pl.ds(i * short, short)
+
+    def b_z(u, j):
+        to = peer_y(j)
+        return remote(sent(u).at[:, to], (rd, rx, ry)[j - 1].at[u], fzs.at[u, j - 1], fzr.at[u, j - 1], (gx, to))
+
+    def b_diag(u, n, i):
+        return remote(cz.at[n, dq, part(i)], rz.at[u, 0, part(i)], fds.at[u, i], fdr.at[u, i], ((yn, xn)[i], gy))
+
+    def b_x(u, n, i):
+        return remote(cz.at[n, xq, part(i)], rz.at[u, 1, part(i)], fxs.at[u, i], fxr.at[u, i], (xn, gy))
+
+    def b_y(u, n, i):
+        return remote(cz.at[n, yq, part(i)], rz.at[u, 2, part(i)], fys.at[u, i], fyr.at[u, i], (yn, gy))
+
+    def b_gather(u, n):
+        for j in range(1, ny):
+            b_z(u, j).wait()
+            if u >= ZSEND and u - ZSEND not in ACROSS_SUM:
+                f_copy(u - ZSEND, j).wait_send()
+        total = sb[lax.rem(u, SEND), :, gy].astype(F32)
+        for ref in (rd, rx, ry):
+            total = total + ref[u].astype(F32)
+        cz[n] = total.astype(BF16)
+        for i in (0, 1):
+            b_diag(u, n, i).start()
+        b_x(u, n, 1).start()
+        b_y(u, n, 0).start()
+
+    def b_meet(u, n):
+        for i in (0, 1):
+            b_diag(u, n, i).wait_recv()
+        fold(cz, (n, xq, part(0)), rz[u, 0, part(0)])
+        b_x(u, n, 0).start()
+        fold(cz, (n, yq, part(1)), rz[u, 0, part(1)])
+        b_y(u, n, 1).start()
+
+    def b_settle(u, n):
+        for i in (0, 1):
+            b_x(u, n, i).wait_recv()
+            b_y(u, n, i).wait_recv()
+        place_sum(u, cz[n, own].astype(F32) + rz[u, 1].astype(F32) + rz[u, 2].astype(F32))
+
+    def b_drain(u, n):
+        for i in (0, 1):
+            b_diag(u, n, i).wait_send()
+            b_x(u, n, i).wait_send()
+            b_y(u, n, i).wait_send()
 
     def finish(i):
         r = pl.ds(pl.multiple_of(i * BAND, BAND), BAND)
@@ -700,15 +846,21 @@
     def tick(k, _):
         u = k - 3
         v = u - WEIGH
-        pl.when(k + AHEAD_Z < units)(lambda: z_start(k + AHEAD_Z))
-        pl.when(k + AHEAD_B < units)(lambda: z_wait(k + AHEAD_B))
-        pl.when(k < units)(lambda: xy_wait(k))
-        pl.when((k >= 1) & (k <= units))(lambda: diag_wait(k - 1))
-        pl.when(k == 0)(late_start)
-
-        pl.when((v >= LAG1) & (v < units + LAG1))(lambda: meet(v - LAG1))
-        pl.when((v >= LAG2) & (v < units + LAG2))(lambda: column(v - LAG2))
-        pl.when(v >= LAG3)(lambda: settle(v - LAG3))
+        gather_tick(k)
+        pl.when(k == 3)(late_start)
+        pl.when(k == 5)(late_turn)
+
+        def summed(lag, run):
+            w = v - lag
+            pl.when((w >= 0) & (w < units) & jnp.logical_not(among(w, ACROSS_SUM)))(lambda: run(w))
+
+        summed(LAG1, meet)
+        summed(LAG2, column)
+        summed(LAG3, settle)
+        for n, c in enumerate(ACROSS_SUM):
+            pl.when(v == c + GATHER)(functools.partial(b_gather, c, n))
+            pl.when(v == c + MEET)(functools.partial(b_meet, c, n))
+            pl.when(v == c + SETTLE)(functools.partial(b_settle, c, n))
 
         @pl.when(v == 0)
         def _():
@@ -721,6 +873,10 @@
             weigh(v)
             spread(v)
 
+        for c in ACROSS_SUM:
+            for j in range(1, ny):
+                pl.when(v == c + PACE * (j - 1))(lambda c=c, j=j: b_z(c, j).start())
+
         pl.when((v >= -1) & (v < units - 1))(lambda: next_loads(v + 1))
 
         def event(lag, run):
@@ -736,9 +892,11 @@
         def _():
             project(u)
 
-        @pl.when((u >= -1) & (u < units - 1))
+        @pl.when((u >= 0) & (u < units - 1))
         def _():
-            core_wait(u + 1)
+            straight(u + 1, core_wait)
+            for c in across:
+                pl.when(u + 1 == c)(lambda c=c: a_core(c).wait_recv())
             front_load(u + 1).start()
 
         @pl.when((u >= 0) & (u < units))
@@ -756,7 +914,8 @@
         pl.when(v == units + 2)(natural)
         return 0
 
-    lax.fori_loop(0, units + WEIGH + 3 + LAG3, tick, 0)
+    front_load(0).start()
+    lax.fori_loop(3, units + WEIGH + 3 + LAST, tick, 0)
 
     each(count, lambda j: v_recv(j).wait_recv(), 1)
     vin[me] = vtot[me // 2]
@@ -772,7 +931,17 @@
         for i in (1, 2, 3):
             core_copy(u, i).wait_send()
 
-    each(units, drain)
+    each(units, lambda u: straight(u, drain))
+    for c in across:
+        for j in range(1, ny):
+            a_z(c, j).wait_send()
+        for i in (1, 2):
+            a_copy(c, i).wait_send()
+        for i in (0, 1):
+            a_diag(c, i).wait_send()
+        a_core(c).wait_send()
+    for n, c in enumerate(ACROSS_SUM):
+        b_drain(c, n)
 
     def drain_send(u):
         for i in (0, 1):
@@ -780,7 +949,7 @@
             x_copy(u, i).wait_send()
             y_copy(u, i).wait_send()
 
-    each(units, drain_send, units - SEND)
+    each(units, lambda u: pl.when(jnp.logical_not(among(u, ACROSS_SUM)))(lambda: drain_send(u)), units - SEND)
 
     def drain_z(u):
         for j in range(1, ny):
@@ -806,9 +975,10 @@
         grad_copy(c).wait()
 
 
-def layer(nx, ny, tok, cot, keep, wsrc, vsrc):
+def layer(nx, ny, tok, cot, mask, weight, vectors):
     tokens, width = tok.shape
-    units, rows, cols = wsrc.shape
+    rows, cols = weight.shape[0], 3 * LANES
+    units = width // LANES
     groups, glanes, block, count = units // GROUP, GROUP * LANES, rows * ny, nx * ny
     dma = pltpu.SemaphoreType.DMA
     any_, vmem = pl.BlockSpec(memory_space=pl.ANY), pl.BlockSpec(memory_space=pltpu.VMEM)
@@ -818,30 +988,32 @@
         functools.partial(layer_kernel, nx, ny, units),
         name="layer",
         out_shape=(
-            s((units, width, cols), BF16), s((units, tokens, cols), BF16),
+            s((units, nx // 2, 2, ny, rows, cols), BF16), s((units, tokens, cols), BF16),
             s((tokens, width), BF16), s((tokens, width), F32), s((rows, 3 * width), F32), s((8, LANES), F32),
         ),
-        in_specs=[any_, any_, vmem, any_, any_],
+        in_specs=[any_, any_, vmem, any_, vmem],
         out_specs=(any_,) * 4 + (vmem,) * 2,
         scratch_shapes=[
             v((count, 16, LANES), BF16), v((8, width), F32),
             v((tokens, width), BF16), v((tokens, width), BF16), v((tokens, LANES), F32), v((tokens, LANES), F32),
             v((tokens, width), BF16), v((width // 2, 2 * tokens), BF16), v((width // 2, tokens), BF16),
-            v((width, cols), BF16),
+            v((nx // 2, 2, ny, rows, cols), BF16),
             v((SLOTS, tokens, cols), F32), v((SLOTS, tokens, LANES), F32),
             v((tokens, width), F32), v((tokens, glanes), BF16), v((2, tokens, glanes), BF16),
             v((tokens, tokens), BF16), v((PAIR, 2 * tokens, cols), BF16),
-            v((width, cols), BF16), v((SEND, width // 2, cols), BF16),
-            v((units, block, cols), BF16), v((units, block, cols), BF16), v((units, block, cols), BF16),
-            v((units, ny - 1, rows, cols), BF16), v((ZSEND, block, cols), BF16),
+            v((nx // 2, 2, ny, rows, cols), BF16), v((SEND, nx // 2, ny, rows, cols), BF16),
+            *[v((units, ny, rows, cols), BF16)] * 3,
+            v((units, ny - 1, rows, cols), BF16), v((ZSEND, ny, rows, cols), BF16),
             v((tokens, width), F32), v((8, width), F32), v((16, width), F32),
             v((width // LANES, 8, LANES), F32), v((count, 8, LANES), F32),
+            v((max(1, len(ACROSS_SUM)), nx // 2, rows, cols), BF16), v((tokens, LANES), F32),
+            v((rows, 3 * width), BF16), v((units, rows, cols), BF16), v((16, LANES), BF16),
             *[v((groups,) + msg, F32)] * 5,
             v((groups, ny) + msg, F32), v((groups, nx) + msg, F32),
             v((groups, ny) + msg, F32), v((groups, nx) + msg, F32),
             dma((units, ny - 1)), dma((units, ny - 1)), dma((units,)), dma((units, 3)), dma((units, 2)),
             dma((units, 2)), dma((units, 2)), dma((units, 3)), dma((units, 4)), dma,
-            dma((ny - 1,)), dma((ny - 1,)), dma((nx - 1,)), dma((nx - 1,)), dma, dma((2,)),
+            dma((ny - 1,)), dma((ny - 1,)), dma((nx - 1,)), dma((nx - 1,)), dma, dma, dma((2,)),
             dma, dma, dma((units,)), dma((units,)), dma, dma, dma((groups,)),
             dma((groups, ny - 1)), dma((groups, ny - 1)), dma((groups, nx - 1)), dma((groups, nx - 1)),
             dma((groups, ny - 1)), dma((groups, ny - 1)), dma((groups, nx - 1)), dma((groups, nx - 1)),
@@ -854,20 +1026,14 @@
         cost_estimate=pl.CostEstimate(
             flops=6 * tokens * width * units * cols, bytes_accessed=4 * width * units * cols, transcendentals=0
         ),
-    )(tok, cot, keep, wsrc, vsrc)
+    )(tok, cot, mask, weight, vectors)
 
 
 def fast(nx, ny, tokens, reset_mask, weight, vectors, cotangent):
-    count, width = tokens.shape
     rows = weight.shape[0]
-    units, steps = width // LANES, count // RUNS
-    keep = (1 - reset_mask).astype(F32).reshape(RUNS, steps).T.reshape(count, 1)
-    keep = jnp.broadcast_to(keep, (count, LANES))
-    wsrc = weight.reshape(rows, 3, units, LANES).transpose(2, 0, 1, 3).reshape(units, rows, 3 * LANES)
     odd = lax.rem(lax.axis_index("gx") * ny + lax.axis_index("gy"), 2) == 1
-    low, high = (jnp.pad(vectors, ((0, 10), side)) for side in ((0, rows), (rows, 0)))
-    vsrc = jnp.where(odd, high, low)
-    _, _, outp, grad, weight_grad, tile = layer(nx, ny, tokens, cotangent, keep, wsrc, vsrc)
+    mask = reset_mask.reshape(1, -1)
+    _, _, outp, grad, weight_grad, tile = layer(nx, ny, tokens, cotangent, mask, weight, vectors)
     vector_grad = jnp.where(odd, tile[:6, rows:2 * rows], tile[:6, :rows])
     return outp, grad, weight_grad, vector_grad
 
@@ -884,7 +1050,7 @@
 
     def body(tokens, reset_mask, weight, vectors, cotangent):
         whole_tiles = weight.shape[0] % 16 == 0 and tokens.shape[0] % 256 == 0
-        if nx == 8 and whole_tiles and 2 * weight.shape[0] == LANES and tokens.shape[1] % 2048 == 0:
+        if (nx, ny) == (8, 4) and whole_tiles and 2 * weight.shape[0] == LANES and tokens.shape[1] % 2048 == 0:
             return fast(nx, ny, tokens, reset_mask, weight, vectors, cotangent)
         return local(tokens, reset_mask, weight, vectors, cotangent)
 

time: 271 us -> 263 us (0.970)
  local copies, waits for them, and re-layouts: 11.3 us -> 7 us
    unnamed x8 -> x7, local copies, waits for them, and re-layouts: 8.25 us -> 7 us
where the time goes in v5:
time: 263 us; the launch traced here: 262 us
  Pallas kernels  253 us (96%)
  local copies, waits for them, and re-layouts  7 us (3%)
    pallas_call x1, Pallas kernels, layer(): pl.pallas_call(functools.partial(layer_kernel, nx, ny, units), name='laye...  253 us
    unnamed x7, local copies, waits for them, and re-layouts  7 us

profile of v5, /device:TPU:0, one launch (start us, length us, event | category | flops | bytes accessed | tf_op | source)
XLA Modules:
  0.0 262.0 jit_solution(7557499268537366893)
XLA Ops:
  0.6 253.0 %layer.1 = (bf16[16,4,2,4,64,384]{5,4,3,2,1,0:T(8,128)(2,1)}, bf16[16,512,384]{2,1,0:T(8,128)(2,1)}, bf16[512,2048]{1,0:T(8,128)(2,1)}, f32[512,2048]{1,0:T(8,12...) custom-call(bf16[512,2048]{1,0:T(8,128)(2,1)} %tok.1, bf16[512,2048]{1,0:T(8,128)(2,1)} %cot.1, s32[1,512]{1,0:T(1,128)} %bitcast.1, ...), custom_call_target="tpu_custom_call" | custom-call | flops 38654705664 | bytes 50331648 | tf_op jit(solution)/shard_map/layer/pallas_call | solution.py:987
  253.6 1.4 slice_select_fusion
  255.0 0.0 copy-start
  255.0 3.3 %copy.12 = bf16[512,2048]{1,0:T(8,128)(2,1)} copy(bf16[512,2048]{1,0:T(8,128)(2,1)} %get-tuple-element.16) | data formatting | bytes 4194304
  258.4 0.0 copy-done
  258.4 0.0 copy-start.1
  258.4 2.0 copy.13
  260.4 0.5 copy-done.1
  260.9 1.1 copy.14
Async XLA Ops:
  255.0 3.3 %copy-start = (f32[512,2048]{1,0:T(8,128)S(1)}, f32[512,2048]{1,0:T(8,128)}, u32[]{:S(2)}) copy-start(f32[512,2048]{1,0:T(8,128)} %get-tuple-element.17) | copy-start | bytes 12582916
  258.4 2.5 copy-start.1

commit v6 on v5

--- a/solution.py
+++ b/solution.py
@@ -156,11 +156,10 @@
 TOTALS, FORE, GRADS, BACK, WEIGH = 3, 5, 6, 8, 10
 LAG1, LAG2, LAG3 = 2, 4, 6
 LAST = 6
-AHEAD_Z, AHEAD_B = 4, 3
+AHEAD_Z, AHEAD_B = 5, 3
 BAND = 32
 ACROSS = ((10, (0, 3, 6)), (15, (8, 11, 13)))
 ACROSS_SUM = ()
-PACE, GATHER, MEET, SETTLE = 2, 7, 9, 11
 
 
 def layer_kernel(
@@ -214,6 +213,7 @@
         return hit
 
     across = tuple(c for c, _ in ACROSS)
+    turned = tuple(c for c, _, _ in ACROSS_SUM)
 
     def straight(u, run):
         pl.when(jnp.logical_not(among(u, across)))(lambda: run(u))
@@ -344,8 +344,7 @@
         vz(j).start()
     for u in across:
         a_start(u)
-    for u in range(AHEAD_Z):
-        z_start(u)
+    z_start(0)
 
     def to_runs(i, into):
         stage_copy(i).wait()
@@ -394,6 +393,8 @@
     for i in range(chunks // 2):
         to_runs(i, xs)
     z_wait(0)
+    z_start(1)
+    z_start(2)
     for i in range(chunks // 2, chunks):
         to_runs(i, xs)
     own_vec.wait()
@@ -404,6 +405,8 @@
     for u in across:
         a_turn(u)
     z_wait(1)
+    for u in range(3, AHEAD_Z):
+        z_start(u)
     each(bands // 2, moments)
     for u in range(2, AHEAD_B):
         z_wait(u)
@@ -681,7 +684,7 @@
     def weigh(u):
         slot, pair = lax.rem(u, SEND), lax.rem(u, PAIR)
 
-        @pl.when((u >= SEND) & jnp.logical_not(among(u - SEND, ACROSS_SUM)))
+        @pl.when((u >= SEND) & jnp.logical_not(among(u - SEND, turned)))
         def _():
             for i in (0, 1):
                 d_copy(u - SEND, i).wait_send()
@@ -691,7 +694,7 @@
         pg_load(u).wait()
         sb[slot] = jnp.dot(rt[...], pgs[pair], preferred_element_type=F32).astype(BF16).reshape(sb.shape[1:])
 
-        @pl.when(jnp.logical_not(among(u, ACROSS_SUM)))
+        @pl.when(jnp.logical_not(among(u, turned)))
         def _():
             for i in (0, 1):
                 d_copy(u, i).start()
@@ -721,7 +724,7 @@
     def column(u):
         slot, zslot = lax.rem(u, SEND), lax.rem(u, ZSEND)
 
-        @pl.when((u >= ZSEND) & jnp.logical_not(among(u - ZSEND, ACROSS_SUM)))
+        @pl.when((u >= ZSEND) & jnp.logical_not(among(u - ZSEND, turned)))
         def _():
             for j in range(1, ny):
                 f_copy(u - ZSEND, j).wait_send()
@@ -766,7 +769,7 @@
     def b_gather(u, n):
         for j in range(1, ny):
             b_z(u, j).wait()
-            if u >= ZSEND and u - ZSEND not in ACROSS_SUM:
+            if u >= ZSEND and u - ZSEND not in turned:
                 f_copy(u - ZSEND, j).wait_send()
         total = sb[lax.rem(u, SEND), :, gy].astype(F32)
         for ref in (rd, rx, ry):
@@ -852,15 +855,14 @@
 
         def summed(lag, run):
             w = v - lag
-            pl.when((w >= 0) & (w < units) & jnp.logical_not(among(w, ACROSS_SUM)))(lambda: run(w))
+            pl.when((w >= 0) & (w < units) & jnp.logical_not(among(w, turned)))(lambda: run(w))
 
         summed(LAG1, meet)
         summed(LAG2, column)
         summed(LAG3, settle)
-        for n, c in enumerate(ACROSS_SUM):
-            pl.when(v == c + GATHER)(functools.partial(b_gather, c, n))
-            pl.when(v == c + MEET)(functools.partial(b_meet, c, n))
-            pl.when(v == c + SETTLE)(functools.partial(b_settle, c, n))
+        for n, (c, _, steps) in enumerate(ACROSS_SUM):
+            for t, run in zip(steps, (b_gather, b_meet, b_settle)):
+                pl.when(v == t)(functools.partial(run, c, n))
 
         @pl.when(v == 0)
         def _():
@@ -873,9 +875,9 @@
             weigh(v)
             spread(v)
 
-        for c in ACROSS_SUM:
-            for j in range(1, ny):
-                pl.when(v == c + PACE * (j - 1))(lambda c=c, j=j: b_z(c, j).start())
+        for c, times, _ in ACROSS_SUM:
+            for j, t in enumerate(times):
+                pl.when(v == t)(lambda c=c, j=j: b_z(c, j + 1).start())
 
         pl.when((v >= -1) & (v < units - 1))(lambda: next_loads(v + 1))
 
@@ -940,7 +942,7 @@
         for i in (0, 1):
             a_diag(c, i).wait_send()
         a_core(c).wait_send()
-    for n, c in enumerate(ACROSS_SUM):
+    for n, c in enumerate(turned):
         b_drain(c, n)
 
     def drain_send(u):
@@ -949,7 +951,7 @@
             x_copy(u, i).wait_send()
             y_copy(u, i).wait_send()
 
-    each(units, lambda u: pl.when(jnp.logical_not(among(u, ACROSS_SUM)))(lambda: drain_send(u)), units - SEND)
+    each(units, lambda u: pl.when(jnp.logical_not(among(u, turned)))(lambda: drain_send(u)), units - SEND)
 
     def drain_z(u):
         for j in range(1, ny):
@@ -1009,8 +1011,8 @@
             v((max(1, len(ACROSS_SUM)), nx // 2, rows, cols), BF16), v((tokens, LANES), F32),
             v((rows, 3 * width), BF16), v((units, rows, cols), BF16), v((16, LANES), BF16),
             *[v((groups,) + msg, F32)] * 5,
-            v((groups, ny) + msg, F32), v((groups, nx) + msg, F32),
-            v((groups, ny) + msg, F32), v((groups, nx) + msg, F32),
+            v((groups, ny, 2, glanes), F32), v((groups, nx, 2, glanes), F32),
+            v((groups, ny, 1, glanes), F32), v((groups, nx, 1, glanes), F32),
             dma((units, ny - 1)), dma((units, ny - 1)), dma((units,)), dma((units, 3)), dma((units, 2)),
             dma((units, 2)), dma((units, 2)), dma((units, 3)), dma((units, 4)), dma,
             dma((ny - 1,)), dma((ny - 1,)), dma((nx - 1,)), dma((nx - 1,)), dma, dma, dma((2,)),

time: 263 us -> 248 us (0.943)
  Pallas kernels: 253 us -> 239 us
    pallas_call x1, Pallas kernels: 253 us -> 239 us  [layer(): pl.pallas_call(functools.partial(layer_kernel, nx, ny, units), name='laye...]
where the time goes in v6:
time: 248 us
  Pallas kernels  239 us (96%)
  local copies, waits for them, and re-layouts  7 us (3%)
    pallas_call x1, Pallas kernels, layer(): pl.pallas_call(functools.partial(layer_kernel, nx, ny, units), name='laye...  239 us
    unnamed x7, local copies, waits for them, and re-layouts  7 us

profile of v6, /device:TPU:0, one launch (start us, length us, event | category | flops | bytes accessed | tf_op | source)
XLA Modules:
  0.0 248.1 jit_solution(1900798432976655531)
XLA Ops:
  0.6 239.0 %layer.1 = (bf16[16,4,2,4,64,384]{5,4,3,2,1,0:T(8,128)(2,1)}, bf16[16,512,384]{2,1,0:T(8,128)(2,1)}, bf16[512,2048]{1,0:T(8,128)(2,1)}, f32[512,2048]{1,0:T(8,12...) custom-call(bf16[512,2048]{1,0:T(8,128)(2,1)} %tok.1, bf16[512,2048]{1,0:T(8,128)(2,1)} %cot.1, s32[1,512]{1,0:T(1,128)} %bitcast.1, ...), custom_call_target="tpu_custom_call" | custom-call | flops 38654705664 | bytes 50331648 | tf_op jit(solution)/shard_map/layer/pallas_call | solution.py:989
  239.7 1.4 slice_select_fusion
  241.1 0.0 copy-start
  241.1 3.3 %copy.12 = bf16[512,2048]{1,0:T(8,128)(2,1)} copy(bf16[512,2048]{1,0:T(8,128)(2,1)} %get-tuple-element.16) | data formatting | bytes 4194304
  244.4 0.0 copy-done
  244.4 0.0 copy-start.1
  244.4 2.0 copy.13
  246.4 0.5 copy-done.1
  246.9 1.1 copy.14
Async XLA Ops:
  241.1 3.3 %copy-start = (f32[512,2048]{1,0:T(8,128)S(1)}, f32[512,2048]{1,0:T(8,128)}, u32[]{:S(2)}) copy-start(f32[512,2048]{1,0:T(8,128)} %get-tuple-element.17) | copy-start | bytes 12582916
  244.4 2.5 %copy-start.1 = (f32[64,6144]{1,0:T(8,128)S(1)}, f32[64,6144]{1,0:T(8,128)}, u32[]{:S(2)}) copy-start(f32[64,6144]{1,0:T(8,128)} %get-tuple-element.18) | copy-start | bytes 4718596

commit v7 on v6

--- a/solution.py
+++ b/solution.py
@@ -153,7 +153,7 @@
 
 
 SLOTS, SEND, PAIR, ZSEND = 8, 8, 4, 4
-TOTALS, FORE, GRADS, BACK, WEIGH = 3, 5, 6, 8, 10
+TOTALS, FORE, GRADS, BACK, WEIGH = 2, 4, 5, 7, 9
 LAG1, LAG2, LAG3 = 2, 4, 6
 LAST = 6
 AHEAD_Z, AHEAD_B = 5, 3
@@ -220,13 +220,10 @@
 
     chunks = width // glanes
 
-    def stage_copy(i):
-        src = tok if i < chunks else cot
-        c = i % chunks
-        return pltpu.make_async_copy(src.at[:, pl.ds(c * glanes, glanes)], stage.at[i % 2], sts.at[i % 2])
-
-    stage_copy(0).start()
-    stage_copy(1).start()
+    tok_load = pltpu.make_async_copy(tok, xs, sts.at[0])
+    cot_load = pltpu.make_async_copy(cot, gs, sts.at[1])
+    tok_load.start()
+    cot_load.start()
 
     def vz(j):
         return remote(vsrc, vbuf.at[me], vzs.at[j - 1], vzr.at[j - 1], (gx, peer_y(j)))
@@ -347,13 +344,8 @@
     z_start(0)
 
     def to_runs(i, into):
-        stage_copy(i).wait()
-        c = i % chunks
-        into[:, c * glanes:(c + 1) * glanes] = jnp.dot(
-            perm[...], stage[i % 2], preferred_element_type=F32
-        ).astype(BF16)
-        if i + 2 < 2 * chunks:
-            stage_copy(i + 2).start()
+        at = slice(i * glanes, (i + 1) * glanes)
+        into[:, at] = jnp.dot(perm[...], into[:, at], preferred_element_type=F32).astype(BF16)
 
     def moments(i):
         r = pl.ds(pl.multiple_of(i * BAND, BAND), BAND)
@@ -390,6 +382,7 @@
 
     bands = tokens // BAND
     perm[...] = run_matrix(tokens, False)
+    tok_load.wait()
     for i in range(chunks // 2):
         to_runs(i, xs)
     z_wait(0)
@@ -426,13 +419,14 @@
     keep[...] = jnp.dot(
         (perm[...].astype(F32) * kept).astype(BF16), jnp.ones((tokens, LANES), BF16), preferred_element_type=F32
     )
-    for i in range(chunks, chunks + chunks // 2):
+    cot_load.wait()
+    for i in range(chunks // 2):
         to_runs(i, gs)
     gather_tick(2)
     straight(0, core_wait)
 
     def late_start():
-        for i in range(chunks + chunks // 2, 2 * chunks):
+        for i in range(chunks // 2, chunks):
             to_runs(i, gs)
         perm[...] = run_matrix(tokens, True)
 
@@ -648,6 +642,7 @@
     def backward_group(q):
         enter_back(q)
         each(GROUP, lambda j: backward(q * GROUP + j))
+        drain_group(q)
 
     def pg_load(u):
         return pltpu.make_async_copy(pgm.at[u], pgs.at[lax.rem(u, PAIR), tokens:2 * tokens], pl_)
@@ -846,6 +841,43 @@
             )
             grad_copy(c).start()
 
+    def drain(u):
+        for j in range(1, ny):
+            z_copy(u, j).wait_send()
+        for i in range(3):
+            band_copy(u, i).wait_send()
+        for i in (0, 1):
+            diag_copy(u, i).wait_send()
+        for i in (1, 2, 3):
+            core_copy(u, i).wait_send()
+
+    def drain_group(q):
+        for a in ((m1a, e1as, e1ar, q, 0), (m1b, e1bs, e1br, q, 1), (m2a, e2as, e2ar, q, 0), (m2b, e2bs, e2br, q, 1)):
+            for c in e_copies(*a):
+                c.wait_send()
+
+    def drain_first():
+        for c in across:
+            for j in range(1, ny):
+                a_z(c, j).wait_send()
+            for i in (1, 2):
+                a_copy(c, i).wait_send()
+            for i in (0, 1):
+                a_diag(c, i).wait_send()
+            a_core(c).wait_send()
+        for j in range(1, ny):
+            vz(j).wait_send()
+        for j in range(1, nx):
+            vx(j).wait_send()
+        r_mate.wait_send()
+
+    def vectors_in():
+        each(count, lambda j: v_recv(j).wait_recv(), 1)
+        vin[me] = vtot[me // 2]
+        total = lax.fori_loop(0, count, lambda j, s: s + vin[j], jnp.zeros((8, LANES), F32))
+        vgo[...] = jnp.where(odd, total[0:6, rows:2 * rows], total[0:6, 0:rows])
+        each(count, lambda j: v_copy(j).wait_send(), 1)
+
     def tick(k, _):
         u = k - 3
         v = u - WEIGH
@@ -914,34 +946,19 @@
             vectors_out()
 
         pl.when(v == units + 2)(natural)
+        pl.when(v == units + 3)(vectors_in)
+        w = k - units - 1
+
+        @pl.when((w >= 0) & (w < units))
+        def _():
+            straight(w, drain)
+
+        pl.when(w == 4)(drain_first)
         return 0
 
     front_load(0).start()
     lax.fori_loop(3, units + WEIGH + 3 + LAST, tick, 0)
 
-    each(count, lambda j: v_recv(j).wait_recv(), 1)
-    vin[me] = vtot[me // 2]
-    vgo[...] = lax.fori_loop(0, count, lambda j, s: s + vin[j], jnp.zeros((8, LANES), F32))
-
-    def drain(u):
-        for j in range(1, ny):
-            z_copy(u, j).wait_send()
-        for i in range(3):
-            band_copy(u, i).wait_send()
-        for i in (0, 1):
-            diag_copy(u, i).wait_send()
-        for i in (1, 2, 3):
-            core_copy(u, i).wait_send()
-
-    each(units, lambda u: straight(u, drain))
-    for c in across:
-        for j in range(1, ny):
-            a_z(c, j).wait_send()
-        for i in (1, 2):
-            a_copy(c, i).wait_send()
-        for i in (0, 1):
-            a_diag(c, i).wait_send()
-        a_core(c).wait_send()
     for n, c in enumerate(turned):
         b_drain(c, n)
 
@@ -959,20 +976,8 @@
 
     each(units, drain_z, units - ZSEND)
 
-    def drain_group(q):
-        for a in ((m1a, e1as, e1ar, q, 0), (m1b, e1bs, e1br, q, 1), (m2a, e2as, e2ar, q, 0), (m2b, e2bs, e2br, q, 1)):
-            for c in e_copies(*a):
-                c.wait_send()
-
-    each(groups, drain_group)
     for q in range(groups - 2, groups):
         out_copy(q).wait()
-    for j in range(1, ny):
-        vz(j).wait_send()
-    for j in range(1, nx):
-        vx(j).wait_send()
-    r_mate.wait_send()
-    each(count, lambda j: v_copy(j).wait_send(), 1)
     for c in range(4):
         grad_copy(c).wait()
 
@@ -991,7 +996,7 @@
         name="layer",
         out_shape=(
             s((units, nx // 2, 2, ny, rows, cols), BF16), s((units, tokens, cols), BF16),
-            s((tokens, width), BF16), s((tokens, width), F32), s((rows, 3 * width), F32), s((8, LANES), F32),
+            s((tokens, width), BF16), s((tokens, width), F32), s((rows, 3 * width), F32), s(vectors.shape, F32),
         ),
         in_specs=[any_, any_, vmem, any_, vmem],
         out_specs=(any_,) * 4 + (vmem,) * 2,
@@ -1032,12 +1037,8 @@
 
 
 def fast(nx, ny, tokens, reset_mask, weight, vectors, cotangent):
-    rows = weight.shape[0]
-    odd = lax.rem(lax.axis_index("gx") * ny + lax.axis_index("gy"), 2) == 1
     mask = reset_mask.reshape(1, -1)
-    _, _, outp, grad, weight_grad, tile = layer(nx, ny, tokens, cotangent, mask, weight, vectors)
-    vector_grad = jnp.where(odd, tile[:6, rows:2 * rows], tile[:6, :rows])
-    return outp, grad, weight_grad, vector_grad
+    return layer(nx, ny, tokens, cotangent, mask, weight, vectors)[2:]
 
 
 def solution(mesh):

time: 248 us -> 246 us (level)
    unnamed x7 -> x10, local copies, waits for them, and re-layouts: 7 us -> 7.6 us
where the time goes in v7:
time: 246 us; the launch traced here: 245 us
  Pallas kernels  237 us (96%)
  local copies, waits for them, and re-layouts  7.6 us (3%)
    pallas_call x1, Pallas kernels, layer(): pl.pallas_call(functools.partial(layer_kernel, nx, ny, units), name='laye...  237 us
    unnamed x10, local copies, waits for them, and re-layouts  7.6 us

profile of v7, /device:TPU:0, one launch (start us, length us, event | category | flops | bytes accessed | tf_op | source)
XLA Modules:
  0.0 245.5 jit_solution(2562053152519677516)
XLA Ops:
  0.6 237.2 %layer.1 = (bf16[16,4,2,4,64,384]{5,4,3,2,1,0:T(8,128)(2,1)}, bf16[16,512,384]{2,1,0:T(8,128)(2,1)}, bf16[512,2048]{1,0:T(8,128)(2,1)}, f32[512,2048]{1,0:T(8,12...) custom-call(bf16[512,2048]{1,0:T(8,128)(2,1)} %tok.1, bf16[512,2048]{1,0:T(8,128)(2,1)} %cot.1, s32[1,512]{1,0:T(1,128)} %bitcast.1, ...), custom_call_target="tpu_custom_call" | custom-call | flops 38654705664 | bytes 50331648 | tf_op jit(solution)/shard_map/layer/pallas_call | solution.py:994
  237.8 0.0 copy-start
  237.9 3.3 %copy.13 = bf16[512,2048]{1,0:T(8,128)(2,1)} copy(bf16[512,2048]{1,0:T(8,128)(2,1)} %get-tuple-element.16) | data formatting | bytes 4194304
  241.2 0.0 copy-done
  241.2 0.0 copy-start.1
  241.2 2.0 copy.14
  243.2 0.5 copy-done.1
  243.7 0.0 copy-start.2
  243.7 1.1 copy.15
  244.9 0.0 copy-done.2
  244.9 0.6 copy.16
Async XLA Ops:
  237.8 3.3 %copy-start = (f32[512,2048]{1,0:T(8,128)S(1)}, f32[512,2048]{1,0:T(8,128)}, u32[]{:S(2)}) copy-start(f32[512,2048]{1,0:T(8,128)} %get-tuple-element.17) | copy-start | bytes 12582916
  241.2 2.5 %copy-start.1 = (f32[64,6144]{1,0:T(8,128)S(1)}, f32[64,6144]{1,0:T(8,128)}, u32[]{:S(2)}) copy-start(f32[64,6144]{1,0:T(8,128)} %get-tuple-element.18) | copy-start | bytes 4718596
  243.7 1.1 copy-start.2

commit v8 on v7

--- a/solution.py
+++ b/solution.py
@@ -158,7 +158,7 @@
 LAST = 6
 AHEAD_Z, AHEAD_B = 5, 3
 BAND = 32
-ACROSS = ((10, (0, 3, 6)), (15, (8, 11, 13)))
+ACROSS = ((10, (0, 3, 5)), (14, (6, 8, 10)), (15, (11, 13, 15)))
 ACROSS_SUM = ()
 
 
@@ -293,9 +293,27 @@
         part = wall.at[u, (xq, yq)[i], core, gy, short * i:short * (i + 1)]
         return remote(part, part, dsn.at[u, i], dr.at[u, i], ((yn, xn)[i], gy))
 
-    def a_z(u, j):
-        part = wall.at[u, :, core, gy]
-        return remote(part, part, zs.at[u, j - 1], zr.at[u, j - 1], (gx, peer_y(j)))
+    def a_up(u, h):
+        part = wall.at[u, :, core, gy - h]
+        return remote(part, part, zs.at[u, h], zr.at[u, h], (gx, lax.rem(gy + 1, ny)))
+
+    def a_down(u, h):
+        part = wall.at[u, :, core, gy + h]
+        return remote(part, part, cs.at[u, h], cr.at[u, h + 1], (gx, lax.rem(gy + ny - 1, ny)))
+
+    def a_landed(u, h):
+        pl.when(gy > h)(lambda: a_up(u, h).wait_recv())
+        pl.when(gy + h + 1 < ny)(lambda: a_down(u, h).wait_recv())
+
+    def a_hop(u, h):
+        if h:
+            a_landed(u, h - 1)
+        pl.when((gy + 1 < ny) & (gy >= h))(lambda: a_up(u, h).start())
+        pl.when((gy >= 1) & (gy + h < ny))(lambda: a_down(u, h).start())
+
+    def a_left(u, h):
+        pl.when((gy + 1 < ny) & (gy >= h))(lambda: a_up(u, h).wait_send())
+        pl.when((gy >= 1) & (gy + h < ny))(lambda: a_down(u, h).wait_send())
 
     def a_core(u):
         part = wall.at[u, :, core]
@@ -318,8 +336,7 @@
             a_diag(u, i).wait_recv()
 
     def a_share(u):
-        for j in range(1, ny):
-            a_z(u, j).wait_recv()
+        a_landed(u, ny - 2)
         a_core(u).start()
 
     zero = jnp.zeros((vectors.shape[0], LANES - rows), BF16)
@@ -377,7 +394,7 @@
         pl.when((k >= 1) & (k <= units))(lambda: straight(k - 1, diag_wait))
         for c, times in ACROSS:
             for j, t in enumerate(times):
-                pl.when(k == t)(lambda c=c, j=j: a_z(c, j + 1).start())
+                pl.when(k == t)(functools.partial(a_hop, c, j))
             pl.when(k == c + 1)(functools.partial(a_share, c))
 
     bands = tokens // BAND
@@ -858,8 +875,8 @@
 
     def drain_first():
         for c in across:
-            for j in range(1, ny):
-                a_z(c, j).wait_send()
+            for h in range(ny - 1):
+                a_left(c, h)
             for i in (1, 2):
                 a_copy(c, i).wait_send()
             for i in (0, 1):

time: 246 us -> 243 us (0.988)
    pallas_call x1, Pallas kernels: 237 us -> 235 us  [layer(): pl.pallas_call(functools.partial(layer_kernel, nx, ny, units), name='laye...]
where the time goes in v8:
time: 243 us
  Pallas kernels  235 us (97%)
  local copies, waits for them, and re-layouts  7.6 us (3%)
    pallas_call x1, Pallas kernels, layer(): pl.pallas_call(functools.partial(layer_kernel, nx, ny, units), name='laye...  235 us
    unnamed x10, local copies, waits for them, and re-layouts  7.6 us

profile of v8, /device:TPU:0, one launch (start us, length us, event | category | flops | bytes accessed | tf_op | source)
XLA Modules:
  0.0 243.0 jit_solution(11167575971823280201)
XLA Ops:
  0.6 234.7 %layer.1 = (bf16[16,4,2,4,64,384]{5,4,3,2,1,0:T(8,128)(2,1)}, bf16[16,512,384]{2,1,0:T(8,128)(2,1)}, bf16[512,2048]{1,0:T(8,128)(2,1)}, f32[512,2048]{1,0:T(8,12...) custom-call(bf16[512,2048]{1,0:T(8,128)(2,1)} %tok.1, bf16[512,2048]{1,0:T(8,128)(2,1)} %cot.1, s32[1,512]{1,0:T(1,128)} %bitcast.1, ...), custom_call_target="tpu_custom_call" | custom-call | flops 38654705664 | bytes 50331648 | tf_op jit(solution)/shard_map/layer/pallas_call | solution.py:1011
  235.4 0.0 copy-start
  235.4 3.3 %copy.13 = bf16[512,2048]{1,0:T(8,128)(2,1)} copy(bf16[512,2048]{1,0:T(8,128)(2,1)} %get-tuple-element.16) | data formatting | bytes 4194304
  238.7 0.0 copy-done
  238.7 0.0 copy-start.1
  238.7 2.0 copy.14
  240.7 0.5 copy-done.1
  241.2 0.0 copy-start.2
  241.2 1.1 copy.15
  242.4 0.0 copy-done.2
  242.4 0.6 copy.16
Async XLA Ops:
  235.4 3.3 %copy-start = (f32[512,2048]{1,0:T(8,128)S(1)}, f32[512,2048]{1,0:T(8,128)}, u32[]{:S(2)}) copy-start(f32[512,2048]{1,0:T(8,128)} %get-tuple-element.17) | copy-start | bytes 12582916
  238.7 2.5 %copy-start.1 = (f32[64,6144]{1,0:T(8,128)S(1)}, f32[64,6144]{1,0:T(8,128)}, u32[]{:S(2)}) copy-start(f32[64,6144]{1,0:T(8,128)} %get-tuple-element.18) | copy-start | bytes 4718596
  241.2 1.1 copy-start.2

commit v9 on v8

--- a/solution.py
+++ b/solution.py
@@ -472,12 +472,18 @@
 
     double = tokens // (2 * RUNS)
 
+    def side(u):
+        return pl.ds(pl.multiple_of(lax.rem(u, 2) * cols, LANES), cols)
+
     def front_load(u):
-        return pltpu.make_async_copy(wall.at[u], wf, ws)
+        return pltpu.make_async_copy(wall.at[u], wf.at[:, :, :, :, side(u)], ws.at[lax.rem(u, 2)])
 
     def project(u):
+        front_load(u - 1).wait()
         front_load(u).wait()
-        pj[lax.rem(u, SLOTS)] = jnp.dot(rnd[...], wf[...].reshape(width, -1), preferred_element_type=F32)
+        both = jnp.dot(rnd[...], wf[...].reshape(width, -1), preferred_element_type=F32)
+        pj[lax.rem(u - 1, SLOTS)] = both[:, :cols]
+        pj[lax.rem(u, SLOTS)] = both[:, cols:]
 
     def vec(i, u):
         return vecs[i:i + 1, lanes_of(u)]
@@ -939,7 +945,9 @@
         event(FORE, forward_group)
         event(TOTALS, totals_x)
 
-        @pl.when((u >= 0) & (u < units))
+        paired = (u >= 0) & (u < units) & (lax.rem(u, 2) == 1)
+
+        @pl.when(paired)
         def _():
             project(u)
 
@@ -950,10 +958,11 @@
                 pl.when(u + 1 == c)(lambda c=c: a_core(c).wait_recv())
             front_load(u + 1).start()
 
-        @pl.when((u >= 0) & (u < units))
+        @pl.when(paired)
         def _():
+            gates(u - 1)
             gates(u)
-            pl.when(lax.rem(u, GROUP) == GROUP - 1)(lambda: totals(u // GROUP))
+            totals(u // GROUP)
 
         pl.when(v == units)(lambda: each(bands // 2, finish))
 
@@ -1021,7 +1030,7 @@
             v((count, 16, LANES), BF16), v((8, width), F32),
             v((tokens, width), BF16), v((tokens, width), BF16), v((tokens, LANES), F32), v((tokens, LANES), F32),
             v((tokens, width), BF16), v((width // 2, 2 * tokens), BF16), v((width // 2, tokens), BF16),
-            v((nx // 2, 2, ny, rows, cols), BF16),
+            v((nx // 2, 2, ny, rows, 2 * cols), BF16),
             v((SLOTS, tokens, cols), F32), v((SLOTS, tokens, LANES), F32),
             v((tokens, width), F32), v((tokens, glanes), BF16), v((2, tokens, glanes), BF16),
             v((tokens, tokens), BF16), v((PAIR, 2 * tokens, cols), BF16),
@@ -1036,7 +1045,7 @@
             v((groups, ny, 2, glanes), F32), v((groups, nx, 2, glanes), F32),
             v((groups, ny, 1, glanes), F32), v((groups, nx, 1, glanes), F32),
             dma((units, ny - 1)), dma((units, ny - 1)), dma((units,)), dma((units, 3)), dma((units, 2)),
-            dma((units, 2)), dma((units, 2)), dma((units, 3)), dma((units, 4)), dma,
+            dma((units, 2)), dma((units, 2)), dma((units, 3)), dma((units, 4)), dma((2,)),
             dma((ny - 1,)), dma((ny - 1,)), dma((nx - 1,)), dma((nx - 1,)), dma, dma, dma((2,)),
             dma, dma, dma((units,)), dma((units,)), dma, dma, dma((groups,)),
             dma((groups, ny - 1)), dma((groups, ny - 1)), dma((groups, nx - 1)), dma((groups, nx - 1)),

time: 243 us -> 241 us (level)
  no operation moved by 1% of the time
where the time goes in v9:
time: 241 us
  Pallas kernels  233 us (97%)
  local copies, waits for them, and re-layouts  7.6 us (3%)
    pallas_call x1, Pallas kernels, layer(): pl.pallas_call(functools.partial(layer_kernel, nx, ny, units), name='laye...  233 us
    unnamed x10, local copies, waits for them, and re-layouts  7.6 us

profile of v9, /device:TPU:0, one launch (start us, length us, event | category | flops | bytes accessed | tf_op | source)
XLA Modules:
  0.0 241.1 jit_solution(9871681400112820347)
XLA Ops:
  0.6 232.9 %layer.1 = (bf16[16,4,2,4,64,384]{5,4,3,2,1,0:T(8,128)(2,1)}, bf16[16,512,384]{2,1,0:T(8,128)(2,1)}, bf16[512,2048]{1,0:T(8,128)(2,1)}, f32[512,2048]{1,0:T(8,12...) custom-call(bf16[512,2048]{1,0:T(8,128)(2,1)} %tok.1, bf16[512,2048]{1,0:T(8,128)(2,1)} %cot.1, s32[1,512]{1,0:T(1,128)} %bitcast.1, ...), custom_call_target="tpu_custom_call" | custom-call | flops 38654705664 | bytes 50331648 | tf_op jit(solution)/shard_map/layer/pallas_call | solution.py:1020
  233.5 0.0 copy-start
  233.5 3.3 %copy.13 = bf16[512,2048]{1,0:T(8,128)(2,1)} copy(bf16[512,2048]{1,0:T(8,128)(2,1)} %get-tuple-element.16) | data formatting | bytes 4194304
  236.8 0.0 copy-done
  236.8 0.0 copy-start.1
  236.8 2.0 copy.14
  238.8 0.5 copy-done.1
  239.4 0.0 copy-start.2
  239.4 1.1 copy.15
  240.5 0.0 copy-done.2
  240.5 0.6 copy.16
Async XLA Ops:
  233.5 3.3 %copy-start = (f32[512,2048]{1,0:T(8,128)S(1)}, f32[512,2048]{1,0:T(8,128)}, u32[]{:S(2)}) copy-start(f32[512,2048]{1,0:T(8,128)} %get-tuple-element.17) | copy-start | bytes 12582916
  236.8 2.5 %copy-start.1 = (f32[64,6144]{1,0:T(8,128)S(1)}, f32[64,6144]{1,0:T(8,128)}, u32[]{:S(2)}) copy-start(f32[64,6144]{1,0:T(8,128)} %get-tuple-element.18) | copy-start | bytes 4718596
  239.4 1.1 copy-start.2

commit v10 on v9

--- a/solution.py
+++ b/solution.py
@@ -156,7 +156,7 @@
 TOTALS, FORE, GRADS, BACK, WEIGH = 2, 4, 5, 7, 9
 LAG1, LAG2, LAG3 = 2, 4, 6
 LAST = 6
-AHEAD_Z, AHEAD_B = 5, 3
+AHEAD_Z, AHEAD_B = 6, 3
 BAND = 32
 ACROSS = ((10, (0, 3, 5)), (14, (6, 8, 10)), (15, (11, 13, 15)))
 ACROSS_SUM = ()

time: 241 us -> 242 us (level)
  no operation moved by 1% of the time
where the time goes in v10:
time: 242 us
  Pallas kernels  233 us (96%)
  local copies, waits for them, and re-layouts  7.6 us (3%)
    pallas_call x1, Pallas kernels, layer(): pl.pallas_call(functools.partial(layer_kernel, nx, ny, units), name='laye...  233 us
    unnamed x10, local copies, waits for them, and re-layouts  7.6 us

profile of v10, /device:TPU:0, one launch (start us, length us, event | category | flops | bytes accessed | tf_op | source)
XLA Modules:
  0.0 241.7 jit_solution(11744661718834153762)
XLA Ops:
  0.6 233.5 %layer.1 = (bf16[16,4,2,4,64,384]{5,4,3,2,1,0:T(8,128)(2,1)}, bf16[16,512,384]{2,1,0:T(8,128)(2,1)}, bf16[512,2048]{1,0:T(8,128)(2,1)}, f32[512,2048]{1,0:T(8,12...) custom-call(bf16[512,2048]{1,0:T(8,128)(2,1)} %tok.1, bf16[512,2048]{1,0:T(8,128)(2,1)} %cot.1, s32[1,512]{1,0:T(1,128)} %bitcast.1, ...), custom_call_target="tpu_custom_call" | custom-call | flops 38654705664 | bytes 50331648 | tf_op jit(solution)/shard_map/layer/pallas_call | solution.py:1020
  234.1 0.0 copy-start
  234.1 3.3 %copy.13 = bf16[512,2048]{1,0:T(8,128)(2,1)} copy(bf16[512,2048]{1,0:T(8,128)(2,1)} %get-tuple-element.16) | data formatting | bytes 4194304
  237.4 0.0 copy-done
  237.4 0.0 copy-start.1
  237.4 2.0 copy.14
  239.5 0.5 copy-done.1
  240.0 0.0 copy-start.2
  240.0 1.1 copy.15
  241.1 0.0 copy-done.2
  241.1 0.6 copy.16
Async XLA Ops:
  234.1 3.3 %copy-start = (f32[512,2048]{1,0:T(8,128)S(1)}, f32[512,2048]{1,0:T(8,128)}, u32[]{:S(2)}) copy-start(f32[512,2048]{1,0:T(8,128)} %get-tuple-element.17) | copy-start | bytes 12582916
  237.4 2.5 %copy-start.1 = (f32[64,6144]{1,0:T(8,128)S(1)}, f32[64,6144]{1,0:T(8,128)}, u32[]{:S(2)}) copy-start(f32[64,6144]{1,0:T(8,128)} %get-tuple-element.18) | copy-start | bytes 4718596
  240.0 1.1 copy-start.2
